TPU v7x, 32 devices: a whole 2x2x4 slice. The times are simulated.
32 devices in a mesh: ctx: 8 (over z, y), mp: 4 (over x, core).
Axes of the slice: x: 2, y: 2, z: 4, core: 2. Of those that a mesh axis runs over, the one named last changes fastest.
Arguments:
- queries: bfloat16 [16384, 2048], P('ctx', 'mp'), may hold values from -6 to 6
- key_vectors: bfloat16 [16384, 2048], P('ctx', 'mp'), may hold values from -6 to 6
- value_vectors: bfloat16 [16384, 2048], P('ctx', 'mp'), may hold values from -6 to 6
- level_index: int32 [16384], P('ctx'), may hold values from 0 to 15
- level_table: float32 [16, 16, 20], P(None, 'mp'), may hold values from 0.1 to 4
- out_weight: bfloat16 [2048, 2048], P('mp'), may hold values from -0.125 to 0.125
Outputs:
- layer_out: bfloat16 [16384, 2048], P(('ctx', 'mp'))
All inputs are finite; a program needn't handle non-finite values.
Results may differ from a plain program's by a relative error of at most 0.015.
Values may be sent and summed in bfloat16 or wider, within the bound.
No kernel may reach another device: no remote copies, remote signals or barrier semaphores. Data moves between devices by JAX's collectives and lax.ppermute only.
A program may use at most 128 MiB of HBM per device.

v0:
```python
import jax
import jax.numpy as jnp
from jax import lax
from jax.sharding import PartitionSpec as P

STRETCH = 256


EPSILON = 1e-06


def fenwick_level(offsets, digits):
    counted = jnp.zeros(offsets.shape, jnp.int32)
    for bit_index in range(digits):
        counted = counted + (offsets >= 1 << bit_index).astype(jnp.int32)
    return counted


def body(queries, key_vectors, value_vectors, level_index, level_table, out_weight):
    tok_rows = queries.shape[0]
    plans = level_table.shape[0]
    heads_here = level_table.shape[1]
    level_total = level_table.shape[2]
    head_size = queries.shape[1] // heads_here
    stretch_count = tok_rows // STRETCH
    stretch_bits = STRETCH.bit_length() - 1
    local_bits = stretch_count.bit_length() - 1
    ctx_bits = lax.axis_size("ctx").bit_length() - 1
    position = lax.axis_index("ctx")
    onehot = (level_index[:, None] == jnp.arange(plans, dtype=jnp.int32)[None, :]).astype(
        jnp.float32
    )
    token_weights = jnp.dot(
        onehot,
        level_table.reshape(plans, heads_here * level_total),
        precision=lax.Precision.HIGHEST,
        preferred_element_type=jnp.float32,
    )
    weight_blocks = token_weights.reshape(
        stretch_count, STRETCH, heads_here, level_total
    ).transpose(0, 2, 1, 3)
    query_blocks = queries.reshape(stretch_count, STRETCH, heads_here, head_size).transpose(
        0, 2, 1, 3
    )
    key_blocks = key_vectors.reshape(stretch_count, STRETCH, heads_here, head_size).transpose(
        0, 2, 1, 3
    )
    value_blocks = value_vectors.reshape(stretch_count, STRETCH, heads_here, head_size).transpose(
        0, 2, 1, 3
    )
    states = jnp.einsum(
        "nhsd,nhse->nhde", key_blocks, value_blocks, preferred_element_type=jnp.float32
    )
    own_total = jnp.sum(states, axis=0)
    zero_states = jnp.zeros((ctx_bits, heads_here, head_size, head_size), jnp.float32)
    shards = lax.all_gather(own_total[None].astype(jnp.bfloat16), "ctx", axis=0, tiled=True).astype(
        jnp.float32
    )
    sources = jnp.arange(shards.shape[0], dtype=jnp.int32)
    crossed = fenwick_level(jnp.bitwise_xor(position, sources), ctx_bits + 1)
    earlier = sources < position
    select = (
        (crossed[None, :] - 1 == jnp.arange(ctx_bits, dtype=jnp.int32)[:, None]) & earlier[None, :]
    ).astype(jnp.float32)
    remote = zero_states + jnp.einsum(
        "li,ihde->lhde", select, shards, precision=lax.Precision.HIGHEST
    )
    scores = jnp.einsum(
        "nhtd,nhsd->nhts", query_blocks, key_blocks, preferred_element_type=jnp.float32
    )
    offsets = jnp.arange(STRETCH, dtype=jnp.int32)
    levels = fenwick_level(jnp.bitwise_xor(offsets[:, None], offsets[None, :]), stretch_bits + 1)
    level_onehot = (
        levels[:, :, None] == jnp.arange(stretch_bits + 1, dtype=jnp.int32)[None, None, :]
    ).astype(jnp.float32)
    picked = jnp.einsum(
        "nhto,tso->nhts",
        weight_blocks[..., : stretch_bits + 1],
        level_onehot,
        precision=lax.Precision.HIGHEST,
    )
    causal = offsets[None, :] <= offsets[:, None]
    weighted = jnp.where(causal, scores * picked, 0.0).astype(jnp.bfloat16)
    output = jnp.einsum(
        "nhts,nhse->nhte", weighted, value_blocks, preferred_element_type=jnp.float32
    )
    level_list = []
    for bit_index in range(local_bits):
        span_width = 1 << bit_index
        groups = stretch_count // (2 * span_width)
        lower_sum = states.reshape(groups, 2, span_width, heads_here, head_size, head_size)[
            :, 0
        ].sum(axis=1)
        spread = jnp.broadcast_to(
            lower_sum[:, None], (groups, span_width, heads_here, head_size, head_size)
        )
        placed = jnp.stack([jnp.zeros_like(spread), spread], axis=1).reshape(
            stretch_count, heads_here, head_size, head_size
        )
        level_list.append(placed.astype(jnp.bfloat16))
    remote_rounded = remote.astype(jnp.bfloat16)
    for bit_index in range(ctx_bits):
        level_list.append(
            jnp.broadcast_to(
                remote_rounded[bit_index][None], (stretch_count, heads_here, head_size, head_size)
            )
        )
    all_levels = jnp.stack(level_list, axis=1)
    reached = jnp.einsum(
        "nhtd,nlhde->nhtle", query_blocks, all_levels, preferred_element_type=jnp.float32
    )
    level_scale = weight_blocks[..., stretch_bits + 1 : stretch_bits + 1 + local_bits + ctx_bits]
    output = output + jnp.sum(reached * level_scale[..., None], axis=3)
    normed = output * lax.rsqrt(jnp.mean(output * output, axis=-1, keepdims=True) + EPSILON)
    mixed_heads = (
        normed.astype(jnp.bfloat16).transpose(0, 2, 1, 3).reshape(tok_rows, heads_here * head_size)
    )
    return lax.psum_scatter(
        jnp.dot(mixed_heads, out_weight, preferred_element_type=jnp.float32).astype(jnp.bfloat16),
        "mp",
        scatter_dimension=0,
        tiled=True,
    )


def solution(mesh):
    placed = (
        P("ctx", "mp"),
        P("ctx", "mp"),
        P("ctx", "mp"),
        P("ctx"),
        P(None, "mp", None),
        P("mp", None),
    )
    return jax.shard_map(
        body, mesh=mesh, in_specs=placed, out_specs=P(("ctx", "mp"), None), check_vma=False
    )
```

profile of v0, /device:TPU:0, one launch (start us, length us, event | category | flops | bytes accessed | tf_op | source)
XLA Modules:
  0.0 187.3 jit_solution(13763648218421524824)
XLA Ops:
  6.5 0.0 copy-start
  6.5 0.0 all-gather.3.cloned.1.call-start
  6.5 4.1 %reshape.182 = bf16[8,256,4,128]{3,2,1,0:T(4,128)(2,1)} reshape(bf16[2048,512]{1,0:T(8,128)(2,1)} %param.7) | data formatting | bytes 4194304 | tf_op jit(solution)/shard_map/reshape | solution.py:45
  10.6 4.2 %copy.49 = bf16[8,256,4,128]{1,3,2,0:T(8,128)(2,1)} copy(bf16[8,256,4,128]{3,2,1,0:T(4,128)(2,1)} %reshape.182) | data formatting | bytes 4194304 | tf_op jit(solution)/shard_map/transpose | solution.py:45
  14.8 4.0 %reshape.184 = bf16[8,256,4,128]{3,2,1,0:T(4,128)(2,1)} reshape(bf16[2048,512]{1,0:T(8,128)(2,1)} %param.8) | data formatting | bytes 4194304 | tf_op jit(solution)/shard_map/reshape | solution.py:48
  18.8 0.0 copy-start.4
  18.8 0.0 copy-start.5
  18.8 5.0 %fusion.62 = (bf16[4,128,128]{2,1,0:T(8,128)(2,1)}, bf16[8,4,128,128]{3,2,1,0:T(8,128)(2,1)S(1)}, f32[8,4,128,128]{3,2,1,0:T(8,128)}) fusion(bf16[8,256,4,128]{3,2,1,0:T(4,128)(2,1)} %reshape.184, bf16[8,256,4,128]{1,3,2,0:T(8,128)(2,1)} %copy.49), kind=kOutput, calls=%fused_computation.73 | convolution fusion | flops 269418496 | bytes 7471104 | tf_op jit(solution)/shard_map/nhsd,nhse->nhde/dot_general | solution.py:51
  23.8 0.0 all-gather.3.cloned.1.call-update
  23.8 0.0 reduce-scatter.2.cloned.1.call-start
  23.8 0.0 copy-done.4
  23.8 0.1 reshape.183
  23.9 0.1 dot_general.32
  24.0 0.0 copy-done.5
  24.0 0.5 convolution_bitcast_fusion
  24.5 0.7 slice.49
  25.3 0.9 slice.42
  26.2 2.1 %slice_reduce_fusion.1 = bf16[2,4,128,128]{3,2,1,0:T(8,128)(2,1)} fusion(f32[2,2,2,4,128,128]{5,4,3,2,1,0:T(8,128)} %bitcast.105), kind=kLoop, calls=%fused_computation.32 | loop fusion | flops 131072 | bytes 1310720 | tf_op jit(solution)/shard_map/reduce_sum | solution.py:93
  28.2 1.1 copy.35
  29.4 0.8 slice.43
  30.2 2.1 %copy.55 = bf16[4,1,1,4,128,128]{4,5,3,1,0,2:T(8,128)(2,1)} copy(bf16[4,1,1,4,128,128]{5,4,3,1,0,2:T(8,128)(2,1)} %slice.43) | data formatting | bytes 1048576
  32.3 0.0 copy-start.2
  32.3 0.1 stack_broadcast_in_dim.10
  32.4 0.2 stack.16
  32.5 2.3 %stack.15.clone = bf16[4,2,1,4,128,128]{4,5,3,1,0,2:T(8,128)(2,1)} pad(bf16[4,1,1,4,128,128]{4,5,3,1,0,2:T(8,128)(2,1)} %copy.55, bf16[]{:T(256)} %constant.9.clone.1), padding=0_0x1_0x0_0x0_0x0_0x0_0 | pad | bytes 1572866 | tf_op jit(solution)/shard_map/stack | solution.py:97
  34.9 0.0 copy-done.2
  34.9 0.1 slice_reduce_fusion
  34.9 0.1 copy.36
  35.1 0.1 stack_broadcast_in_dim.11
  35.2 1.2 stack.17
  36.3 4.0 %reshape.181 = bf16[8,256,4,128]{3,2,1,0:T(4,128)(2,1)} reshape(bf16[2048,512]{1,0:T(8,128)(2,1)} %param.6) | data formatting | bytes 4194304 | tf_op jit(solution)/shard_map/reshape | solution.py:42
  40.3 5.3 %copy.30 = f32[8,4,256,9]{3,0,1,2:T(8,128)} copy(f32[8,4,256,9]{2,3,1,0:T(8,128)} %slice.42) | data formatting | bytes 589824 | tf_op jit(solution)/shard_map/slice | solution.py:78
  45.6 0.0 copy-start.1
  45.7 0.1 convert_add_fusion
  45.8 2.7 %constant_dynamic-update-slice_fusion.2 = bf16[8,6,4,128,128]{3,4,1,2,0:T(8,128)(2,1)} fusion(bf16[8,1,4,128,128]{3,4,1,2,0:T(8,128)(2,1)} %bitcast.109), kind=kLoop, calls=%fused_computation.57 | loop fusion | bytes 2097152
  48.5 1.2 constant_dynamic-update-slice_fusion.1
  49.6 2.5 %constant_dynamic-update-slice_fusion = bf16[8,6,4,128,128]{3,4,1,2,0:T(8,128)(2,1)} fusion(bf16[8,6,4,128,128]{3,4,1,2,0:T(8,128)(2,1)} %constant_dynamic-update-slice_fusion.1, bf16[8,1,4,128,128]{3,4,1,2,0:T(8,128)(2,1)} %bitcast.110), kind=kLoop, calls=%fused_computation.55 | loop fusion | bytes 2097152
  52.1 0.0 copy-done.1
  52.1 6.5 %fusion.8 = f32[256,256,8,4]{1,2,3,0:T(8,128)} fusion(f32[8,4,256,9]{3,0,1,2:T(8,128)S(1)} %copy-done.1, s32[256,256]{1,0:T(8,128)S(1)} %convert_add_fusion), kind=kOutput, calls=%fused_computation.13 | convolution fusion | flops 227082240 | bytes 8945664 | tf_op jit(solution)/shard_map/nhto,tso->nhts/dot_general | solution.py:76
  58.6 0.0 copy-start.3
  58.6 8.2 %all-gather.3.cloned.1.call-done = bf16[32,128,128]{2,1,0:T(8,128)(2,1)} async-done(((bf16[4,128,128]{2,1,0:T(8,128)(2,1)}), bf16[32,128,128]{2,1,0:T(8,128)(2,1)}) %all-gather.3.cloned.1.call-update) | async-done | bytes 1048592 | tf_op jit(solution)/shard_map/all_gather | solution.py:56
  66.8 2.0 %convolution_convert_fusion.1 = bf16[3,4,128,128]{3,0,2,1:T(4,128)(2,1)S(1)} fusion(bf16[8,4,128,128]{3,2,1,0:T(8,128)(2,1)} %bitcast.113, s32[8]{0:T(128)S(1)} %fusion.60, pred[8]{0:T(512)(128)(4,1)S(1)} %iota_compare_fusion.4), kind=kOutput, calls=%fused_computation.29 | convolution fusion | flops 3342384 | bytes 1441832 | tf_op jit(solution)/shard_map/li,ihde->lhde/dot_general | solution.py:65
  68.8 0.7 fusion.63
  69.4 0.1 copy.52
  69.6 0.2 copy.53
  69.7 0.2 copy.54
  69.9 1.2 broadcast_dynamic-update-slice_fusion.2
  71.1 1.3 broadcast_dynamic-update-slice_fusion.1
  72.4 1.2 broadcast_dynamic-update-slice_fusion
  73.6 0.0 copy-done.3
  73.6 9.1 %fusion = f32[8,4,256,128]{2,3,1,0:T(8,128)} fusion(f32[8,4,256,6]{2,3,1,0:T(8,128)S(1)} %copy-done.3, bf16[8,6,4,128,128]{3,4,1,2,0:T(8,128)(2,1)} %broadcast_dynamic-update-slice_fusion, bf16[8,256,4,128]{3,2,1,0:T(4,128)(2,1)} %reshape.181), kind=kOutput, calls=%fused_computation.1 | convolution fusion | flops 1622147072 | bytes 12779520 | tf_op jit(solution)/shard_map/nhtd,nlhde->nhtle/dot_general | solution.py:109
  82.7 15.6 %multiply_reduce_fusion = (f32[8,4,256]{2,1,0:T(4,128)S(1)}, f32[8,4,256,128]{2,3,1,0:T(8,128)}) fusion(f32[8,4,256,128]{2,3,1,0:T(8,128)} %fusion, bf16[8,256,4,128]{3,2,1,0:T(4,128)(2,1)} %reshape.184, f32[256,256,8,4]{1,2,3,0:T(8,128)} %fusion.8, pred[256,256]{1,0:T(8,128)(4,1)S(1)} %iota_compare_fusion.1, bf16[8,256,4,128]{1,3,2,0:T(8,128)(2,1)} %copy.49, ...), kind=kOutput, calls=%fused_computation.9 | convolution fusion | flops 1083170816 | bytes 23166976 | tf_op jit(solution)/shard_map/nhts,nhse->nhte/dot_general | solution.py:84
  98.4 2.7 %fusion.5 = bf16[8,256,4,128]{1,3,2,0:T(8,128)(2,1)S(1)} fusion(f32[8,4,256,128]{2,3,1,0:T(8,128)} %get-tuple-element.12, f32[8,256,4]{1,2,0:T(4,128)S(1)} %rsqrt_bitcast_fusion), kind=kLoop, calls=%fused_computation.8 | loop fusion | flops 2097152 | bytes 6324224 | tf_op jit(solution)/shard_map/convert_element_type | solution.py:116
  101.0 1.2 copy.41
  102.2 0.7 copy.56
  102.9 0.0 copy-done
  102.9 6.8 %convolution_convert_fusion = bf16[2048,2048]{1,0:T(8,128)(2,1)} fusion(bf16[2048,512]{0,1:T(8,128)(2,1)S(1)} %bitcast.112, bf16[512,2048]{1,0:T(8,128)(2,1)S(1)} %copy-done), kind=kOutput, calls=%fused_computation.5 | convolution fusion | flops 4299161600 | bytes 12582912 | tf_op jit(solution)/shard_map/dot_general | solution.py:119
  109.8 0.0 reduce-scatter.2.cloned.1.call-update
  109.8 70.6 %reduce-scatter.2.cloned.1.call-done = bf16[512,2048]{1,0:T(8,128)(2,1)} async-done(((bf16[2048,2048]{1,0:T(8,128)(2,1)}), bf16[512,2048]{1,0:T(8,128)(2,1)}) %reduce-scatter.2.cloned.1.call-update) | async-done | bytes 2097168 | tf_op jit(solution)/shard_map/reduce_scatter | solution.py:118
  (5 shorter events, 0.1 us)
Async XLA Ops:
  6.5 96.4 %copy-start = (bf16[512,2048]{1,0:T(8,128)(2,1)S(1)}, bf16[512,2048]{1,0:T(8,128)(2,1)}, u32[]{:S(2)}) copy-start(bf16[512,2048]{1,0:T(8,128)(2,1)} %param.11) | copy-start | bytes 6291460
  6.5 60.2 %all-gather.3.cloned.1.call-start = ((), (), s32[]{:S(2)}) async-start(), calls=%async_computation.2 | async-start | bytes 1179648 | tf_op jit(solution)/shard_map/all_gather | solution.py:56
  18.8 5.1 %copy-start.4 = (f32[16,4,20]{2,1,0:T(4,128)S(1)}, f32[16,4,20]{2,1,0:T(4,128)}, u32[]{:S(2)}) copy-start(f32[16,4,20]{2,1,0:T(4,128)} %param.10) | copy-start | bytes 15364
  18.8 5.2 %copy-start.5 = (s32[2048]{0:T(1024)S(1)}, s32[2048]{0:T(1024)}, u32[]{:S(2)}) copy-start(s32[2048]{0:T(1024)} %param.9) | copy-start | bytes 24580
  23.8 156.7 %reduce-scatter.2.cloned.1.call-start = ((), (), s32[]{:S(2)}) async-start(), calls=%async_computation.1 | async-start | bytes 10485760 | tf_op jit(solution)/shard_map/reduce_scatter | solution.py:118
  32.3 2.6 %copy-start.2 = (f32[8,4,128,128]{3,2,1,0:T(8,128)S(1)}, f32[8,4,128,128]{3,2,1,0:T(8,128)}, u32[]{:S(2)}) copy-start(f32[8,4,128,128]{3,2,1,0:T(8,128)} %get-tuple-element.10) | copy-start | bytes 6291460
  45.6 6.5 %copy-start.1 = (f32[8,4,256,9]{3,0,1,2:T(8,128)S(1)}, f32[8,4,256,9]{3,0,1,2:T(8,128)}, u32[]{:S(2)}) copy-start(f32[8,4,256,9]{3,0,1,2:T(8,128)} %copy.30) | copy-start | bytes 884740
  58.6 15.0 %copy-start.3 = (f32[8,4,256,6]{2,3,1,0:T(8,128)S(1)}, f32[8,4,256,6]{2,3,1,0:T(8,128)}, u32[]{:S(2)}) copy-start(f32[8,4,256,6]{2,3,1,0:T(8,128)} %slice.49) | copy-start | bytes 589828
Sparse Core Ops, SparseCore 0:
  23.9 42.8 all-gather.2
  109.9 70.4 reduce-scatter.1
where the time goes:
time: 188 us; the launch traced here: 187 us
  waiting for transfers between devices  78.8 us (42%)
  matrix products  45.5 us (24%)
  local copies, waits for them, and re-layouts  44.4 us (24%)
  between operations  13.6 us (7%)
  other arithmetic  4.98 us (3%)
    reduce_scatter x1, waiting for transfers between devices, body(): lax.psum_scatter(jnp.dot(mixed_heads, out_weight, preferred_element_type=...  70.6 us
    dot_general x1, matrix products, body(): jnp.einsum('nhts,nhse->nhte', weighted, value_blocks, preferred_element_t...  15.6 us
    unnamed x19, local copies, waits for them, and re-layouts  11.6 us
    dot_general x1, matrix products, body(): jnp.einsum('nhtd,nlhde->nhtle', query_blocks, all_levels, preferred_eleme...  9.11 us
    all_gather x1, waiting for transfers between devices, body(): lax.all_gather(own_total[None].astype(jnp.bfloat16), 'ctx', axis=0, tiled...  8.18 us
    dot_general x1, matrix products, body(): jnp.dot(mixed_heads, out_weight, preferred_element_type=jnp.float32)  6.85 us
    dot_general x1, matrix products, body(): jnp.einsum('nhto,tso->nhts', weight_blocks[..., :stretch_bits + 1], level...  6.48 us
    slice x2, local copies, waits for them, and re-layouts, body(): weight_blocks[..., :stretch_bits + 1]  6.2 us
  transfers between devices with their start and end apart: 2, of which 2 were waited for; matrix products, arithmetic and copies ran while one was open for 19% of the time, Pallas kernels for 0%

commit v1 on v0

v1 whole, which is shorter than its diff:
```python
import functools

import jax
import jax.numpy as jnp
from jax import lax
from jax.experimental import pallas as pl
from jax.experimental.pallas import tpu as pltpu
from jax.sharding import PartitionSpec as P

STRETCH = 256
LANES = 128
EPSILON = 1e-06
MIB = 1024 * 1024


def bit_count(n):
    return n.bit_length() - 1


def contract_rows(a, b):
    return lax.dot_general(a, b, (((0,), (0,)), ((), ())), preferred_element_type=jnp.float32)


def dot(a, b):
    return jnp.dot(a, b, preferred_element_type=jnp.float32)


def state_kernel(count, k_ref, v_ref, level_ref, own_ref):
    states = []
    for n in range(count):
        rows = pl.ds(n * STRETCH, STRETCH)
        states.append(contract_rows(k_ref[rows, :], v_ref[rows, :]))
    at = 0
    sums = states
    while len(sums) > 1:
        for g in range(len(sums) // 2):
            level_ref[at, 0] = sums[2 * g].astype(jnp.bfloat16)
            at += 1
        sums = [sums[2 * g] + sums[2 * g + 1] for g in range(len(sums) // 2)]
    own_ref[...] = sums[0].astype(jnp.bfloat16)


def block_states(keys, values, heads, size):
    tokens = keys.shape[0]
    count = tokens // STRETCH
    column = pl.BlockSpec((tokens, size), lambda h: (0, h))
    return pl.pallas_call(
        functools.partial(state_kernel, count),
        grid=(heads,),
        in_specs=[column, column],
        out_specs=[
            pl.BlockSpec((count - 1, 1, size, size), lambda h: (0, h, 0, 0)),
            pl.BlockSpec((size, size), lambda h: (h, 0)),
        ],
        out_shape=[
            jax.ShapeDtypeStruct((count - 1, heads, size, size), jnp.bfloat16),
            jax.ShapeDtypeStruct((heads * size, size), jnp.bfloat16),
        ],
        compiler_params=pltpu.CompilerParams(vmem_limit_bytes=24 * MIB),
        cost_estimate=pl.CostEstimate(
            flops=2 * tokens * heads * size * size,
            bytes_accessed=4 * tokens * heads * size,
            transcendentals=0,
        ),
        name="block_states",
    )(keys, values)


def spread_weights(index_row, table):
    plans = table.shape[0]
    high = table.astype(jnp.bfloat16)
    rest = table - high.astype(jnp.float32)
    middle = rest.astype(jnp.bfloat16)
    low = (rest - middle.astype(jnp.float32)).astype(jnp.bfloat16)
    plan = lax.broadcasted_iota(jnp.int32, (plans, index_row.shape[1]), 0)
    onehot = (plan == index_row).astype(jnp.float32).astype(jnp.bfloat16)
    return contract_rows(
        jnp.concatenate([onehot] * 3, axis=0), jnp.concatenate([high, middle, low], axis=0)
    )


def local_kernel(heads, size, count, q_ref, k_ref, v_ref, index_ref, table_ref, level_ref, out_ref):
    n = pl.program_id(0)
    tiles = STRETCH // LANES
    tile_bits = bit_count(LANES)
    block_bits = bit_count(STRETCH)
    weights = spread_weights(index_ref[0], table_ref[...])
    row = lax.broadcasted_iota(jnp.int32, (LANES, LANES), 0)
    col = lax.broadcasted_iota(jnp.int32, (LANES, LANES), 1)
    across = row ^ col
    level = jnp.zeros_like(row)
    for b in range(tile_bits):
        level = level + (across >= (1 << b)).astype(jnp.int32)
    level = jnp.where(col <= row, level, LANES - 1)
    for h in range(heads):
        cols = slice(h * size, (h + 1) * size)
        q = q_ref[:, cols]
        k = k_ref[:, cols]
        v = v_ref[:, cols]
        w = weights[:, h * LANES : (h + 1) * LANES]
        scores = lax.dot_general(
            q, k, (((1,), (1,)), ((), ())), preferred_element_type=jnp.float32
        )
        parts = []
        for i in range(tiles):
            rows = slice(i * LANES, (i + 1) * LANES)
            w_tile = w[rows]
            total = None
            pieces = []
            for j in range(i + 1):
                s = scores[rows, j * LANES : (j + 1) * LANES]
                if j == i:
                    factor = jnp.take_along_axis(w_tile, level, axis=1)
                else:
                    at = tile_bits + (i ^ j).bit_length()
                    factor = w_tile[:, at : at + 1]
                pieces.append((s * factor).astype(jnp.bfloat16))
            weighted = pieces[0] if i == 0 else jnp.concatenate(pieces, axis=1)
            parts.append(dot(weighted, v[: (i + 1) * LANES]))
        total = jnp.concatenate(parts, axis=0)
        first = 0
        for b in range(bit_count(count)):
            inside = ((n >> b) & 1).astype(jnp.float32)
            reached = dot(q, level_ref[first + (n >> (b + 1)), h])
            at = block_bits + 1 + b
            total = total + reached * (w[:, at : at + 1] * inside)
            first += count >> (b + 1)
        out_ref[:, cols] = total.astype(out_ref.dtype)


def local_attention(queries, keys, values, index_rows, table, levels):
    tokens, width = queries.shape
    count = tokens // STRETCH
    heads, size = levels.shape[1], levels.shape[3]
    rows = pl.BlockSpec((STRETCH, width), lambda n: (n, 0))
    return pl.pallas_call(
        functools.partial(local_kernel, heads, size, count),
        grid=(count,),
        in_specs=[
            rows,
            rows,
            rows,
            pl.BlockSpec((1, 1, STRETCH), lambda n: (n, 0, 0)),
            pl.BlockSpec(table.shape, lambda n: (0, 0)),
            pl.BlockSpec(levels.shape, lambda n: (0, 0, 0, 0)),
        ],
        out_specs=rows,
        out_shape=jax.ShapeDtypeStruct((tokens, width), jnp.bfloat16),
        compiler_params=pltpu.CompilerParams(vmem_limit_bytes=24 * MIB),
        cost_estimate=pl.CostEstimate(
            flops=2 * tokens * heads * size * (2 * STRETCH + 3 * size),
            bytes_accessed=8 * tokens * width,
            transcendentals=0,
        ),
        name="local_attention",
    )(queries, keys, values, index_rows, table, levels)


def finish_kernel(heads, size, first, remotes, s_ref, q_ref, local_ref, index_ref, table_ref, *refs):
    state_refs, out_ref = refs[:remotes], refs[remotes]
    weights = spread_weights(index_ref[0], table_ref[...])
    for h in range(heads):
        cols = slice(h * size, (h + 1) * size)
        q = q_ref[:, cols]
        w = weights[:, h * LANES : (h + 1) * LANES]
        total = local_ref[:, cols].astype(jnp.float32)
        for b in range(remotes):
            inside = s_ref[1 + b].astype(jnp.float32)
            reached = dot(q, state_refs[b][cols, :])
            total = total + reached * (w[:, first + b : first + b + 1] * inside)
        scale = lax.rsqrt(jnp.mean(total * total, axis=1, keepdims=True) + EPSILON)
        out_ref[:, cols] = (total * scale).astype(out_ref.dtype)


def finish_rows(scalars, rows, queries, local, index_rows, table, states, first):
    tokens, width = queries.shape
    size = states[0].shape[1]
    heads = width // size
    step = min(STRETCH, rows)
    steps = rows // step
    take = pl.BlockSpec((step, width), lambda i, s: (s[0] * steps + i, 0))
    whole = lambda a: pl.BlockSpec(a.shape, lambda i, s: (0,) * a.ndim)
    return pl.pallas_call(
        functools.partial(finish_kernel, heads, size, first, len(states)),
        grid_spec=pltpu.PrefetchScalarGridSpec(
            num_scalar_prefetch=1,
            grid=(steps,),
            in_specs=[
                take,
                take,
                pl.BlockSpec((1, 1, step), lambda i, s: (s[0] * steps + i, 0, 0)),
                whole(table),
            ]
            + [whole(a) for a in states],
            out_specs=pl.BlockSpec((step, width), lambda i, s: (i, 0)),
        ),
        out_shape=jax.ShapeDtypeStruct((rows, width), jnp.bfloat16),
        compiler_params=pltpu.CompilerParams(vmem_limit_bytes=24 * MIB),
        cost_estimate=pl.CostEstimate(
            flops=2 * rows * width * size * len(states),
            bytes_accessed=6 * rows * width,
            transcendentals=rows,
        ),
        name="finish_rows",
    )(scalars, queries, local, index_rows, table, *states)


def project_kernel(parts, has_total, s_ref, *refs):
    a_refs, w_refs = refs[:parts], refs[parts : 2 * parts]
    out_ref = refs[-1]
    total = refs[2 * parts][...] if has_total else None
    for a_ref, w_ref in zip(a_refs, w_refs):
        piece = dot(a_ref[...], w_ref[...])
        total = piece if total is None else total + piece
    out_ref[...] = total.astype(out_ref.dtype)


def project(scalars, pairs, total, dtype, tile=512):
    rows = pairs[0][0].shape[0]
    columns = pairs[0][1].shape[1]
    tile = min(tile, columns)

    def a_spec(a, w, at):
        depth = w.shape[0]
        if at is None:
            return pl.BlockSpec((rows, depth), lambda i, s: (0, 0))
        return pl.BlockSpec((rows, depth), lambda i, s: (0, s[at]))

    out = pl.BlockSpec((rows, tile), lambda i, s: (0, i))
    flops = sum(2 * rows * w.shape[0] * columns for _, w, _ in pairs)
    return pl.pallas_call(
        functools.partial(project_kernel, len(pairs), total is not None),
        grid_spec=pltpu.PrefetchScalarGridSpec(
            num_scalar_prefetch=1,
            grid=(columns // tile,),
            in_specs=[a_spec(*p) for p in pairs]
            + [pl.BlockSpec((w.shape[0], tile), lambda i, s: (0, i)) for _, w, _ in pairs]
            + ([out] if total is not None else []),
            out_specs=out,
        ),
        out_shape=jax.ShapeDtypeStruct((rows, columns), dtype),
        compiler_params=pltpu.CompilerParams(vmem_limit_bytes=32 * MIB),
        cost_estimate=pl.CostEstimate(
            flops=flops, bytes_accessed=flops // rows, transcendentals=0
        ),
        name="project",
    )(scalars, *[a for a, _, _ in pairs], *[w for _, w, _ in pairs], *([] if total is None else [total]))


def flip(x, axis, bits):
    n = lax.axis_size(axis)
    return lax.ppermute(x, axis, [(i, i ^ bits) for i in range(n)])


def add_rounded(*arrays):
    total = arrays[0].astype(jnp.float32)
    for a in arrays[1:]:
        total = total + a.astype(jnp.float32)
    return total.astype(jnp.bfloat16)


def body(queries, key_vectors, value_vectors, level_index, level_table, out_weight):
    tokens, width = queries.shape
    plans, heads, level_total = level_table.shape
    size = width // heads
    ctx_size, mp_size = lax.axis_size("ctx"), lax.axis_size("mp")
    ctx_bits = bit_count(ctx_size)
    position, me = lax.axis_index("ctx"), lax.axis_index("mp")
    count = tokens // STRETCH
    first = bit_count(STRETCH) + 1 + bit_count(count)

    table = jnp.pad(level_table, ((0, 0), (0, 0), (0, LANES - level_total))).reshape(
        plans, heads * LANES
    )
    index_rows = level_index.reshape(count, 1, STRETCH)

    levels, own = block_states(key_vectors, value_vectors, heads, size)

    remote = []
    near = [flip(own, "ctx", b) for b in range(1, min(4, ctx_size))]
    if ctx_bits > 0:
        remote.append(near[0])
    if ctx_bits > 1:
        remote.append(add_rounded(near[1], near[2]))
    running = add_rounded(own, *near) if ctx_bits > 2 else None
    for b in range(2, ctx_bits):
        far = flip(running, "ctx", 1 << b)
        remote.append(far)
        if b + 1 < ctx_bits:
            running = add_rounded(running, far)

    weight, _ = lax.optimization_barrier((out_weight, own))
    depth = out_weight.shape[0]
    half = depth // 2
    mine = lax.rem(position, 2)
    gathered = {0: [(weight, None)]}
    if mp_size > 1:
        gathered[1] = [(flip(weight, "mp", 1), None)]
    for j in range(2, mp_size, 2):
        part = lax.dynamic_slice_in_dim(weight, mine * half, half, axis=0)
        got = flip(part, "mp", j)
        other = flip(got, "ctx", 1)
        gathered[j] = [(got, 0), (other, 1)]
        gathered[j + 1] = [(flip(got, "mp", 1), 0), (flip(other, "mp", 1), 1)]

    local = local_attention(queries, key_vectors, value_vectors, index_rows, table, levels)

    bits = [(position >> b) & 1 for b in range(ctx_bits)]
    rows = tokens // mp_size

    def finished(j):
        scalars = jnp.stack([me ^ j] + bits).astype(jnp.int32)
        return finish_rows(scalars, rows, queries, local, index_rows, table, remote, first)

    order = list(range(2, mp_size)) + list(range(1, min(2, mp_size)))
    received = {}
    for j in order:
        received[j] = flip(finished(j), "mp", j)
    received[0] = finished(0)

    places = jnp.stack([mine, 1 - mine]).astype(jnp.int32)
    tail = order[-2] if mp_size > 2 else 0
    total = None
    early = [j for j in range(mp_size) if j != tail]
    if early:
        pairs = [(received[j], w, at) for j in early for w, at in gathered[j]]
        total = project(places, pairs, None, jnp.float32)
    pairs = [(received[tail], w, at) for w, at in gathered[tail]]
    return project(places, pairs, total, jnp.bfloat16)


def solution(mesh):
    placed = (
        P("ctx", "mp"),
        P("ctx", "mp"),
        P("ctx", "mp"),
        P("ctx"),
        P(None, "mp", None),
        P("mp", None),
    )
    return jax.shard_map(
        body, mesh=mesh, in_specs=placed, out_specs=P(("ctx", "mp"), None), check_vma=False
    )
```

time: 188 us -> 118 us (0.63)
  matrix products: 45.5 us -> 0 us
  Pallas kernels: 0 us -> 35.4 us
  local copies, waits for them, and re-layouts: 44.4 us -> 14.8 us
  waiting for transfers between devices: 78.8 us -> 53.3 us
  between operations: 13.6 us -> 0.13 us
  starting transfers between devices: 0.04 us -> 13 us
  other arithmetic: 4.98 us -> 0.47 us
    reduce_scatter x1 -> x0, waiting for transfers between devices: 70.6 us -> none  [body(): lax.psum_scatter(jnp.dot(mixed_heads, out_weight, preferred_element_type=...]
    ppermute x0 -> x12, waiting for transfers between devices: none -> 53.3 us  [flip(): return lax.ppermute(x, axis, [(i, i ^ bits) for i in range(n)])]
    dot_general x7 -> x0, matrix products: 45.5 us -> none  [the longest x1 15.6 us: body(): jnp.einsum('nhts,nhse->nhte', weighted, value_blocks, preferred_element_t...]
    pallas_call x0 -> x8, Pallas kernels: none -> 35.4 us  [the longest x4 12 us: finish_rows(): pl.pallas_call(functools.partial(finish_kernel, heads, size, first, len(s...]
    ppermute x0 -> x12, starting transfers between devices: none -> 13 us  [flip(): return lax.ppermute(x, axis, [(i, i ^ bits) for i in range(n)])]
    reshape x4 -> x0, local copies, waits for them, and re-layouts: 12.1 us -> none  [the longest x1 4.1 us: body(): key_vectors.reshape(stretch_count, STRETCH, heads_here, head_size)]
    slice x8 -> x0, local copies, waits for them, and re-layouts: 8.88 us -> none  [the longest x2 6.2 us: body(): weight_blocks[..., :stretch_bits + 1]]
    all_gather x1 -> x0, waiting for transfers between devices: 8.18 us -> none  [body(): lax.all_gather(own_total[None].astype(jnp.bfloat16), 'ctx', axis=0, tiled...]
  transfers between devices with their start and end apart: 2 -> 12, of which waited for: 2 -> 4; matrix products, arithmetic and copies ran while one was open for 19% -> 0% of each run, Pallas kernels for 0% -> 24%
where the time goes in v1:
time: 118 us; the launch traced here: 117 us
  waiting for transfers between devices  53.3 us (45%)
  Pallas kernels  35.4 us (30%)
  local copies, waits for them, and re-layouts  14.8 us (13%)
  starting transfers between devices  13 us (11%)
    ppermute x12, waiting for transfers between devices, flip(): return lax.ppermute(x, axis, [(i, i ^ bits) for i in range(n)])  53.3 us
    unnamed x29, local copies, waits for them, and re-layouts  13.4 us
    ppermute x12, starting transfers between devices, flip(): return lax.ppermute(x, axis, [(i, i ^ bits) for i in range(n)])  13 us
    pallas_call x4, Pallas kernels, finish_rows(): pl.pallas_call(functools.partial(finish_kernel, heads, size, first, len(s...  12 us
    pallas_call x2, Pallas kernels, project(): pl.pallas_call(functools.partial(project_kernel, len(pairs), total is not...  11.6 us
    pallas_call x1, Pallas kernels, local_attention(): pl.pallas_call(functools.partial(local_kernel, heads, size, count), grid=...  9.58 us
  transfers between devices with their start and end apart: 12, of which 4 were waited for; matrix products, arithmetic and copies ran while one was open for 0% of the time, Pallas kernels for 24%

profile of v1, /device:TPU:0, one launch (start us, length us, event | category | flops | bytes accessed | tf_op | source)
XLA Modules:
  0.0 117.1 jit_solution(3117242273516840240)
XLA Ops:
  0.0 0.0 copy-start.5
  0.0 1.6 %copy-done.5 = bf16[2048,512]{1,0:T(8,128)(2,1)S(1)} copy-done((bf16[2048,512]{1,0:T(8,128)(2,1)S(1)}, bf16[2048,512]{1,0:T(8,128)(2,1)}, u32[]{:S(2)}) %copy-start.5) | copy-done | bytes 2097176
  1.6 0.0 copy-start.7
  1.6 1.6 %copy-done.7 = bf16[2048,512]{1,0:T(8,128)(2,1)S(1)} copy-done((bf16[2048,512]{1,0:T(8,128)(2,1)S(1)}, bf16[2048,512]{1,0:T(8,128)(2,1)}, u32[]{:S(2)}) %copy-start.7) | copy-done | bytes 2097176
  3.2 0.0 copy-start.13
  3.2 2.2 %block_states.1 = (bf16[7,4,128,128]{3,2,1,0:T(8,128)(2,1)S(1)}, bf16[512,128]{1,0:T(8,128)(2,1)S(1)}) custom-call(bf16[2048,512]{1,0:T(8,128)(2,1)S(1)} %copy-done.5, bf16[2048,512]{1,0:T(8,128)(2,1)S(1)} %copy-done.7), custom_call_target="tpu_custom_call" | custom-call | flops 268435456 | bytes 4194304 | tf_op jit(solution)/shard_map/block_states/pallas_call | solution.py:47
  5.4 0.0 copy-start.10
  5.4 0.9 copy-done.10
  6.3 0.0 copy-start
  6.3 0.0 copy-start.12
  6.4 1.4 %constant_dynamic-slice_fusion = bf16[256,2048]{1,0:T(8,128)(2,1)S(1)} fusion(bf16[512,2048]{1,0:T(8,128)(2,1)} %refs_4_, s32[]{:T(128)S(6)} %select_n.3), kind=kLoop, calls=%fused_computation.11 | loop fusion | bytes 2097156 | tf_op jit(solution)/shard_map/dynamic_slice | solution.py:300
  7.8 3.0 %collective-permute-start.5 = (bf16[256,2048]{1,0:T(8,128)(2,1)S(1)}, bf16[256,2048]{1,0:T(8,128)(2,1)}, u32[]{:S(2)}, u32[]{:S(2)}) collective-permute-start(bf16[256,2048]{1,0:T(8,128)(2,1)S(1)} %constant_dynamic-slice_fusion), channel_id=1, source_target_pairs={{0,2},{1,3},{2,0},{3,1},{4,6},{5,7},{6,4},{7,5},{8,10},{9,11},{10,... | collective-permute-start | bytes 3145736 | tf_op jit(solution)/shard_map/ppermute | solution.py:252
  10.8 0.0 collective-permute-start.11
  10.8 23.3 %collective-permute-done.5.refs_6_ = bf16[256,2048]{1,0:T(8,128)(2,1)} collective-permute-done((bf16[256,2048]{1,0:T(8,128)(2,1)S(1)}, bf16[256,2048]{1,0:T(8,128)(2,1)}, u32[]{:S(2)}, u32[]{:S(2)}) %collective-permute-start.5) | collective-permute-done | bytes 1048608 | tf_op jit(solution)/shard_map/ppermute | solution.py:252
  34.1 1.8 %collective-permute-start.7 = (bf16[256,2048]{1,0:T(8,128)(2,1)}, bf16[256,2048]{1,0:T(8,128)(2,1)}, u32[]{:S(2)}, u32[]{:S(2)}) collective-permute-start(bf16[256,2048]{1,0:T(8,128)(2,1)} %collective-permute-done.5.refs_6_), channel_id=1, source_target_pairs={{0,4},{4,0},{8,12},{12,8},{16,20},{20,16},{24,28},{28,24},{1,5},{5... | collective-permute-start | bytes 3145736 | tf_op jit(solution)/shard_map/ppermute | solution.py:252
  35.8 0.3 collective-permute-start
  36.1 1.8 %collective-permute-start.1 = (bf16[512,128]{1,0:T(8,128)(2,1)S(1)}, bf16[512,128]{1,0:T(8,128)(2,1)S(1)}, u32[]{:S(2)}, u32[]{:S(2)}) collective-permute-start(bf16[512,128]{1,0:T(8,128)(2,1)S(1)} %get-tuple-element.9), channel_id=1, source_target_pairs={{0,8},{4,12},{8,0},{12,4},{16,24},{20,28},{24,16},{28,20},{1,9},{5... | collective-permute-start | bytes 393224 | tf_op jit(solution)/shard_map/ppermute | solution.py:252
  37.9 1.4 %collective-permute-start.2 = (bf16[512,128]{1,0:T(8,128)(2,1)S(1)}, bf16[512,128]{1,0:T(8,128)(2,1)S(1)}, u32[]{:S(2)}, u32[]{:S(2)}) collective-permute-start(bf16[512,128]{1,0:T(8,128)(2,1)S(1)} %get-tuple-element.9), channel_id=1, source_target_pairs={{0,12},{4,8},{8,4},{12,0},{16,28},{20,24},{24,20},{28,16},{1,13},{... | collective-permute-start | bytes 393224 | tf_op jit(solution)/shard_map/ppermute | solution.py:252
  39.3 0.0 copy-done.13
  39.4 24.9 %collective-permute-done.refs_0_ = bf16[512,128]{1,0:T(8,128)(2,1)S(1)} collective-permute-done((bf16[512,128]{1,0:T(8,128)(2,1)S(1)}, bf16[512,128]{1,0:T(8,128)(2,1)S(1)}, u32[]{:S(2)}, u32[]{:S(2)}) %collective-permute-start) | collective-permute-done | bytes 131104 | tf_op jit(solution)/shard_map/ppermute | solution.py:252
  64.2 0.0 collective-permute-done.1
  64.2 0.0 collective-permute-done.2
  64.2 0.1 fusion.1
  64.3 2.6 %collective-permute-start.3 = (bf16[512,128]{1,0:T(8,128)(2,1)S(1)}, bf16[512,128]{1,0:T(8,128)(2,1)S(1)}, u32[]{:S(2)}, u32[]{:S(2)}) collective-permute-start(bf16[512,128]{1,0:T(8,128)(2,1)S(1)} %get-tuple-element.11), channel_id=1, source_target_pairs={{0,16},{4,20},{8,24},{12,28},{16,0},{20,4},{24,8},{28,12},{1,17},{... | collective-permute-start | bytes 393224 | tf_op jit(solution)/shard_map/ppermute | solution.py:252
  66.9 0.0 copy-done
  66.9 0.0 copy-done.12
  66.9 0.0 copy-done.11
  66.9 0.0 copy-start.6
  66.9 1.6 %copy-done.6 = bf16[2048,512]{1,0:T(8,128)(2,1)S(1)} copy-done((bf16[2048,512]{1,0:T(8,128)(2,1)S(1)}, bf16[2048,512]{1,0:T(8,128)(2,1)}, u32[]{:S(2)}) %copy-start.6) | copy-done | bytes 2097176
  68.5 0.0 copy-start.8
  68.5 1.6 %copy-done.8 = bf16[2048,512]{1,0:T(8,128)(2,1)S(1)} copy-done((bf16[2048,512]{1,0:T(8,128)(2,1)S(1)}, bf16[2048,512]{1,0:T(8,128)(2,1)}, u32[]{:S(2)}) %copy-start.8) | copy-done | bytes 2097176
  70.1 9.6 %local_attention.1.local_ref = bf16[2048,512]{1,0:T(8,128)(2,1)S(1)} custom-call(bf16[2048,512]{1,0:T(8,128)(2,1)S(1)} %copy-done, bf16[2048,512]{1,0:T(8,128)(2,1)S(1)} %copy-done.6, bf16[2048,512]{1,0:T(8,128)(2,1)S(1)} %copy-done.8, s32[8,1,256]{2,1,0:T(1,128)S(1)} %bitcast.19, f32[16,512]{1,0:T(8,128)S(1)} %bitcast.14, ...), custom_call_target="tpu_custom_call" | custom-call | flops 1879048192 | bytes 8388608 | tf_op jit(solution)/shard_map/local_attention/pallas_call | solution.py:136
  79.7 0.0 copy-start.1
  79.7 1.3 %copy-done.1 = bf16[2048,512]{1,0:T(8,128)(2,1)} copy-done((bf16[2048,512]{1,0:T(8,128)(2,1)}, bf16[2048,512]{1,0:T(8,128)(2,1)S(1)}, u32[]{:S(2)}) %copy-start.1) | copy-done | bytes 2097176
  81.0 0.1 add_add_fusion.3.s_ref
  81.1 0.0 collective-permute-done.3.refs_2_
  81.1 0.0 copy-start.2
  81.1 1.6 %copy-done.2 = bf16[2048,512]{1,0:T(8,128)(2,1)S(1)} copy-done((bf16[2048,512]{1,0:T(8,128)(2,1)S(1)}, bf16[2048,512]{1,0:T(8,128)(2,1)}, u32[]{:S(2)}) %copy-start.2) | copy-done | bytes 2097176
  82.7 3.3 %finish_rows.7 = bf16[512,512]{1,0:T(8,128)(2,1)} custom-call(s32[4]{0:T(128)S(1)} %add_add_fusion.3.s_ref, bf16[2048,512]{1,0:T(8,128)(2,1)S(1)} %copy-done, bf16[2048,512]{1,0:T(8,128)(2,1)S(1)} %copy-done.2, s32[8,1,256]{2,1,0:T(1,128)S(1)} %bitcast.20, f32[16,512]{1,0:T(8,128)S(1)} %bitcast.15, bf16[512,128]{1,0:T(8,128)(2,1)S(1)} %collective-permute-done.refs_0_, ...), custom_call_target="tpu_custom_call" | custom-call | flops 201326592 | bytes 1572864 | tf_op jit(solution)/shard_map/finish_rows/pallas_call | solution.py:183
  86.0 1.5 %collective-permute-start.10 = (bf16[512,512]{1,0:T(8,128)(2,1)}, bf16[512,512]{1,0:T(8,128)(2,1)S(1)}, u32[]{:S(2)}, u32[]{:S(2)}) collective-permute-start(bf16[512,512]{1,0:T(8,128)(2,1)} %finish_rows.7), channel_id=1, source_target_pairs={{0,2},{1,3},{2,0},{3,1},{4,6},{5,7},{6,4},{7,5},{8,10},{9,11},{10,... | collective-permute-start | bytes 1572872 | tf_op jit(solution)/shard_map/ppermute | solution.py:252
  87.5 0.0 collective-permute-start.6
  87.5 0.0 collective-permute-done.7.refs_7_
  87.5 0.5 collective-permute-start.8
  88.1 0.1 add_add_fusion.2.s_ref
  88.1 0.0 copy-start.3
  88.1 1.6 %copy-done.3 = bf16[2048,512]{1,0:T(8,128)(2,1)S(1)} copy-done((bf16[2048,512]{1,0:T(8,128)(2,1)S(1)}, bf16[2048,512]{1,0:T(8,128)(2,1)}, u32[]{:S(2)}) %copy-start.3) | copy-done | bytes 2097176
  89.7 3.3 %finish_rows.6 = bf16[512,512]{1,0:T(8,128)(2,1)} custom-call(s32[4]{0:T(128)S(1)} %add_add_fusion.2.s_ref, bf16[2048,512]{1,0:T(8,128)(2,1)S(1)} %copy-done, bf16[2048,512]{1,0:T(8,128)(2,1)S(1)} %copy-done.3, s32[8,1,256]{2,1,0:T(1,128)S(1)} %bitcast.21, f32[16,512]{1,0:T(8,128)S(1)} %bitcast.16, bf16[512,128]{1,0:T(8,128)(2,1)S(1)} %collective-permute-done.refs_0_, ...), custom_call_target="tpu_custom_call" | custom-call | flops 201326592 | bytes 1572864 | tf_op jit(solution)/shard_map/finish_rows/pallas_call | solution.py:183
  93.1 0.0 collective-permute-start.9
  93.1 0.1 add_add_fusion.s_ref
  93.1 1.6 %copy-done.4 = bf16[2048,512]{1,0:T(8,128)(2,1)S(1)} copy-done((bf16[2048,512]{1,0:T(8,128)(2,1)S(1)}, bf16[2048,512]{1,0:T(8,128)(2,1)}, u32[]{:S(2)}) %copy-start.4) | copy-done | bytes 2097176
  94.7 2.6 %finish_rows.4 = bf16[512,512]{1,0:T(8,128)(2,1)S(1)} custom-call(s32[4]{0:T(128)S(1)} %add_add_fusion.s_ref, bf16[2048,512]{1,0:T(8,128)(2,1)S(1)} %copy-done, bf16[2048,512]{1,0:T(8,128)(2,1)S(1)} %copy-done.4, s32[8,1,256]{2,1,0:T(1,128)S(1)} %bitcast.22, f32[16,512]{1,0:T(8,128)S(1)} %bitcast.17, bf16[512,128]{1,0:T(8,128)(2,1)S(1)} %collective-permute-done.refs_0_, ...), custom_call_target="tpu_custom_call" | custom-call | flops 201326592 | bytes 1572864 | tf_op jit(solution)/shard_map/finish_rows/pallas_call | solution.py:183
  97.4 0.6 collective-permute-done.10.refs_2_.refs_3_
  97.9 0.2 collective-permute-start.4
  98.1 0.1 add_add_fusion.1.s_ref
  98.2 0.1 pad_add_fusion.s_ref
  98.3 2.6 %finish_rows.5.refs_0_ = bf16[512,512]{1,0:T(8,128)(2,1)S(1)} custom-call(s32[4]{0:T(128)S(1)} %add_add_fusion.1.s_ref, bf16[2048,512]{1,0:T(8,128)(2,1)S(1)} %copy-done, bf16[2048,512]{1,0:T(8,128)(2,1)S(1)} %copy-done.4, s32[8,1,256]{2,1,0:T(1,128)S(1)} %bitcast.23, f32[16,512]{1,0:T(8,128)S(1)} %bitcast.18, ...), custom_call_target="tpu_custom_call" | custom-call | flops 201326592 | bytes 1572864 | tf_op jit(solution)/shard_map/finish_rows/pallas_call | solution.py:183
  100.9 0.0 collective-permute-done.9.refs_1_
  100.9 0.0 collective-permute-done.11.refs_5_
  100.9 0.0 copy-done.9
  101.0 6.5 %project.2.refs_4_ = f32[512,2048]{1,0:T(8,128)S(1)} custom-call(s32[2]{0:T(128)S(1)} %pad_add_fusion.s_ref, bf16[512,512]{1,0:T(8,128)(2,1)S(1)} %finish_rows.5.refs_0_, bf16[512,512]{1,0:T(8,128)(2,1)} %collective-permute-done.9.refs_1_, bf16[512,512]{1,0:T(8,128)(2,1)S(1)} %collective-permute-done.10.refs_2_.refs_3_, ...), custom_call_target="tpu_custom_call" | custom-call | flops 3221225472 | bytes 6291456 | tf_op jit(solution)/shard_map/project/pallas_call | solution.py:231
  107.4 4.5 %collective-permute-done.4.refs_0_.refs_1_ = bf16[512,512]{1,0:T(8,128)(2,1)S(1)} collective-permute-done((bf16[512,512]{1,0:T(8,128)(2,1)S(1)}, bf16[512,512]{1,0:T(8,128)(2,1)S(1)}, u32[]{:S(2)}, u32[]{:S(2)}) %collective-permute-start.4) | collective-permute-done | bytes 524320 | tf_op jit(solution)/shard_map/ppermute | solution.py:252
  112.0 0.0 collective-permute-done.6.refs_2_
  112.0 0.0 collective-permute-done.8.refs_3_
  112.0 5.1 %project.3 = bf16[512,2048]{1,0:T(8,128)(2,1)} custom-call(s32[2]{0:T(128)S(1)} %pad_add_fusion.s_ref, bf16[512,512]{1,0:T(8,128)(2,1)S(1)} %collective-permute-done.4.refs_0_.refs_1_, bf16[512,512]{1,0:T(8,128)(2,1)S(1)} %collective-permute-done.4.refs_0_.refs_1_, bf16[256,2048]{1,0:T(8,128)(2,1)} %collective-permute-done.6.refs_2_, ...), custom_call_target="tpu_custom_call" | custom-call | flops 1073741824 | bytes 2097152 | tf_op jit(solution)/shard_map/project/pallas_call | solution.py:231
  (5 shorter events, 0.0 us)
Async XLA Ops:
  0.0 1.6 %copy-start.5 = (bf16[2048,512]{1,0:T(8,128)(2,1)S(1)}, bf16[2048,512]{1,0:T(8,128)(2,1)}, u32[]{:S(2)}) copy-start(bf16[2048,512]{1,0:T(8,128)(2,1)} %k_ref.3) | copy-start | bytes 6291460
  1.6 1.6 %copy-start.7 = (bf16[2048,512]{1,0:T(8,128)(2,1)S(1)}, bf16[2048,512]{1,0:T(8,128)(2,1)}, u32[]{:S(2)}) copy-start(bf16[2048,512]{1,0:T(8,128)(2,1)} %v_ref.3) | copy-start | bytes 6291460
  3.2 36.1 %copy-start.13 = (f32[16,4,20]{2,1,0:T(4,128)S(1)}, f32[16,4,20]{2,1,0:T(4,128)}, u32[]{:S(2)}) copy-start(f32[16,4,20]{2,1,0:T(4,128)} %param.10) | copy-start | bytes 15364
  5.4 0.9 copy-start.10
  6.3 60.6 %copy-start = (bf16[2048,512]{1,0:T(8,128)(2,1)S(1)}, bf16[2048,512]{1,0:T(8,128)(2,1)}, u32[]{:S(2)}) copy-start(bf16[2048,512]{1,0:T(8,128)(2,1)} %q_ref.9) | copy-start | bytes 6291460
  6.3 60.6 %copy-start.12 = (s32[2048]{0:T(1024)S(1)}, s32[2048]{0:T(1024)}, u32[]{:S(2)}) copy-start(s32[2048]{0:T(1024)} %param.9) | copy-start | bytes 24580
  6.4 60.6 %copy-start.11 = (bf16[7,4,128,128]{3,2,1,0:T(8,128)(2,1)S(1)}, bf16[7,4,128,128]{3,2,1,0:T(8,128)(2,1)}, u32[]{:S(2)}) copy-start(bf16[7,4,128,128]{3,2,1,0:T(8,128)(2,1)} %copy-done.10) | copy-start | bytes 2752516
  7.8 26.3 %collective-permute-start.5 = (bf16[256,2048]{1,0:T(8,128)(2,1)S(1)}, bf16[256,2048]{1,0:T(8,128)(2,1)}, u32[]{:S(2)}, u32[]{:S(2)}) collective-permute-start(bf16[256,2048]{1,0:T(8,128)(2,1)S(1)} %constant_dynamic-slice_fusion), channel_id=1, source_target_pairs={{0,2},{1,3},{2,0},{3,1},{4,6},{5,7},{6,4},{7,5},{8,10},{9,11},{10,... | collective-permute-start | bytes 3145736 | tf_op jit(solution)/shard_map/ppermute | solution.py:252
  10.8 90.1 %collective-permute-start.11 = (bf16[512,2048]{1,0:T(8,128)(2,1)}, bf16[512,2048]{1,0:T(8,128)(2,1)}, u32[]{:S(2)}, u32[]{:S(2)}) collective-permute-start(bf16[512,2048]{1,0:T(8,128)(2,1)} %refs_4_), channel_id=1, source_target_pairs={{0,1},{1,0},{2,3},{3,2},{4,5},{5,4},{6,7},{7,6},{8,9},{9,8},{10,11... | collective-permute-start | bytes 6291464 | tf_op jit(solution)/shard_map/ppermute | solution.py:252
  34.1 53.5 %collective-permute-start.7 = (bf16[256,2048]{1,0:T(8,128)(2,1)}, bf16[256,2048]{1,0:T(8,128)(2,1)}, u32[]{:S(2)}, u32[]{:S(2)}) collective-permute-start(bf16[256,2048]{1,0:T(8,128)(2,1)} %collective-permute-done.5.refs_6_), channel_id=1, source_target_pairs={{0,4},{4,0},{8,12},{12,8},{16,20},{20,16},{24,28},{28,24},{1,5},{5... | collective-permute-start | bytes 3145736 | tf_op jit(solution)/shard_map/ppermute | solution.py:252
  35.8 28.4 %collective-permute-start = (bf16[512,128]{1,0:T(8,128)(2,1)S(1)}, bf16[512,128]{1,0:T(8,128)(2,1)S(1)}, u32[]{:S(2)}, u32[]{:S(2)}) collective-permute-start(bf16[512,128]{1,0:T(8,128)(2,1)S(1)} %get-tuple-element.9), channel_id=1, source_target_pairs={{0,4},{4,0},{8,12},{12,8},{16,20},{20,16},{24,28},{28,24},{1,5},{5... | collective-permute-start | bytes 393224 | tf_op jit(solution)/shard_map/ppermute | solution.py:252
  36.1 28.1 %collective-permute-start.1 = (bf16[512,128]{1,0:T(8,128)(2,1)S(1)}, bf16[512,128]{1,0:T(8,128)(2,1)S(1)}, u32[]{:S(2)}, u32[]{:S(2)}) collective-permute-start(bf16[512,128]{1,0:T(8,128)(2,1)S(1)} %get-tuple-element.9), channel_id=1, source_target_pairs={{0,8},{4,12},{8,0},{12,4},{16,24},{20,28},{24,16},{28,20},{1,9},{5... | collective-permute-start | bytes 393224 | tf_op jit(solution)/shard_map/ppermute | solution.py:252
  37.9 26.3 %collective-permute-start.2 = (bf16[512,128]{1,0:T(8,128)(2,1)S(1)}, bf16[512,128]{1,0:T(8,128)(2,1)S(1)}, u32[]{:S(2)}, u32[]{:S(2)}) collective-permute-start(bf16[512,128]{1,0:T(8,128)(2,1)S(1)} %get-tuple-element.9), channel_id=1, source_target_pairs={{0,12},{4,8},{8,4},{12,0},{16,28},{20,24},{24,20},{28,16},{1,13},{... | collective-permute-start | bytes 393224 | tf_op jit(solution)/shard_map/ppermute | solution.py:252
  64.3 16.8 %collective-permute-start.3 = (bf16[512,128]{1,0:T(8,128)(2,1)S(1)}, bf16[512,128]{1,0:T(8,128)(2,1)S(1)}, u32[]{:S(2)}, u32[]{:S(2)}) collective-permute-start(bf16[512,128]{1,0:T(8,128)(2,1)S(1)} %get-tuple-element.11), channel_id=1, source_target_pairs={{0,16},{4,20},{8,24},{12,28},{16,0},{20,4},{24,8},{28,12},{1,17},{... | collective-permute-start | bytes 393224 | tf_op jit(solution)/shard_map/ppermute | solution.py:252
  66.9 1.6 %copy-start.6 = (bf16[2048,512]{1,0:T(8,128)(2,1)S(1)}, bf16[2048,512]{1,0:T(8,128)(2,1)}, u32[]{:S(2)}) copy-start(bf16[2048,512]{1,0:T(8,128)(2,1)} %k_ref.3) | copy-start | bytes 6291460
  68.5 1.6 %copy-start.8 = (bf16[2048,512]{1,0:T(8,128)(2,1)S(1)}, bf16[2048,512]{1,0:T(8,128)(2,1)}, u32[]{:S(2)}) copy-start(bf16[2048,512]{1,0:T(8,128)(2,1)} %v_ref.3) | copy-start | bytes 6291460
  79.7 1.3 %copy-start.1 = (bf16[2048,512]{1,0:T(8,128)(2,1)}, bf16[2048,512]{1,0:T(8,128)(2,1)S(1)}, u32[]{:S(2)}) copy-start(bf16[2048,512]{1,0:T(8,128)(2,1)S(1)} %local_attention.1.local_ref) | copy-start | bytes 6291460
  81.1 1.6 %copy-start.2 = (bf16[2048,512]{1,0:T(8,128)(2,1)S(1)}, bf16[2048,512]{1,0:T(8,128)(2,1)}, u32[]{:S(2)}) copy-start(bf16[2048,512]{1,0:T(8,128)(2,1)} %copy-done.1) | copy-start | bytes 6291460
  86.0 11.9 %collective-permute-start.10 = (bf16[512,512]{1,0:T(8,128)(2,1)}, bf16[512,512]{1,0:T(8,128)(2,1)S(1)}, u32[]{:S(2)}, u32[]{:S(2)}) collective-permute-start(bf16[512,512]{1,0:T(8,128)(2,1)} %finish_rows.7), channel_id=1, source_target_pairs={{0,2},{1,3},{2,0},{3,1},{4,6},{5,7},{6,4},{7,5},{8,10},{9,11},{10,... | collective-permute-start | bytes 1572872 | tf_op jit(solution)/shard_map/ppermute | solution.py:252
  87.5 24.4 %collective-permute-start.6 = (bf16[256,2048]{1,0:T(8,128)(2,1)}, bf16[256,2048]{1,0:T(8,128)(2,1)}, u32[]{:S(2)}, u32[]{:S(2)}) collective-permute-start(bf16[256,2048]{1,0:T(8,128)(2,1)} %collective-permute-done.5.refs_6_), channel_id=1, source_target_pairs={{0,1},{1,0},{2,3},{3,2},{4,5},{5,4},{6,7},{7,6},{8,9},{9,8},{10,11... | collective-permute-start | bytes 3145736 | tf_op jit(solution)/shard_map/ppermute | solution.py:252
  87.5 24.4 %collective-permute-start.8 = (bf16[256,2048]{1,0:T(8,128)(2,1)}, bf16[256,2048]{1,0:T(8,128)(2,1)}, u32[]{:S(2)}, u32[]{:S(2)}) collective-permute-start(bf16[256,2048]{1,0:T(8,128)(2,1)} %collective-permute-done.7.refs_7_), channel_id=1, source_target_pairs={{0,1},{1,0},{2,3},{3,2},{4,5},{5,4},{6,7},{7,6},{8,9},{9,8},{10,11... | collective-permute-start | bytes 3145736 | tf_op jit(solution)/shard_map/ppermute | solution.py:252
  88.1 1.6 %copy-start.3 = (bf16[2048,512]{1,0:T(8,128)(2,1)S(1)}, bf16[2048,512]{1,0:T(8,128)(2,1)}, u32[]{:S(2)}) copy-start(bf16[2048,512]{1,0:T(8,128)(2,1)} %copy-done.1) | copy-start | bytes 6291460
  93.1 7.9 %collective-permute-start.9 = (bf16[512,512]{1,0:T(8,128)(2,1)}, bf16[512,512]{1,0:T(8,128)(2,1)}, u32[]{:S(2)}, u32[]{:S(2)}) collective-permute-start(bf16[512,512]{1,0:T(8,128)(2,1)} %finish_rows.6), channel_id=1, source_target_pairs={{0,1},{1,0},{2,3},{3,2},{4,5},{5,4},{6,7},{7,6},{8,9},{9,8},{10,11... | collective-permute-start | bytes 1572872 | tf_op jit(solution)/shard_map/ppermute | solution.py:252
  93.1 1.6 %copy-start.4 = (bf16[2048,512]{1,0:T(8,128)(2,1)S(1)}, bf16[2048,512]{1,0:T(8,128)(2,1)}, u32[]{:S(2)}) copy-start(bf16[2048,512]{1,0:T(8,128)(2,1)} %copy-done.1) | copy-start | bytes 6291460
  97.9 14.0 %collective-permute-start.4 = (bf16[512,512]{1,0:T(8,128)(2,1)S(1)}, bf16[512,512]{1,0:T(8,128)(2,1)S(1)}, u32[]{:S(2)}, u32[]{:S(2)}) collective-permute-start(bf16[512,512]{1,0:T(8,128)(2,1)S(1)} %finish_rows.4), channel_id=1, source_target_pairs={{0,3},{1,2},{2,1},{3,0},{4,7},{5,6},{6,5},{7,4},{8,11},{9,10},{10,... | collective-permute-start | bytes 1572872 | tf_op jit(solution)/shard_map/ppermute | solution.py:252
  98.3 2.7 %copy-start.9 = (bf16[512,2048]{1,0:T(8,128)(2,1)S(1)}, bf16[512,2048]{1,0:T(8,128)(2,1)}, u32[]{:S(2)}) copy-start(bf16[512,2048]{1,0:T(8,128)(2,1)} %refs_4_) | copy-start | bytes 6291460

commit v2 on v0

v2 whole, which is shorter than its diff:
```python
import functools

import jax
import jax.numpy as jnp
from jax import lax
from jax.experimental import pallas as pl
from jax.experimental.pallas import tpu as pltpu
from jax.sharding import PartitionSpec as P

STRETCH = 256
LANES = 128
EPSILON = 1e-06
MIB = 1024 * 1024
TILE = 512
HALVES = 2


def cost(us):
    return pl.CostEstimate(flops=int(us * 1e9), bytes_accessed=int(us * 3e6), transcendentals=0)


def call(kernel, out_shape, name, us, mib, anywhere_in=(), anywhere_out=(), n_in=0, **kw):
    vmem = pl.BlockSpec(memory_space=pltpu.VMEM)
    anywhere = pl.BlockSpec(memory_space=pl.ANY)
    out_specs = [anywhere if i in anywhere_out else vmem for i in range(len(out_shape))]
    return pl.pallas_call(
        kernel,
        in_specs=[anywhere if i in anywhere_in else vmem for i in range(n_in)],
        out_specs=out_specs,
        out_shape=out_shape,
        compiler_params=pltpu.CompilerParams(vmem_limit_bytes=mib * MIB),
        cost_estimate=cost(us),
        name=name,
        **kw,
    )


def bit_count(n):
    return n.bit_length() - 1


def contract_rows(a, b):
    return lax.dot_general(a, b, (((0,), (0,)), ((), ())), preferred_element_type=jnp.float32)


def dot(a, b):
    return jnp.dot(a, b, preferred_element_type=jnp.float32)


def slice_kernel(shared, w_ref, *refs):
    outs, sem = refs[:HALVES], refs[HALVES]
    depth, width = outs[0].shape
    at = lax.rem(lax.axis_index("ctx"), 2) * depth if shared else 0
    copies = []
    for c in range(HALVES):
        rows, cols = pl.ds(at, depth), pl.ds(c * width, width)
        copies.append(pltpu.make_async_copy(w_ref.at[rows, cols], outs[c], sem.at[c]))
    for copy in copies:
        copy.start()
    for copy in copies:
        copy.wait()


def slice_weight(weight, shared):
    depth, width = weight.shape
    part = jax.ShapeDtypeStruct((depth // 2 if shared else depth, width // HALVES), weight.dtype)
    return call(
        functools.partial(slice_kernel, shared),
        [part] * HALVES,
        "slice_weight",
        1,
        4,
        n_in=1,
        anywhere_in=(0,),
        scratch_shapes=[pltpu.SemaphoreType.DMA((HALVES,))],
    )(weight)


def state_kernel(heads, size, count, k_ref, v_ref, level_ref, own_ref):
    for h in range(heads):
        cols = slice(h * size, (h + 1) * size)
        states = []
        for n in range(count):
            rows = pl.ds(n * STRETCH, STRETCH)
            states.append(contract_rows(k_ref[rows, cols], v_ref[rows, cols]))
        at = 0
        while len(states) > 1:
            for g in range(len(states) // 2):
                level_ref[at, h] = states[2 * g].astype(jnp.bfloat16)
                at += 1
            states = [states[2 * g] + states[2 * g + 1] for g in range(len(states) // 2)]
        own_ref[cols, :] = states[0].astype(jnp.bfloat16)


def block_states(keys, values, heads, size):
    count = keys.shape[0] // STRETCH
    return call(
        functools.partial(state_kernel, heads, size, count),
        [
            jax.ShapeDtypeStruct((count - 1, heads, size, size), jnp.bfloat16),
            jax.ShapeDtypeStruct((heads * size, size), jnp.bfloat16),
        ],
        "block_states",
        2,
        6,
        n_in=2,
    )(keys, values)


def merge_kernel(own_ref, a_ref, b_ref, c_ref, local_ref, pair_ref, all_ref, passed_ref):
    pair = b_ref[...].astype(jnp.float32) + c_ref[...].astype(jnp.float32)
    pair_ref[...] = pair.astype(jnp.bfloat16)
    own = own_ref[...].astype(jnp.float32) + a_ref[...].astype(jnp.float32)
    all_ref[...] = (own + pair).astype(jnp.bfloat16)


def merge_states(own, near, local):
    return call(
        merge_kernel,
        [jax.ShapeDtypeStruct(own.shape, own.dtype)] * 2
        + [jax.ShapeDtypeStruct(local.shape, local.dtype)],
        "merge_states",
        0.2,
        2,
        n_in=5,
        anywhere_in=(4,),
        anywhere_out=(2,),
        input_output_aliases={4: 2},
    )(own, *near, local)


def gate_kernel(*refs):
    pass


def gate(x, *after):
    (out,) = call(
        gate_kernel,
        [jax.ShapeDtypeStruct(x.shape, x.dtype)],
        "gate",
        0.1,
        1,
        n_in=1 + len(after),
        anywhere_in=range(1 + len(after)),
        anywhere_out=(0,),
        input_output_aliases={0: 0},
    )(x, *after)
    return out


def spread_weights(index_row, table):
    plans = table.shape[0]
    high = table.astype(jnp.bfloat16)
    rest = table - high.astype(jnp.float32)
    middle = rest.astype(jnp.bfloat16)
    low = (rest - middle.astype(jnp.float32)).astype(jnp.bfloat16)
    plan = lax.broadcasted_iota(jnp.int32, (plans, index_row.shape[1]), 0)
    onehot = (plan == index_row).astype(jnp.float32).astype(jnp.bfloat16)
    return contract_rows(
        jnp.concatenate([onehot] * 3, axis=0), jnp.concatenate([high, middle, low], axis=0)
    )


def local_kernel(
    heads, size, count, start, blocks, q_ref, k_ref, v_ref, index_ref, table_ref, level_ref, *refs
):
    out_ref = refs[-1]
    tiles = STRETCH // LANES
    tile_bits = bit_count(LANES)
    block_bits = bit_count(STRETCH)
    row = lax.broadcasted_iota(jnp.int32, (LANES, LANES), 0)
    col = lax.broadcasted_iota(jnp.int32, (LANES, LANES), 1)
    across = row ^ col
    level = jnp.zeros_like(row)
    for b in range(tile_bits):
        level = level + (across >= (1 << b)).astype(jnp.int32)
    level = jnp.where(col <= row, level, LANES - 1)
    for n in range(start, start + blocks):
        block = pl.ds(n * STRETCH, STRETCH)
        weights = spread_weights(index_ref[n], table_ref[...])
        for h in range(heads):
            cols = slice(h * size, (h + 1) * size)
            q = q_ref[block, cols]
            k = k_ref[block, cols]
            v = v_ref[block, cols]
            w = weights[:, h * LANES : (h + 1) * LANES]
            scores = lax.dot_general(
                q, k, (((1,), (1,)), ((), ())), preferred_element_type=jnp.float32
            )
            parts = []
            for i in range(tiles):
                rows = slice(i * LANES, (i + 1) * LANES)
                w_tile = w[rows]
                pieces = []
                for j in range(i + 1):
                    s = scores[rows, j * LANES : (j + 1) * LANES]
                    if j == i:
                        factor = jnp.take_along_axis(w_tile, level, axis=1)
                    else:
                        at = tile_bits + (i ^ j).bit_length()
                        factor = w_tile[:, at : at + 1]
                    pieces.append((s * factor).astype(jnp.bfloat16))
                weighted = pieces[0] if i == 0 else jnp.concatenate(pieces, axis=1)
                parts.append(dot(weighted, v[: (i + 1) * LANES]))
            total = jnp.concatenate(parts, axis=0)
            first = 0
            for b in range(bit_count(count)):
                if (n >> b) & 1:
                    reached = dot(q, level_ref[first + (n >> (b + 1)), h])
                    at = block_bits + 1 + b
                    total = total + reached * w[:, at : at + 1]
                first += count >> (b + 1)
            out_ref[block, cols] = total.astype(out_ref.dtype)


def local_attention(queries, keys, values, index_rows, table, levels, start, blocks, earlier=None):
    tokens, width = queries.shape
    count = tokens // STRETCH
    heads, size = levels.shape[1], levels.shape[3]
    extra = [] if earlier is None else [earlier]
    (out,) = call(
        functools.partial(local_kernel, heads, size, count, start, blocks),
        [jax.ShapeDtypeStruct((tokens, width), jnp.bfloat16)],
        "local_attention",
        blocks * 1.2,
        8,
        n_in=6 + len(extra),
        input_output_aliases={6: 0} if extra else {},
    )(queries, keys, values, index_rows, table, levels, *extra)
    return out


def finish_kernel(
    heads, size, first, remotes, offset, part, parts, blocks, q_ref, local_ref, index_ref, table_ref, *refs
):
    state_refs, out_ref = refs[:remotes], refs[remotes]
    start = (lax.axis_index("mp") ^ offset) * parts + part
    position = lax.axis_index("ctx")
    for i in range(blocks):
        block = pl.ds(pl.multiple_of((start + i) * STRETCH, STRETCH), STRETCH)
        weights = spread_weights(index_ref[start + i], table_ref[...])
        for h in range(heads):
            cols = slice(h * size, (h + 1) * size)
            q = q_ref[block, cols]
            w = weights[:, h * LANES : (h + 1) * LANES]
            total = local_ref[block, cols].astype(jnp.float32)
            for b in range(remotes):
                inside = ((position >> b) & 1).astype(jnp.float32)
                reached = dot(q, state_refs[b][cols, :])
                total = total + reached * (w[:, first + b : first + b + 1] * inside)
            scale = lax.rsqrt(jnp.mean(total * total, axis=1, keepdims=True) + EPSILON)
            out_ref[i * STRETCH : (i + 1) * STRETCH, cols] = (total * scale).astype(out_ref.dtype)


def finish_rows(offset, part, blocks, queries, local, index_rows, table, states, first):
    tokens, width = queries.shape
    size = states[0].shape[1]
    heads = width // size
    parts = tokens // STRETCH // lax.axis_size("mp")
    (out,) = call(
        functools.partial(
            finish_kernel, heads, size, first, len(states), offset, part, parts, blocks
        ),
        [jax.ShapeDtypeStruct((blocks * STRETCH, width), jnp.bfloat16)],
        "finish_rows",
        1.5 * blocks,
        4,
        n_in=4 + len(states),
    )(queries, local, index_rows, table, *states)
    return out


def weight_columns(pieces, w_refs, cols):
    start = 0
    for at, width, ref in zip([p[0] for p in pieces], [p[1] for p in pieces], w_refs):
        if start <= cols < start + width:
            yield at, ref[:, pl.ds(cols - start, min(TILE, width))]
        start += width


def project_kernel(groups, before, rows_at, *refs):
    refs = list(refs)
    a_refs = [refs.pop(0) for _ in groups]
    w_refs = [[[refs.pop(0) for _ in row] for _, row in g] for g in groups]
    before_refs = [refs.pop(0) for _ in range(before)]
    yours = refs
    return a_refs, w_refs, before_refs, yours


def products(groups, a_refs, w_refs, cols, rows=slice(None)):
    total = None
    mine = lax.rem(lax.axis_index("ctx"), 2)
    for (g, a_ref), ws in zip(zip(groups, a_refs), w_refs):
        for (place, row), row_refs in zip(g, ws):
            width = row_refs[0].shape[1]
            ref = row_refs[cols // width]
            depth = ref.shape[0]
            if place is None:
                a = a_ref[rows, :]
            else:
                at = pl.multiple_of((mine ^ place) * depth, depth)
                a = a_ref[rows, pl.ds(at, depth)]
            piece = dot(a, ref[:, cols % width : cols % width + TILE])
            total = piece if total is None else total + piece
    return total


def start_kernel(groups, parts, *refs):
    a_refs, w_refs, _, outs = project_kernel(groups, 0, 0, *refs)
    for part in range(parts):
        for cols in range(0, outs[0].shape[1], TILE):
            rows = slice(part * STRETCH, (part + 1) * STRETCH)
            outs[part][:, cols : cols + TILE] = products(groups, a_refs, w_refs, cols, rows)


def add_kernel(groups, *refs):
    a_refs, w_refs, (before,), (out,) = project_kernel(groups, 1, 0, *refs)
    for cols in range(0, out.shape[1], TILE):
        tile = slice(cols, cols + TILE)
        out[:, tile] = before[:, tile] + products(groups, a_refs, w_refs, cols)


def last_kernel(groups, part, aliased, *refs):
    a_refs, w_refs, before, (out, tile_ref, sem) = project_kernel(groups, 1 + aliased, 0, *refs)
    copies = []
    for i, cols in enumerate(range(0, out.shape[1], TILE)):
        tile = slice(cols, cols + TILE)
        total = before[0][:, tile] + products(groups, a_refs, w_refs, cols)
        tile_ref[i] = total.astype(tile_ref.dtype)
        to = out.at[pl.ds(part * STRETCH, STRETCH), pl.ds(cols, TILE)]
        copies.append(pltpu.make_async_copy(tile_ref.at[i], to, sem.at[i]))
        copies[-1].start()
    for copy in copies:
        copy.wait()


def operands(pairs):
    groups = [[(place, [None] * len(row)) for place, row in g] for _, g in pairs]
    arrays = [a for a, _ in pairs] + [w for _, g in pairs for _, row in g for w in row]
    return groups, arrays


def project_start(pairs, columns):
    groups, arrays = operands(pairs)
    parts = pairs[0][0].shape[0] // STRETCH
    return call(
        functools.partial(start_kernel, groups, parts),
        [jax.ShapeDtypeStruct((STRETCH, columns), jnp.float32)] * parts,
        "project_start",
        3,
        6,
        n_in=len(arrays),
    )(*arrays)


def project_add(pairs, before):
    groups, arrays = operands(pairs)
    (out,) = call(
        functools.partial(add_kernel, groups),
        [jax.ShapeDtypeStruct(before.shape, before.dtype)],
        "project_add",
        1,
        6,
        n_in=len(arrays) + 1,
        input_output_aliases={len(arrays): 0},
    )(*arrays, before)
    return out


def project_last(pairs, before, out, part, parts):
    groups, arrays = operands(pairs)
    columns = before.shape[1]
    extra = [] if out is None else [out]
    (out,) = call(
        functools.partial(last_kernel, groups, part, len(extra)),
        [jax.ShapeDtypeStruct((parts * STRETCH, columns), jnp.bfloat16)],
        "project_last",
        1,
        8,
        n_in=len(arrays) + 1 + len(extra),
        anywhere_in=(len(arrays) + 1,),
        anywhere_out=(0,),
        input_output_aliases={len(arrays) + 1: 0} if extra else {},
        scratch_shapes=[
            pltpu.VMEM((columns // TILE, STRETCH, TILE), jnp.bfloat16),
            pltpu.SemaphoreType.DMA((columns // TILE,)),
        ],
    )(*arrays, before, *extra)
    return out


def flip(x, axis, bits):
    n = lax.axis_size(axis)
    return lax.ppermute(x, axis, [(i, i ^ bits) for i in range(n)])


def add_rounded(*arrays):
    total = arrays[0].astype(jnp.float32)
    for a in arrays[1:]:
        total = total + a.astype(jnp.float32)
    return total.astype(jnp.bfloat16)


def body(queries, key_vectors, value_vectors, level_index, level_table, out_weight):
    tokens, width = queries.shape
    plans, heads, level_total = level_table.shape
    size = width // heads
    ctx_size, mp_size = lax.axis_size("ctx"), lax.axis_size("mp")
    ctx_bits = bit_count(ctx_size)
    count = tokens // STRETCH
    columns = out_weight.shape[1]
    first = bit_count(STRETCH) + 1 + bit_count(count)

    table = jnp.pad(level_table, ((0, 0), (0, 0), (0, LANES - level_total))).reshape(
        plans, heads * LANES
    )
    index_rows = level_index.reshape(count, 1, STRETCH)

    shared = ctx_size > 1
    portion = slice_weight(out_weight, shared)
    got = {j: [flip(p, "mp", j) for p in portion] for j in range(2, mp_size, 2)}

    levels, own = block_states(key_vectors, value_vectors, heads, size)
    near = [flip(own, "ctx", b) for b in range(1, min(4, ctx_size))]

    attend = functools.partial(
        local_attention, queries, key_vectors, value_vectors, index_rows, table, levels
    )
    cut = count // 2
    local = attend(0, cut)
    remote = near[:1]
    after = local
    if ctx_bits > 1:
        pair, running, local = merge_states(own, near, local)
        remote.append(pair)
        after = running
    far = None
    for b in range(2, ctx_bits):
        if b > 2:
            running = add_rounded(running, far)
        far = flip(running, "ctx", 1 << b)
        remote.append(far)

    there = {}
    for j in got:
        got[j][0] = gate(got[j][0], after)
        there[j] = [flip(got[j][0], "ctx", 1)]
    mate = flip(gate(out_weight, after) if False else out_weight, "mp", 1)

    local = attend(cut, count - cut, local)

    parts = tokens // mp_size // STRETCH

    def finished(j, part, blocks):
        return finish_rows(j, part, blocks, queries, local, index_rows, table, remote, first)

    received = {}
    last = None
    for part in range(parts):
        for j in range(2, mp_size):
            last = finished(j, part, 1)
            received[j, part] = flip(last, "mp", j)
        if part == 0:
            for j in got:
                for c in range(1, HALVES):
                    got[j][c] = gate(got[j][c], last)
                    there[j].append(flip(got[j][c], "ctx", 1))
    gathered = {}
    for j in got:
        gathered[j] = [(0, got[j]), (1, there[j])]
        gathered[j + 1] = [(at, [flip(w, "mp", 1) for w in row]) for at, row in gathered[j]]

    close = [(finished(0, 0, parts), [(None, [out_weight])])]
    if mp_size > 1:
        close.append((flip(finished(1, 0, parts), "mp", 1), [(None, [mate])]))
    totals = project_start(close, columns)

    far_groups = list(range(2, mp_size))
    out = None
    for part in range(parts):
        total = totals[part]
        pairs = [(received[j, part], gathered[j]) for j in far_groups]
        if part + 1 == parts and len(pairs) > 1:
            total = project_add(pairs[:-1], total)
            pairs = pairs[-1:]
        out = project_last(pairs, total, out, part, parts)
    return out


def solution(mesh):
    placed = (
        P("ctx", "mp"),
        P("ctx", "mp"),
        P("ctx", "mp"),
        P("ctx"),
        P(None, "mp", None),
        P("mp", None),
    )
    return jax.shard_map(
        body, mesh=mesh, in_specs=placed, out_specs=P(("ctx", "mp"), None), check_vma=False
    )
```

time: 188 us -> 73.8 us (0.39)
  waiting for transfers between devices: 78.8 us -> 25.8 us
  matrix products: 45.5 us -> 0 us
  local copies, waits for them, and re-layouts: 44.4 us -> 3.22 us
  Pallas kernels: 0 us -> 24.7 us
  starting transfers between devices: 0.04 us -> 19.6 us
  between operations: 13.6 us -> 0.39 us
  other arithmetic: 4.98 us -> 0 us
    reduce_scatter x1 -> x0, waiting for transfers between devices: 70.6 us -> none  [body(): lax.psum_scatter(jnp.dot(mixed_heads, out_weight, preferred_element_type=...]
    dot_general x7 -> x0, matrix products: 45.5 us -> none  [the longest x1 15.6 us: body(): jnp.einsum('nhts,nhse->nhte', weighted, value_blocks, preferred_element_t...]
    ppermute x0 -> x18, waiting for transfers between devices: none -> 25.8 us  [flip(): return lax.ppermute(x, axis, [(i, i ^ bits) for i in range(n)])]
    pallas_call x0 -> x17, Pallas kernels: none -> 24.7 us  [the longest x6 8.88 us: finish_rows(): call(functools.partial(finish_kernel, heads, size, first, len(states), of...]
    ppermute x0 -> x18, starting transfers between devices: none -> 19.6 us  [flip(): return lax.ppermute(x, axis, [(i, i ^ bits) for i in range(n)])]
    reshape x4 -> x0, local copies, waits for them, and re-layouts: 12.1 us -> none  [the longest x1 4.1 us: body(): key_vectors.reshape(stretch_count, STRETCH, heads_here, head_size)]
    slice x8 -> x0, local copies, waits for them, and re-layouts: 8.88 us -> none  [the longest x2 6.2 us: body(): weight_blocks[..., :stretch_bits + 1]]
    unnamed x19 -> x17, local copies, waits for them, and re-layouts: 11.6 us -> 3.22 us
  transfers between devices with their start and end apart: 2 -> 18, of which waited for: 2 -> 7; matrix products, arithmetic and copies ran while one was open for 19% -> 0% of each run, Pallas kernels for 0% -> 30%
where the time goes in v2:
time: 73.8 us; the launch traced here: 73.7 us
  waiting for transfers between devices  25.8 us (35%)
  Pallas kernels  24.7 us (33%)
  starting transfers between devices  19.6 us (27%)
  local copies, waits for them, and re-layouts  3.22 us (4%)
    ppermute x18, waiting for transfers between devices, flip(): return lax.ppermute(x, axis, [(i, i ^ bits) for i in range(n)])  25.8 us
    ppermute x18, starting transfers between devices, flip(): return lax.ppermute(x, axis, [(i, i ^ bits) for i in range(n)])  19.6 us
    pallas_call x6, Pallas kernels, finish_rows(): call(functools.partial(finish_kernel, heads, size, first, len(states), of...  8.88 us
    pallas_call x2, Pallas kernels, local_attention(): call(functools.partial(local_kernel, heads, size, count, start, blocks),...  8.13 us
    pallas_call x2, Pallas kernels, project_last(): call(functools.partial(last_kernel, groups, part, len(extra)), [jax.Shape...  3.5 us
    unnamed x17, local copies, waits for them, and re-layouts  3.22 us
    pallas_call x1, Pallas kernels, project_start(): call(functools.partial(start_kernel, groups, parts), [jax.ShapeDtypeStruc...  2.33 us
  transfers between devices with their start and end apart: 18, of which 7 were waited for; matrix products, arithmetic and copies ran while one was open for 0% of the time, Pallas kernels for 30%

profile of v2, /device:TPU:0, one launch (start us, length us, event | category | flops | bytes accessed | tf_op | source)
XLA Modules:
  0.0 73.7 jit_solution(4010747444865680328)
XLA Ops:
  0.0 0.0 copy-start
  0.0 1.6 %copy-done = bf16[2048,512]{1,0:T(8,128)(2,1)S(1)} copy-done((bf16[2048,512]{1,0:T(8,128)(2,1)S(1)}, bf16[2048,512]{1,0:T(8,128)(2,1)}, u32[]{:S(2)}) %copy-start) | copy-done | bytes 2097176
  1.6 0.0 copy-start.2
  1.6 1.6 %copy-done.2 = bf16[2048,512]{1,0:T(8,128)(2,1)S(1)} copy-done((bf16[2048,512]{1,0:T(8,128)(2,1)S(1)}, bf16[2048,512]{1,0:T(8,128)(2,1)}, u32[]{:S(2)}) %copy-start.2) | copy-done | bytes 2097176
  3.2 0.8 %block_states.1 = (bf16[7,4,128,128]{3,2,1,0:T(8,128)(2,1)S(1)}, bf16[512,128]{1,0:T(8,128)(2,1)S(1)}) custom-call(bf16[2048,512]{1,0:T(8,128)(2,1)S(1)} %copy-done, bf16[2048,512]{1,0:T(8,128)(2,1)S(1)} %copy-done.2), custom_call_target="tpu_custom_call" | custom-call | flops 2000000000 | bytes 6000000 | tf_op jit(solution)/shard_map/block_states/pallas_call | solution.py:97
  4.0 0.0 copy-start.7
  4.0 0.0 copy-start.1
  4.0 0.0 copy-start.6
  4.0 4.0 %collective-permute-start.2 = (bf16[512,128]{1,0:T(8,128)(2,1)S(1)}, bf16[512,128]{1,0:T(8,128)(2,1)S(1)}, u32[]{:S(2)}, u32[]{:S(2)}) collective-permute-start(bf16[512,128]{1,0:T(8,128)(2,1)S(1)} %get-tuple-element.15.own_ref), channel_id=1, source_target_pairs={{0,12},{4,8},{8,4},{12,0},{16,28},{20,24},{24,20},{28,16},{1,13},{... | collective-permute-start | bytes 393224 | tf_op jit(solution)/shard_map/ppermute | solution.py:394
  8.1 0.4 collective-permute-start.1
  8.5 0.2 collective-permute-start
  8.7 0.0 copy-done.5
  8.7 0.0 collective-permute-start.15
  8.7 0.1 slice_weight.1
  8.8 1.9 %collective-permute-start.5 = (bf16[256,1024]{1,0:T(8,128)(2,1)S(1)}, bf16[256,1024]{1,0:T(8,128)(2,1)S(1)}, u32[]{:S(2)}, u32[]{:S(2)}) collective-permute-start(bf16[256,1024]{1,0:T(8,128)(2,1)S(1)} %get-tuple-element.19), channel_id=1, source_target_pairs={{0,2},{1,3},{2,0},{3,1},{4,6},{5,7},{6,4},{7,5},{8,10},{9,11},{10,... | collective-permute-start | bytes 1572872 | tf_op jit(solution)/shard_map/ppermute | solution.py:394
  10.7 0.0 copy-done.7
  10.7 0.0 copy-done.3
  10.7 0.0 copy-done.4
  10.7 0.0 copy-done.1
  10.7 0.0 copy-done.6
  10.7 3.8 %local_attention.2.local_ref = bf16[2048,512]{1,0:T(8,128)(2,1)S(1)} custom-call(bf16[2048,512]{1,0:T(8,128)(2,1)S(1)} %copy-done.4, bf16[2048,512]{1,0:T(8,128)(2,1)S(1)} %copy-done.1, bf16[2048,512]{1,0:T(8,128)(2,1)S(1)} %copy-done.3, s32[8,1,256]{2,1,0:T(1,128)S(1)} %bitcast.13, f32[16,512]{1,0:T(8,128)S(1)} %bitcast.5, ...), custom_call_target="tpu_custom_call" | custom-call | flops 4800000000 | bytes 14400000 | tf_op jit(solution)/shard_map/local_attention/pallas_call | solution.py:221
  14.6 0.0 collective-permute-done.2.c_ref
  14.6 0.3 collective-permute-start.7
  14.9 0.0 collective-permute-done.1.b_ref
  14.9 0.0 collective-permute-done.a_ref.refs_0_
  14.9 0.1 merge_states.1
  14.9 3.0 %collective-permute-start.3 = (bf16[512,128]{1,0:T(8,128)(2,1)S(1)}, bf16[512,128]{1,0:T(8,128)(2,1)S(1)}, u32[]{:S(2)}, u32[]{:S(2)}) collective-permute-start(bf16[512,128]{1,0:T(8,128)(2,1)S(1)} %get-tuple-element.18.refs_1_), channel_id=1, source_target_pairs={{0,16},{4,20},{8,24},{12,28},{16,0},{20,4},{24,8},{28,12},{1,17},{... | collective-permute-start | bytes 393224 | tf_op jit(solution)/shard_map/ppermute | solution.py:394
  17.9 4.3 %local_attention.3.local_ref = bf16[2048,512]{1,0:T(8,128)(2,1)S(1)} custom-call(bf16[2048,512]{1,0:T(8,128)(2,1)S(1)} %copy-done.4, bf16[2048,512]{1,0:T(8,128)(2,1)S(1)} %copy-done.1, bf16[2048,512]{1,0:T(8,128)(2,1)S(1)} %copy-done.3, s32[8,1,256]{2,1,0:T(1,128)S(1)} %bitcast.14, f32[16,512]{1,0:T(8,128)S(1)} %bitcast.6, ...), custom_call_target="tpu_custom_call", output_to_operand_aliasing={{}: (6, {})} | custom-call | flops 4800000000 | bytes 14400000 | tf_op jit(solution)/shard_map/local_attention/pallas_call | solution.py:221
  22.3 2.1 %collective-permute-done.3.refs_2_ = bf16[512,128]{1,0:T(8,128)(2,1)S(1)} collective-permute-done((bf16[512,128]{1,0:T(8,128)(2,1)S(1)}, bf16[512,128]{1,0:T(8,128)(2,1)S(1)}, u32[]{:S(2)}, u32[]{:S(2)}) %collective-permute-start.3) | collective-permute-done | bytes 131104 | tf_op jit(solution)/shard_map/ppermute | solution.py:394
  24.3 1.0 %finish_rows.8 = bf16[256,512]{1,0:T(8,128)(2,1)S(1)} custom-call(bf16[2048,512]{1,0:T(8,128)(2,1)S(1)} %copy-done.4, bf16[2048,512]{1,0:T(8,128)(2,1)S(1)} %local_attention.3.local_ref, s32[8,1,256]{2,1,0:T(1,128)S(1)} %bitcast.15, f32[16,512]{1,0:T(8,128)S(1)} %bitcast.7, bf16[512,128]{1,0:T(8,128)(2,1)S(1)} %collective-permute-done.a_ref.refs_0_, ...), custom_call_target="tpu_custom_call" | custom-call | flops 1500000000 | bytes 4500000 | tf_op jit(solution)/shard_map/finish_rows/pallas_call | solution.py:260
  25.4 1.6 %collective-permute-start.13 = (bf16[256,512]{1,0:T(8,128)(2,1)S(1)}, bf16[256,512]{1,0:T(8,128)(2,1)S(1)}, u32[]{:S(2)}, u32[]{:S(2)}) collective-permute-start(bf16[256,512]{1,0:T(8,128)(2,1)S(1)} %finish_rows.8), channel_id=1, source_target_pairs={{0,2},{1,3},{2,0},{3,1},{4,6},{5,7},{6,4},{7,5},{8,10},{9,11},{10,... | collective-permute-start | bytes 786440 | tf_op jit(solution)/shard_map/ppermute | solution.py:394
  27.0 1.0 %finish_rows.11 = bf16[256,512]{1,0:T(8,128)(2,1)S(1)} custom-call(bf16[2048,512]{1,0:T(8,128)(2,1)S(1)} %copy-done.4, bf16[2048,512]{1,0:T(8,128)(2,1)S(1)} %local_attention.3.local_ref, s32[8,1,256]{2,1,0:T(1,128)S(1)} %bitcast.16, f32[16,512]{1,0:T(8,128)S(1)} %bitcast.8, bf16[512,128]{1,0:T(8,128)(2,1)S(1)} %collective-permute-done.a_ref.refs_0_, ...), custom_call_target="tpu_custom_call" | custom-call | flops 1500000000 | bytes 4500000 | tf_op jit(solution)/shard_map/finish_rows/pallas_call | solution.py:260
  28.0 0.6 collective-permute-start.16
  28.6 1.0 %finish_rows.7.refs_1_ = bf16[256,512]{1,0:T(8,128)(2,1)S(1)} custom-call(bf16[2048,512]{1,0:T(8,128)(2,1)S(1)} %copy-done.4, bf16[2048,512]{1,0:T(8,128)(2,1)S(1)} %local_attention.3.local_ref, s32[8,1,256]{2,1,0:T(1,128)S(1)} %bitcast.17, f32[16,512]{1,0:T(8,128)S(1)} %bitcast.9, bf16[512,128]{1,0:T(8,128)(2,1)S(1)} %collective-permute-done.a_ref.refs_0_, ...), custom_call_target="tpu_custom_call" | custom-call | flops 1500000000 | bytes 4500000 | tf_op jit(solution)/shard_map/finish_rows/pallas_call | solution.py:260
  29.6 2.4 %finish_rows.10 = bf16[512,512]{1,0:T(8,128)(2,1)S(1)} custom-call(bf16[2048,512]{1,0:T(8,128)(2,1)S(1)} %copy-done.4, bf16[2048,512]{1,0:T(8,128)(2,1)S(1)} %local_attention.3.local_ref, s32[8,1,256]{2,1,0:T(1,128)S(1)} %bitcast.18, f32[16,512]{1,0:T(8,128)S(1)} %bitcast.10, bf16[512,128]{1,0:T(8,128)(2,1)S(1)} %collective-permute-done.a_ref.refs_0_, ...), custom_call_target="tpu_custom_call" | custom-call | flops 3000000000 | bytes 9000000 | tf_op jit(solution)/shard_map/finish_rows/pallas_call | solution.py:260
  32.1 2.7 %collective-permute-done.7.refs_0_ = bf16[256,1024]{1,0:T(8,128)(2,1)S(1)} collective-permute-done((bf16[256,1024]{1,0:T(8,128)(2,1)S(1)}, bf16[256,1024]{1,0:T(8,128)(2,1)S(1)}, u32[]{:S(2)}, u32[]{:S(2)}) %collective-permute-start.7) | collective-permute-done | bytes 524320 | tf_op jit(solution)/shard_map/ppermute | solution.py:394
  34.8 0.0 collective-permute-start.14
  34.8 0.0 collective-permute-done.5.refs_0_
  34.8 1.9 %collective-permute-start.11 = (bf16[256,1024]{1,0:T(8,128)(2,1)S(1)}, bf16[256,1024]{1,0:T(8,128)(2,1)S(1)}, u32[]{:S(2)}, u32[]{:S(2)}) collective-permute-start(bf16[256,1024]{1,0:T(8,128)(2,1)S(1)} %gate.3.refs_2_.refs_3_), channel_id=1, source_target_pairs={{0,4},{4,0},{8,12},{12,8},{16,20},{20,16},{24,28},{28,24},{1,5},{5... | collective-permute-start | bytes 1572872 | tf_op jit(solution)/shard_map/ppermute | solution.py:394
  36.7 3.7 %collective-permute-done.13.refs_0_ = bf16[256,512]{1,0:T(8,128)(2,1)S(1)} collective-permute-done((bf16[256,512]{1,0:T(8,128)(2,1)S(1)}, bf16[256,512]{1,0:T(8,128)(2,1)S(1)}, u32[]{:S(2)}, u32[]{:S(2)}) %collective-permute-start.13) | collective-permute-done | bytes 262176 | tf_op jit(solution)/shard_map/ppermute | solution.py:394
  40.4 1.8 %collective-permute-start.9 = (bf16[256,1024]{1,0:T(8,128)(2,1)S(1)}, bf16[256,1024]{1,0:T(8,128)(2,1)S(1)}, u32[]{:S(2)}, u32[]{:S(2)}) collective-permute-start(bf16[256,1024]{1,0:T(8,128)(2,1)S(1)} %gate.2.refs_1_.refs_2_), channel_id=1, source_target_pairs={{0,4},{4,0},{8,12},{12,8},{16,20},{20,16},{24,28},{28,24},{1,5},{5... | collective-permute-start | bytes 1572872 | tf_op jit(solution)/shard_map/ppermute | solution.py:394
  42.3 3.5 %collective-permute-done.16.refs_0_ = bf16[256,512]{1,0:T(8,128)(2,1)S(1)} collective-permute-done((bf16[256,512]{1,0:T(8,128)(2,1)S(1)}, bf16[256,512]{1,0:T(8,128)(2,1)S(1)}, u32[]{:S(2)}, u32[]{:S(2)}) %collective-permute-start.16) | collective-permute-done | bytes 262176 | tf_op jit(solution)/shard_map/ppermute | solution.py:394
  45.7 1.1 %collective-permute-start.17 = (bf16[256,512]{1,0:T(8,128)(2,1)S(1)}, bf16[256,512]{1,0:T(8,128)(2,1)S(1)}, u32[]{:S(2)}, u32[]{:S(2)}) collective-permute-start(bf16[256,512]{1,0:T(8,128)(2,1)S(1)} %finish_rows.7.refs_1_), channel_id=1, source_target_pairs={{0,3},{1,2},{2,1},{3,0},{4,7},{5,6},{6,5},{7,4},{8,11},{9,10},{10,... | collective-permute-start | bytes 786440 | tf_op jit(solution)/shard_map/ppermute | solution.py:394
  46.8 7.2 %collective-permute-done.17.refs_1_ = bf16[256,512]{1,0:T(8,128)(2,1)S(1)} collective-permute-done((bf16[256,512]{1,0:T(8,128)(2,1)S(1)}, bf16[256,512]{1,0:T(8,128)(2,1)S(1)}, u32[]{:S(2)}, u32[]{:S(2)}) %collective-permute-start.17) | collective-permute-done | bytes 262176 | tf_op jit(solution)/shard_map/ppermute | solution.py:394
  54.1 0.4 collective-permute-start.8
  54.5 0.0 collective-permute-done.14.refs_1_
  54.5 0.1 collective-permute-start.6
  54.6 0.0 collective-permute-done.11.refs_4_.refs_5_
  54.6 0.4 collective-permute-start.12
  55.0 5.5 %collective-permute-done.9.refs_3_.refs_4_ = bf16[256,1024]{1,0:T(8,128)(2,1)S(1)} collective-permute-done((bf16[256,1024]{1,0:T(8,128)(2,1)S(1)}, bf16[256,1024]{1,0:T(8,128)(2,1)S(1)}, u32[]{:S(2)}, u32[]{:S(2)}) %collective-permute-start.9) | collective-permute-done | bytes 524320 | tf_op jit(solution)/shard_map/ppermute | solution.py:394
  60.5 0.0 collective-permute-start.10
  60.5 2.3 %finish_rows.9.refs_0_ = bf16[512,512]{1,0:T(8,128)(2,1)S(1)} custom-call(bf16[2048,512]{1,0:T(8,128)(2,1)S(1)} %copy-done.4, bf16[2048,512]{1,0:T(8,128)(2,1)S(1)} %local_attention.3.local_ref, s32[8,1,256]{2,1,0:T(1,128)S(1)} %bitcast.19, f32[16,512]{1,0:T(8,128)S(1)} %bitcast.11, bf16[512,128]{1,0:T(8,128)(2,1)S(1)} %collective-permute-done.a_ref.refs_0_, ...), custom_call_target="tpu_custom_call" | custom-call | flops 3000000000 | bytes 9000000 | tf_op jit(solution)/shard_map/finish_rows/pallas_call | solution.py:260
  62.8 1.0 %finish_rows.6 = bf16[256,512]{1,0:T(8,128)(2,1)S(1)} custom-call(bf16[2048,512]{1,0:T(8,128)(2,1)S(1)} %copy-done.4, bf16[2048,512]{1,0:T(8,128)(2,1)S(1)} %local_attention.3.local_ref, s32[8,1,256]{2,1,0:T(1,128)S(1)} %bitcast.20, f32[16,512]{1,0:T(8,128)S(1)} %bitcast.12, bf16[512,128]{1,0:T(8,128)(2,1)S(1)} %collective-permute-done.a_ref.refs_0_, ...), custom_call_target="tpu_custom_call" | custom-call | flops 1500000000 | bytes 4500000 | tf_op jit(solution)/shard_map/finish_rows/pallas_call | solution.py:260
  63.8 0.0 collective-permute-done.15.refs_3_
  63.8 1.9 %collective-permute-start.4 = (bf16[256,512]{1,0:T(8,128)(2,1)S(1)}, bf16[256,512]{1,0:T(8,128)(2,1)S(1)}, u32[]{:S(2)}, u32[]{:S(2)}) collective-permute-start(bf16[256,512]{1,0:T(8,128)(2,1)S(1)} %finish_rows.6), channel_id=1, source_target_pairs={{0,3},{1,2},{2,1},{3,0},{4,7},{5,6},{6,5},{7,4},{8,11},{9,10},{10,... | collective-permute-start | bytes 786440 | tf_op jit(solution)/shard_map/ppermute | solution.py:394
  65.7 2.3 %project_start.1 = (f32[256,2048]{1,0:T(8,128)S(1)}, f32[256,2048]{1,0:T(8,128)S(1)}) custom-call(bf16[512,512]{1,0:T(8,128)(2,1)S(1)} %finish_rows.9.refs_0_, bf16[512,512]{1,0:T(8,128)(2,1)S(1)} %collective-permute-done.14.refs_1_, bf16[512,2048]{1,0:T(8,128)(2,1)S(1)} %copy-done.5, bf16[512,2048]{1,0:T(8,128)(2,1)S(1)} %collective-permute-done.15.refs_3_), custom_call_target="tpu_custom_call" | custom-call | flops 3000000000 | bytes 9000000 | tf_op jit(solution)/shard_map/project_start/pallas_call | solution.py:346
  68.1 0.9 %project_add.1.refs_5_ = f32[256,2048]{1,0:T(8,128)S(1)} custom-call(bf16[256,512]{1,0:T(8,128)(2,1)S(1)} %collective-permute-done.13.refs_0_, bf16[256,1024]{1,0:T(8,128)(2,1)S(1)} %gate.2.refs_1_.refs_2_, bf16[256,1024]{1,0:T(8,128)(2,1)S(1)} %gate.3.refs_2_.refs_3_, ...), custom_call_target="tpu_custom_call", output_to_operand_aliasing={{}: (5, {})} | custom-call | flops 1000000000 | bytes 3000000 | tf_op jit(solution)/shard_map/project_add/pallas_call | solution.py:358
  69.0 0.0 collective-permute-done.8.refs_7_.refs_2_
  69.0 0.0 collective-permute-done.6.refs_6_.refs_1_
  69.0 0.0 collective-permute-done.12.refs_9_.refs_4_
  69.0 0.0 collective-permute-done.10.refs_8_.refs_3_
  69.0 2.0 %project_last.2.refs_6_ = bf16[512,2048]{1,0:T(8,128)(2,1)} custom-call(bf16[256,512]{1,0:T(8,128)(2,1)S(1)} %collective-permute-done.16.refs_0_, bf16[256,512]{1,0:T(8,128)(2,1)S(1)} %collective-permute-done.17.refs_1_, bf16[256,1024]{1,0:T(8,128)(2,1)S(1)} %gate.2.refs_1_.refs_2_, bf16[256,1024]{1,0:T(8,128)(2,1)S(1)} %gate.3.refs_2_.refs_3_, ...), custom_call_target="tpu_custom_call" | custom-call | flops 1000000000 | bytes 3000000 | tf_op jit(solution)/shard_map/project_last/pallas_call | solution.py:374
  71.0 1.0 %collective-permute-done.4.refs_0_ = bf16[256,512]{1,0:T(8,128)(2,1)S(1)} collective-permute-done((bf16[256,512]{1,0:T(8,128)(2,1)S(1)}, bf16[256,512]{1,0:T(8,128)(2,1)S(1)}, u32[]{:S(2)}, u32[]{:S(2)}) %collective-permute-start.4) | collective-permute-done | bytes 262176 | tf_op jit(solution)/shard_map/ppermute | solution.py:394
  72.0 1.5 %project_last.3 = bf16[512,2048]{1,0:T(8,128)(2,1)} custom-call(bf16[256,512]{1,0:T(8,128)(2,1)S(1)} %collective-permute-done.4.refs_0_, bf16[256,1024]{1,0:T(8,128)(2,1)S(1)} %collective-permute-done.6.refs_6_.refs_1_, bf16[256,1024]{1,0:T(8,128)(2,1)S(1)} %collective-permute-done.8.refs_7_.refs_2_, ...), custom_call_target="tpu_custom_call", output_to_operand_aliasing={{}: (6, {})} | custom-call | flops 1000000000 | bytes 3000000 | tf_op jit(solution)/shard_map/project_last/pallas_call | solution.py:374
  (7 shorter events, 0.0 us)
Async XLA Ops:
  0.0 1.6 %copy-start = (bf16[2048,512]{1,0:T(8,128)(2,1)S(1)}, bf16[2048,512]{1,0:T(8,128)(2,1)}, u32[]{:S(2)}) copy-start(bf16[2048,512]{1,0:T(8,128)(2,1)} %k_ref.5) | copy-start | bytes 6291460
  1.6 1.6 %copy-start.2 = (bf16[2048,512]{1,0:T(8,128)(2,1)S(1)}, bf16[2048,512]{1,0:T(8,128)(2,1)}, u32[]{:S(2)}) copy-start(bf16[2048,512]{1,0:T(8,128)(2,1)} %v_ref.5) | copy-start | bytes 6291460
  3.2 5.5 %copy-start.5 = (bf16[512,2048]{1,0:T(8,128)(2,1)S(1)}, bf16[512,2048]{1,0:T(8,128)(2,1)}, u32[]{:S(2)}) copy-start(bf16[512,2048]{1,0:T(8,128)(2,1)} %refs_2_.1) | copy-start | bytes 6291460
  3.2 7.5 %copy-start.3 = (bf16[2048,512]{1,0:T(8,128)(2,1)S(1)}, bf16[2048,512]{1,0:T(8,128)(2,1)}, u32[]{:S(2)}) copy-start(bf16[2048,512]{1,0:T(8,128)(2,1)} %v_ref.5) | copy-start | bytes 6291460
  3.2 7.5 %copy-start.4 = (bf16[2048,512]{1,0:T(8,128)(2,1)S(1)}, bf16[2048,512]{1,0:T(8,128)(2,1)}, u32[]{:S(2)}) copy-start(bf16[2048,512]{1,0:T(8,128)(2,1)} %q_ref.15) | copy-start | bytes 6291460
  4.0 6.7 %copy-start.7 = (f32[16,4,20]{2,1,0:T(4,128)S(1)}, f32[16,4,20]{2,1,0:T(4,128)}, u32[]{:S(2)}) copy-start(f32[16,4,20]{2,1,0:T(4,128)} %param.10) | copy-start | bytes 15364
  4.0 6.7 %copy-start.1 = (bf16[2048,512]{1,0:T(8,128)(2,1)S(1)}, bf16[2048,512]{1,0:T(8,128)(2,1)}, u32[]{:S(2)}) copy-start(bf16[2048,512]{1,0:T(8,128)(2,1)} %k_ref.5) | copy-start | bytes 6291460
  4.0 6.7 %copy-start.6 = (s32[2048]{0:T(1024)S(1)}, s32[2048]{0:T(1024)}, u32[]{:S(2)}) copy-start(s32[2048]{0:T(1024)} %param.9) | copy-start | bytes 24580
  4.0 10.5 %collective-permute-start.2 = (bf16[512,128]{1,0:T(8,128)(2,1)S(1)}, bf16[512,128]{1,0:T(8,128)(2,1)S(1)}, u32[]{:S(2)}, u32[]{:S(2)}) collective-permute-start(bf16[512,128]{1,0:T(8,128)(2,1)S(1)} %get-tuple-element.15.own_ref), channel_id=1, source_target_pairs={{0,12},{4,8},{8,4},{12,0},{16,28},{20,24},{24,20},{28,16},{1,13},{... | collective-permute-start | bytes 393224 | tf_op jit(solution)/shard_map/ppermute | solution.py:394
  8.1 6.8 %collective-permute-start.1 = (bf16[512,128]{1,0:T(8,128)(2,1)S(1)}, bf16[512,128]{1,0:T(8,128)(2,1)S(1)}, u32[]{:S(2)}, u32[]{:S(2)}) collective-permute-start(bf16[512,128]{1,0:T(8,128)(2,1)S(1)} %get-tuple-element.15.own_ref), channel_id=1, source_target_pairs={{0,8},{4,12},{8,0},{12,4},{16,24},{20,28},{24,16},{28,20},{1,9},{5... | collective-permute-start | bytes 393224 | tf_op jit(solution)/shard_map/ppermute | solution.py:394
  8.5 6.3 %collective-permute-start = (bf16[512,128]{1,0:T(8,128)(2,1)S(1)}, bf16[512,128]{1,0:T(8,128)(2,1)S(1)}, u32[]{:S(2)}, u32[]{:S(2)}) collective-permute-start(bf16[512,128]{1,0:T(8,128)(2,1)S(1)} %get-tuple-element.15.own_ref), channel_id=1, source_target_pairs={{0,4},{4,0},{8,12},{12,8},{16,20},{20,16},{24,28},{28,24},{1,5},{5... | collective-permute-start | bytes 393224 | tf_op jit(solution)/shard_map/ppermute | solution.py:394
  8.7 55.1 %collective-permute-start.15 = (bf16[512,2048]{1,0:T(8,128)(2,1)S(1)}, bf16[512,2048]{1,0:T(8,128)(2,1)S(1)}, u32[]{:S(2)}, u32[]{:S(2)}) collective-permute-start(bf16[512,2048]{1,0:T(8,128)(2,1)S(1)} %copy-done.5), channel_id=1, source_target_pairs={{0,1},{1,0},{2,3},{3,2},{4,5},{5,4},{6,7},{7,6},{8,9},{9,8},{10,11... | collective-permute-start | bytes 6291464 | tf_op jit(solution)/shard_map/ppermute | solution.py:394
  8.8 26.0 %collective-permute-start.5 = (bf16[256,1024]{1,0:T(8,128)(2,1)S(1)}, bf16[256,1024]{1,0:T(8,128)(2,1)S(1)}, u32[]{:S(2)}, u32[]{:S(2)}) collective-permute-start(bf16[256,1024]{1,0:T(8,128)(2,1)S(1)} %get-tuple-element.19), channel_id=1, source_target_pairs={{0,2},{1,3},{2,0},{3,1},{4,6},{5,7},{6,4},{7,5},{8,10},{9,11},{10,... | collective-permute-start | bytes 1572872 | tf_op jit(solution)/shard_map/ppermute | solution.py:394
  14.6 20.3 %collective-permute-start.7 = (bf16[256,1024]{1,0:T(8,128)(2,1)S(1)}, bf16[256,1024]{1,0:T(8,128)(2,1)S(1)}, u32[]{:S(2)}, u32[]{:S(2)}) collective-permute-start(bf16[256,1024]{1,0:T(8,128)(2,1)S(1)} %get-tuple-element.20), channel_id=1, source_target_pairs={{0,2},{1,3},{2,0},{3,1},{4,6},{5,7},{6,4},{7,5},{8,10},{9,11},{10,... | collective-permute-start | bytes 1572872 | tf_op jit(solution)/shard_map/ppermute | solution.py:394
  14.9 9.4 %collective-permute-start.3 = (bf16[512,128]{1,0:T(8,128)(2,1)S(1)}, bf16[512,128]{1,0:T(8,128)(2,1)S(1)}, u32[]{:S(2)}, u32[]{:S(2)}) collective-permute-start(bf16[512,128]{1,0:T(8,128)(2,1)S(1)} %get-tuple-element.18.refs_1_), channel_id=1, source_target_pairs={{0,16},{4,20},{8,24},{12,28},{16,0},{20,4},{24,8},{28,12},{1,17},{... | collective-permute-start | bytes 393224 | tf_op jit(solution)/shard_map/ppermute | solution.py:394
  25.4 15.1 %collective-permute-start.13 = (bf16[256,512]{1,0:T(8,128)(2,1)S(1)}, bf16[256,512]{1,0:T(8,128)(2,1)S(1)}, u32[]{:S(2)}, u32[]{:S(2)}) collective-permute-start(bf16[256,512]{1,0:T(8,128)(2,1)S(1)} %finish_rows.8), channel_id=1, source_target_pairs={{0,2},{1,3},{2,0},{3,1},{4,6},{5,7},{6,4},{7,5},{8,10},{9,11},{10,... | collective-permute-start | bytes 786440 | tf_op jit(solution)/shard_map/ppermute | solution.py:394
  28.0 17.7 %collective-permute-start.16 = (bf16[256,512]{1,0:T(8,128)(2,1)S(1)}, bf16[256,512]{1,0:T(8,128)(2,1)S(1)}, u32[]{:S(2)}, u32[]{:S(2)}) collective-permute-start(bf16[256,512]{1,0:T(8,128)(2,1)S(1)} %finish_rows.11), channel_id=1, source_target_pairs={{0,2},{1,3},{2,0},{3,1},{4,6},{5,7},{6,4},{7,5},{8,10},{9,11},{10,... | collective-permute-start | bytes 786440 | tf_op jit(solution)/shard_map/ppermute | solution.py:394
  34.8 19.7 %collective-permute-start.14 = (bf16[512,512]{1,0:T(8,128)(2,1)S(1)}, bf16[512,512]{1,0:T(8,128)(2,1)S(1)}, u32[]{:S(2)}, u32[]{:S(2)}) collective-permute-start(bf16[512,512]{1,0:T(8,128)(2,1)S(1)} %finish_rows.10), channel_id=1, source_target_pairs={{0,1},{1,0},{2,3},{3,2},{4,5},{5,4},{6,7},{7,6},{8,9},{9,8},{10,11... | collective-permute-start | bytes 1572872 | tf_op jit(solution)/shard_map/ppermute | solution.py:394
  34.8 19.7 %collective-permute-start.11 = (bf16[256,1024]{1,0:T(8,128)(2,1)S(1)}, bf16[256,1024]{1,0:T(8,128)(2,1)S(1)}, u32[]{:S(2)}, u32[]{:S(2)}) collective-permute-start(bf16[256,1024]{1,0:T(8,128)(2,1)S(1)} %gate.3.refs_2_.refs_3_), channel_id=1, source_target_pairs={{0,4},{4,0},{8,12},{12,8},{16,20},{20,16},{24,28},{28,24},{1,5},{5... | collective-permute-start | bytes 1572872 | tf_op jit(solution)/shard_map/ppermute | solution.py:394
  40.4 20.1 %collective-permute-start.9 = (bf16[256,1024]{1,0:T(8,128)(2,1)S(1)}, bf16[256,1024]{1,0:T(8,128)(2,1)S(1)}, u32[]{:S(2)}, u32[]{:S(2)}) collective-permute-start(bf16[256,1024]{1,0:T(8,128)(2,1)S(1)} %gate.2.refs_1_.refs_2_), channel_id=1, source_target_pairs={{0,4},{4,0},{8,12},{12,8},{16,20},{20,16},{24,28},{28,24},{1,5},{5... | collective-permute-start | bytes 1572872 | tf_op jit(solution)/shard_map/ppermute | solution.py:394
  45.7 8.3 %collective-permute-start.17 = (bf16[256,512]{1,0:T(8,128)(2,1)S(1)}, bf16[256,512]{1,0:T(8,128)(2,1)S(1)}, u32[]{:S(2)}, u32[]{:S(2)}) collective-permute-start(bf16[256,512]{1,0:T(8,128)(2,1)S(1)} %finish_rows.7.refs_1_), channel_id=1, source_target_pairs={{0,3},{1,2},{2,1},{3,0},{4,7},{5,6},{6,5},{7,4},{8,11},{9,10},{10,... | collective-permute-start | bytes 786440 | tf_op jit(solution)/shard_map/ppermute | solution.py:394
  54.1 14.9 %collective-permute-start.8 = (bf16[256,1024]{1,0:T(8,128)(2,1)S(1)}, bf16[256,1024]{1,0:T(8,128)(2,1)S(1)}, u32[]{:S(2)}, u32[]{:S(2)}) collective-permute-start(bf16[256,1024]{1,0:T(8,128)(2,1)S(1)} %gate.3.refs_2_.refs_3_), channel_id=1, source_target_pairs={{0,1},{1,0},{2,3},{3,2},{4,5},{5,4},{6,7},{7,6},{8,9},{9,8},{10,11... | collective-permute-start | bytes 1572872 | tf_op jit(solution)/shard_map/ppermute | solution.py:394
  54.5 14.5 %collective-permute-start.6 = (bf16[256,1024]{1,0:T(8,128)(2,1)S(1)}, bf16[256,1024]{1,0:T(8,128)(2,1)S(1)}, u32[]{:S(2)}, u32[]{:S(2)}) collective-permute-start(bf16[256,1024]{1,0:T(8,128)(2,1)S(1)} %gate.2.refs_1_.refs_2_), channel_id=1, source_target_pairs={{0,1},{1,0},{2,3},{3,2},{4,5},{5,4},{6,7},{7,6},{8,9},{9,8},{10,11... | collective-permute-start | bytes 1572872 | tf_op jit(solution)/shard_map/ppermute | solution.py:394
  54.6 14.4 %collective-permute-start.12 = (bf16[256,1024]{1,0:T(8,128)(2,1)S(1)}, bf16[256,1024]{1,0:T(8,128)(2,1)S(1)}, u32[]{:S(2)}, u32[]{:S(2)}) collective-permute-start(bf16[256,1024]{1,0:T(8,128)(2,1)S(1)} %collective-permute-done.11.refs_4_.refs_5_), channel_id=1, source_target_pairs={{0,1},{1,0},{2,3},{3,2},{4,5},{5,4},{6,7},{7,6},{8,9},{9,8},{10,11... | collective-permute-start | bytes 1572872 | tf_op jit(solution)/shard_map/ppermute | solution.py:394
  60.5 8.5 %collective-permute-start.10 = (bf16[256,1024]{1,0:T(8,128)(2,1)S(1)}, bf16[256,1024]{1,0:T(8,128)(2,1)S(1)}, u32[]{:S(2)}, u32[]{:S(2)}) collective-permute-start(bf16[256,1024]{1,0:T(8,128)(2,1)S(1)} %collective-permute-done.9.refs_3_.refs_4_), channel_id=1, source_target_pairs={{0,1},{1,0},{2,3},{3,2},{4,5},{5,4},{6,7},{7,6},{8,9},{9,8},{10,11... | collective-permute-start | bytes 1572872 | tf_op jit(solution)/shard_map/ppermute | solution.py:394
  63.8 8.2 %collective-permute-start.4 = (bf16[256,512]{1,0:T(8,128)(2,1)S(1)}, bf16[256,512]{1,0:T(8,128)(2,1)S(1)}, u32[]{:S(2)}, u32[]{:S(2)}) collective-permute-start(bf16[256,512]{1,0:T(8,128)(2,1)S(1)} %finish_rows.6), channel_id=1, source_target_pairs={{0,3},{1,2},{2,1},{3,0},{4,7},{5,6},{6,5},{7,4},{8,11},{9,10},{10,... | collective-permute-start | bytes 786440 | tf_op jit(solution)/shard_map/ppermute | solution.py:394

commit v3 on v2

--- a/solution.py
+++ b/solution.py
@@ -15,24 +15,34 @@
 HALVES = 2
 
 
+SCALE = 1.0
+
+
 def cost(us):
-    return pl.CostEstimate(flops=int(us * 1e9), bytes_accessed=int(us * 3e6), transcendentals=0)
-
-
-def call(kernel, out_shape, name, us, mib, anywhere_in=(), anywhere_out=(), n_in=0, **kw):
+    return pl.CostEstimate(
+        flops=int(us * SCALE * 1e9), bytes_accessed=int(us * SCALE * 3e6), transcendentals=0
+    )
+
+
+def call(kernel, out_shape, name, us, mib, args, after=(), anywhere_in=(), anywhere_out=(), **kw):
     vmem = pl.BlockSpec(memory_space=pltpu.VMEM)
     anywhere = pl.BlockSpec(memory_space=pl.ANY)
-    out_specs = [anywhere if i in anywhere_out else vmem for i in range(len(out_shape))]
+    n_in = len(args)
+
+    def run(*refs):
+        kernel(*refs[:n_in], *refs[n_in + len(after) :])
+
     return pl.pallas_call(
-        kernel,
-        in_specs=[anywhere if i in anywhere_in else vmem for i in range(n_in)],
-        out_specs=out_specs,
+        run,
+        in_specs=[anywhere if i in anywhere_in else vmem for i in range(n_in)]
+        + [anywhere] * len(after),
+        out_specs=[anywhere if i in anywhere_out else vmem for i in range(len(out_shape))],
         out_shape=out_shape,
         compiler_params=pltpu.CompilerParams(vmem_limit_bytes=mib * MIB),
         cost_estimate=cost(us),
         name=name,
         **kw,
-    )
+    )(*args, *after)
 
 
 def bit_count(n):
@@ -64,15 +74,16 @@
 def slice_weight(weight, shared):
     depth, width = weight.shape
     part = jax.ShapeDtypeStruct((depth // 2 if shared else depth, width // HALVES), weight.dtype)
-    return call(
+    vmem = pl.BlockSpec(memory_space=pltpu.VMEM)
+    return pl.pallas_call(
         functools.partial(slice_kernel, shared),
-        [part] * HALVES,
-        "slice_weight",
-        1,
-        4,
-        n_in=1,
-        anywhere_in=(0,),
+        in_specs=[pl.BlockSpec(memory_space=pltpu.HBM)],
+        out_specs=[vmem] * HALVES,
+        out_shape=[part] * HALVES,
         scratch_shapes=[pltpu.SemaphoreType.DMA((HALVES,))],
+        compiler_params=pltpu.CompilerParams(vmem_limit_bytes=4 * MIB),
+        cost_estimate=cost(1),
+        name="slice_weight",
     )(weight)
 
 
@@ -92,7 +103,7 @@
         own_ref[cols, :] = states[0].astype(jnp.bfloat16)
 
 
-def block_states(keys, values, heads, size):
+def block_states(keys, values, heads, size, after):
     count = keys.shape[0] // STRETCH
     return call(
         functools.partial(state_kernel, heads, size, count),
@@ -101,10 +112,11 @@
             jax.ShapeDtypeStruct((heads * size, size), jnp.bfloat16),
         ],
         "block_states",
-        2,
+        1,
         6,
-        n_in=2,
-    )(keys, values)
+        [keys, values],
+        after,
+    )
 
 
 def merge_kernel(own_ref, a_ref, b_ref, c_ref, local_ref, pair_ref, all_ref, passed_ref):
@@ -122,11 +134,11 @@
         "merge_states",
         0.2,
         2,
-        n_in=5,
+        [own, *near, local],
         anywhere_in=(4,),
         anywhere_out=(2,),
         input_output_aliases={4: 2},
-    )(own, *near, local)
+    )
 
 
 def gate_kernel(*refs):
@@ -140,25 +152,37 @@
         "gate",
         0.1,
         1,
-        n_in=1 + len(after),
-        anywhere_in=range(1 + len(after)),
+        [x],
+        after,
+        anywhere_in=(0,),
         anywhere_out=(0,),
         input_output_aliases={0: 0},
-    )(x, *after)
+    )
     return out
 
 
-def spread_weights(index_row, table):
-    plans = table.shape[0]
-    high = table.astype(jnp.bfloat16)
-    rest = table - high.astype(jnp.float32)
-    middle = rest.astype(jnp.bfloat16)
-    low = (rest - middle.astype(jnp.float32)).astype(jnp.bfloat16)
+def split_table(table_ref):
+    plans, heads, levels = table_ref.shape
+    lane = lax.broadcasted_iota(jnp.int32, (levels, LANES), 1)
+    level = lax.broadcasted_iota(jnp.int32, (levels, LANES), 0)
+    place = (lane == level).astype(jnp.float32).astype(jnp.bfloat16)
+    columns = []
+    for h in range(heads):
+        table = table_ref[:, h, :]
+        high = table.astype(jnp.bfloat16)
+        rest = table - high.astype(jnp.float32)
+        middle = rest.astype(jnp.bfloat16)
+        low = (rest - middle.astype(jnp.float32)).astype(jnp.bfloat16)
+        terms = [dot(term, place).astype(jnp.bfloat16) for term in (high, middle, low)]
+        columns.append(jnp.concatenate(terms, axis=0))
+    return jnp.concatenate(columns, axis=1)
+
+
+def spread_weights(index_row, terms):
+    plans = terms.shape[0] // 3
     plan = lax.broadcasted_iota(jnp.int32, (plans, index_row.shape[1]), 0)
     onehot = (plan == index_row).astype(jnp.float32).astype(jnp.bfloat16)
-    return contract_rows(
-        jnp.concatenate([onehot] * 3, axis=0), jnp.concatenate([high, middle, low], axis=0)
-    )
+    return contract_rows(jnp.concatenate([onehot] * 3, axis=0), terms)
 
 
 def local_kernel(
@@ -213,21 +237,49 @@
             out_ref[block, cols] = total.astype(out_ref.dtype)
 
 
-def local_attention(queries, keys, values, index_rows, table, levels, start, blocks, earlier=None):
+def first_kernel(kernel, w_ref, q_ref, k_ref, v_ref, index_ref, table_ref, level_ref, *refs):
+    out_ref, copy_ref, terms_ref, sem = refs
+    copy = pltpu.make_async_copy(w_ref, copy_ref, sem)
+    copy.start()
+    terms_ref[...] = split_table(table_ref)
+    kernel(q_ref, k_ref, v_ref, index_ref, terms_ref, level_ref, out_ref)
+    copy.wait()
+
+
+def local_attention(args, start, blocks, earlier=None, weight=None, after=()):
+    queries, levels = args[0], args[-1]
     tokens, width = queries.shape
     count = tokens // STRETCH
     heads, size = levels.shape[1], levels.shape[3]
-    extra = [] if earlier is None else [earlier]
-    (out,) = call(
-        functools.partial(local_kernel, heads, size, count, start, blocks),
-        [jax.ShapeDtypeStruct((tokens, width), jnp.bfloat16)],
+    kernel = functools.partial(local_kernel, heads, size, count, start, blocks)
+    out_shape = [jax.ShapeDtypeStruct((tokens, width), jnp.bfloat16)]
+    us, mib = blocks, 8
+    if weight is not None:
+        return call(
+            functools.partial(first_kernel, kernel),
+            out_shape
+            + [
+                jax.ShapeDtypeStruct(weight.shape, weight.dtype),
+                jax.ShapeDtypeStruct((3 * args[4].shape[0], heads * LANES), jnp.bfloat16),
+            ],
+            "local_attention",
+            us,
+            mib,
+            [weight, *args],
+            after,
+            anywhere_in=(0,),
+            scratch_shapes=[pltpu.SemaphoreType.DMA],
+        )
+    return call(
+        kernel,
+        out_shape,
         "local_attention",
-        blocks * 1.2,
-        8,
-        n_in=6 + len(extra),
-        input_output_aliases={6: 0} if extra else {},
-    )(queries, keys, values, index_rows, table, levels, *extra)
-    return out
+        us,
+        mib,
+        [*args, earlier],
+        after,
+        input_output_aliases={len(args): 0},
+    )[0]
 
 
 def finish_kernel(
@@ -252,7 +304,7 @@
             out_ref[i * STRETCH : (i + 1) * STRETCH, cols] = (total * scale).astype(out_ref.dtype)
 
 
-def finish_rows(offset, part, blocks, queries, local, index_rows, table, states, first):
+def finish_rows(after, offset, part, blocks, queries, local, index_rows, table, states, first):
     tokens, width = queries.shape
     size = states[0].shape[1]
     heads = width // size
@@ -263,19 +315,12 @@
         ),
         [jax.ShapeDtypeStruct((blocks * STRETCH, width), jnp.bfloat16)],
         "finish_rows",
-        1.5 * blocks,
+        blocks,
         4,
-        n_in=4 + len(states),
-    )(queries, local, index_rows, table, *states)
+        [queries, local, index_rows, table, *states],
+        after,
+    )
     return out
-
-
-def weight_columns(pieces, w_refs, cols):
-    start = 0
-    for at, width, ref in zip([p[0] for p in pieces], [p[1] for p in pieces], w_refs):
-        if start <= cols < start + width:
-            yield at, ref[:, pl.ds(cols - start, min(TILE, width))]
-        start += width
 
 
 def project_kernel(groups, before, rows_at, *refs):
@@ -340,17 +385,18 @@
     return groups, arrays
 
 
-def project_start(pairs, columns):
+def project_start(pairs, columns, after):
     groups, arrays = operands(pairs)
     parts = pairs[0][0].shape[0] // STRETCH
     return call(
         functools.partial(start_kernel, groups, parts),
         [jax.ShapeDtypeStruct((STRETCH, columns), jnp.float32)] * parts,
         "project_start",
-        3,
+        2.4,
         6,
-        n_in=len(arrays),
-    )(*arrays)
+        arrays,
+        after,
+    )
 
 
 def project_add(pairs, before):
@@ -361,9 +407,9 @@
         "project_add",
         1,
         6,
-        n_in=len(arrays) + 1,
+        [*arrays, before],
         input_output_aliases={len(arrays): 0},
-    )(*arrays, before)
+    )
     return out
 
 
@@ -375,9 +421,9 @@
         functools.partial(last_kernel, groups, part, len(extra)),
         [jax.ShapeDtypeStruct((parts * STRETCH, columns), jnp.bfloat16)],
         "project_last",
-        1,
+        1.5,
         8,
-        n_in=len(arrays) + 1 + len(extra),
+        [*arrays, before, *extra],
         anywhere_in=(len(arrays) + 1,),
         anywhere_out=(0,),
         input_output_aliases={len(arrays) + 1: 0} if extra else {},
@@ -385,7 +431,7 @@
             pltpu.VMEM((columns // TILE, STRETCH, TILE), jnp.bfloat16),
             pltpu.SemaphoreType.DMA((columns // TILE,)),
         ],
-    )(*arrays, before, *extra)
+    )
     return out
 
 
@@ -403,7 +449,7 @@
 
 def body(queries, key_vectors, value_vectors, level_index, level_table, out_weight):
     tokens, width = queries.shape
-    plans, heads, level_total = level_table.shape
+    heads = level_table.shape[1]
     size = width // heads
     ctx_size, mp_size = lax.axis_size("ctx"), lax.axis_size("mp")
     ctx_bits = bit_count(ctx_size)
@@ -411,29 +457,26 @@
     columns = out_weight.shape[1]
     first = bit_count(STRETCH) + 1 + bit_count(count)
 
-    table = jnp.pad(level_table, ((0, 0), (0, 0), (0, LANES - level_total))).reshape(
-        plans, heads * LANES
-    )
     index_rows = level_index.reshape(count, 1, STRETCH)
 
     shared = ctx_size > 1
     portion = slice_weight(out_weight, shared)
     got = {j: [flip(p, "mp", j) for p in portion] for j in range(2, mp_size, 2)}
 
-    levels, own = block_states(key_vectors, value_vectors, heads, size)
+    levels, own = block_states(key_vectors, value_vectors, heads, size, portion)
     near = [flip(own, "ctx", b) for b in range(1, min(4, ctx_size))]
 
-    attend = functools.partial(
-        local_attention, queries, key_vectors, value_vectors, index_rows, table, levels
-    )
+    args = [queries, key_vectors, value_vectors, index_rows, level_table, levels]
     cut = count // 2
-    local = attend(0, cut)
+    local, weight, terms = local_attention(args, 0, cut, weight=out_weight, after=[own])
+    args[4] = terms
+
     remote = near[:1]
-    after = local
+    ready = near[0] if near else local
     if ctx_bits > 1:
         pair, running, local = merge_states(own, near, local)
         remote.append(pair)
-        after = running
+        ready = running
     far = None
     for b in range(2, ctx_bits):
         if b > 2:
@@ -441,41 +484,68 @@
         far = flip(running, "ctx", 1 << b)
         remote.append(far)
 
-    there = {}
-    for j in got:
-        got[j][0] = gate(got[j][0], after)
-        there[j] = [flip(got[j][0], "ctx", 1)]
-    mate = flip(gate(out_weight, after) if False else out_weight, "mp", 1)
-
-    local = attend(cut, count - cut, local)
+    there, across, across_there = {}, {}, {}
+
+    def forward(c, after):
+        for j in got:
+            got[j][c] = gate(got[j][c], *after)
+            if shared:
+                there.setdefault(j, []).append(flip(got[j][c], "ctx", 1))
+            across.setdefault(j, []).append(flip(got[j][c], "mp", 1))
+        return [got[j][c] for j in got]
+
+    def forward_there(c, after):
+        for j in there:
+            there[j][c] = gate(there[j][c], *after)
+            across_there.setdefault(j, []).append(flip(there[j][c], "mp", 1))
+        return [there[j][c] for j in there]
+
+    held = forward(0, [ready])
+    weight = gate(weight, ready, *held)
+    mate = flip(weight, "mp", 1)
+    local = local_attention(
+        args, cut, count - cut, earlier=local, after=[ready, weight] + held
+    )
 
     parts = tokens // mp_size // STRETCH
+    done = [mate] + [across[j][0] for j in got]
 
     def finished(j, part, blocks):
-        return finish_rows(j, part, blocks, queries, local, index_rows, table, remote, first)
+        nonlocal done
+        out = finish_rows(
+            done, j, part, blocks, queries, local, index_rows, terms, remote, first
+        )
+        done = [out]
+        return out
 
     received = {}
-    last = None
-    for part in range(parts):
-        for j in range(2, mp_size):
-            last = finished(j, part, 1)
-            received[j, part] = flip(last, "mp", j)
-        if part == 0:
-            for j in got:
-                for c in range(1, HALVES):
-                    got[j][c] = gate(got[j][c], last)
-                    there[j].append(flip(got[j][c], "ctx", 1))
+    far_groups = list(range(2, mp_size))
+    order = [(j, part) for part in range(parts) for j in far_groups]
+    for i, (j, part) in enumerate(order[:-1]):
+        received[j, part] = flip(finished(j, part, 1), "mp", j)
+        if i == 0:
+            done += [there[j][0] for j in there]
+        if i == 1:
+            done += forward(1, done)
+    later = {(j, part): finished(j, part, 1) for j, part in order[-1:]}
+    close = [(finished(0, 0, parts), [(None, [weight])])]
+    theirs = finished(1, 0, parts) if mp_size > 1 else None
+
+    over = done + list(received.values()) + [across[j][1] for j in got]
+    for c in range(HALVES):
+        over += forward_there(c, over)
+    for (j, part), x in later.items():
+        received[j, part] = flip(x, "mp", j)
+    if mp_size > 1:
+        theirs = gate(theirs, *over)
+        close.append((flip(theirs, "mp", 1), [(None, [mate])]))
+    totals = project_start(close, columns, over)
+
     gathered = {}
     for j in got:
-        gathered[j] = [(0, got[j]), (1, there[j])]
-        gathered[j + 1] = [(at, [flip(w, "mp", 1) for w in row]) for at, row in gathered[j]]
-
-    close = [(finished(0, 0, parts), [(None, [out_weight])])]
-    if mp_size > 1:
-        close.append((flip(finished(1, 0, parts), "mp", 1), [(None, [mate])]))
-    totals = project_start(close, columns)
-
-    far_groups = list(range(2, mp_size))
+        gathered[j] = [(0, got[j])] + ([(1, there[j])] if shared else [])
+        gathered[j + 1] = [(0, across[j])] + ([(1, across_there[j])] if shared else [])
+
     out = None
     for part in range(parts):
         total = totals[part]

time: 73.8 us -> 60 us (0.81)
  waiting for transfers between devices: 25.8 us -> 10.7 us
  local copies, waits for them, and re-layouts: 3.22 us -> 4.97 us
  starting transfers between devices: 19.6 us -> 18.8 us
    ppermute x18, waiting for transfers between devices: 25.8 us -> 10.7 us  [flip(): return lax.ppermute(x, axis, [(i, i ^ bits) for i in range(n)])]
    unnamed x17, local copies, waits for them, and re-layouts: 3.22 us -> 4.97 us
    ppermute x18, starting transfers between devices: 19.6 us -> 18.8 us  [flip(): return lax.ppermute(x, axis, [(i, i ^ bits) for i in range(n)])]
    pallas_call x17 -> x21, Pallas kernels: 24.7 us -> 25 us  [the longest x20 24.9 us: call(): pl.pallas_call(run, in_specs=[anywhere if i in anywhere_in else vmem for...]
  transfers between devices with their start and end apart: 18 -> 18, of which waited for: 7 -> 6; matrix products, arithmetic and copies ran while one was open for 0% -> 0% of each run, Pallas kernels for 30% -> 39%
where the time goes in v3:
time: 60 us; the launch traced here: 59.9 us
  Pallas kernels  25 us (42%)
  starting transfers between devices  18.8 us (31%)
  waiting for transfers between devices  10.7 us (18%)
  local copies, waits for them, and re-layouts  4.97 us (8%)
    pallas_call x20, Pallas kernels, call(): pl.pallas_call(run, in_specs=[anywhere if i in anywhere_in else vmem for...  24.9 us
    ppermute x18, starting transfers between devices, flip(): return lax.ppermute(x, axis, [(i, i ^ bits) for i in range(n)])  18.8 us
    ppermute x18, waiting for transfers between devices, flip(): return lax.ppermute(x, axis, [(i, i ^ bits) for i in range(n)])  10.7 us
    unnamed x17, local copies, waits for them, and re-layouts  4.97 us
  transfers between devices with their start and end apart: 18, of which 6 were waited for; matrix products, arithmetic and copies ran while one was open for 0% of the time, Pallas kernels for 39%

profile of v3, /device:TPU:0, one launch (start us, length us, event | category | flops | bytes accessed | tf_op | source)
XLA Modules:
  0.0 59.9 jit_solution(14073868564252527392)
XLA Ops:
  0.0 0.0 copy-start.1
  0.0 1.7 %copy-done.5 = bf16[512,2048]{1,0:T(8,128)(2,1)S(1)} copy-done((bf16[512,2048]{1,0:T(8,128)(2,1)S(1)}, bf16[512,2048]{1,0:T(8,128)(2,1)}, u32[]{:S(2)}) %copy-start.5) | copy-done | bytes 2097176
  1.7 0.1 slice_weight.1
  1.9 3.0 %collective-permute-start.3 = (bf16[256,1024]{1,0:T(8,128)(2,1)S(1)}, bf16[256,1024]{1,0:T(8,128)(2,1)S(1)}, u32[]{:S(2)}, u32[]{:S(2)}) collective-permute-start(bf16[256,1024]{1,0:T(8,128)(2,1)S(1)} %get-tuple-element.17.refs_2_), channel_id=1, source_target_pairs={{0,2},{1,3},{2,0},{3,1},{4,6},{5,7},{6,4},{7,5},{8,10},{9,11},{10,... | collective-permute-start | bytes 1572872 | tf_op jit(solution)/shard_map/ppermute | solution.py:440
  4.9 0.0 copy-done.1
  4.9 0.0 copy-start.2
  4.9 1.6 %copy-done.2 = bf16[2048,512]{1,0:T(8,128)(2,1)S(1)} copy-done((bf16[2048,512]{1,0:T(8,128)(2,1)S(1)}, bf16[2048,512]{1,0:T(8,128)(2,1)}, u32[]{:S(2)}) %copy-start.2) | copy-done | bytes 2097176
  6.5 0.0 copy-start
  6.5 0.0 copy-start.3
  6.5 0.8 %block_states.1 = (bf16[7,4,128,128]{3,2,1,0:T(8,128)(2,1)S(1)}, bf16[512,128]{1,0:T(8,128)(2,1)S(1)}) custom-call(bf16[2048,512]{1,0:T(8,128)(2,1)S(1)} %copy-done.1, bf16[2048,512]{1,0:T(8,128)(2,1)S(1)} %copy-done.2, bf16[256,1024]{1,0:T(8,128)(2,1)S(1)} %get-tuple-element.17.refs_2_, bf16[256,1024]{1,0:T(8,128)(2,1)S(1)} %get-tuple-element.18.refs_3_), custom_call_target="tpu_custom_call" | custom-call | flops 1000000000 | bytes 3000000 | tf_op jit(solution)/shard_map/block_states/pallas_call | solution.py:35
  7.3 2.6 %collective-permute-start.2 = (bf16[512,128]{1,0:T(8,128)(2,1)S(1)}, bf16[512,128]{1,0:T(8,128)(2,1)S(1)}, u32[]{:S(2)}, u32[]{:S(2)}) collective-permute-start(bf16[512,128]{1,0:T(8,128)(2,1)S(1)} %get-tuple-element.20.refs_7_.refs_0_), channel_id=1, source_target_pairs={{0,12},{4,8},{8,4},{12,0},{16,28},{20,24},{24,20},{28,16},{1,13},{... | collective-permute-start | bytes 393224 | tf_op jit(solution)/shard_map/ppermute | solution.py:440
  9.9 0.4 collective-permute-start.1
  10.3 0.5 collective-permute-start
  10.8 0.0 copy-done
  10.8 0.0 copy-done.3
  10.8 0.0 copy-done.4
  10.8 0.0 copy-done.7
  10.8 0.0 copy-start.6
  10.9 1.6 %copy-done.6 = bf16[512,2048]{1,0:T(8,128)(2,1)S(1)} copy-done((bf16[512,2048]{1,0:T(8,128)(2,1)S(1)}, bf16[512,2048]{1,0:T(8,128)(2,1)}, u32[]{:S(2)}) %copy-start.6) | copy-done | bytes 2097176
  12.4 4.0 %local_attention.2 = (bf16[2048,512]{1,0:T(8,128)(2,1)S(1)}, bf16[512,2048]{1,0:T(8,128)(2,1)S(1)}, bf16[48,512]{1,0:T(8,128)(2,1)S(1)}) custom-call(bf16[512,2048]{1,0:T(8,128)(2,1)S(1)} %copy-done.6, bf16[2048,512]{1,0:T(8,128)(2,1)S(1)} %copy-done, bf16[2048,512]{1,0:T(8,128)(2,1)S(1)} %copy-done.1, bf16[2048,512]{1,0:T(8,128)(2,1)S(1)} %copy-done.3, ...), custom_call_target="tpu_custom_call" | custom-call | flops 4000000000 | bytes 12000000 | tf_op jit(solution)/shard_map/local_attention/pallas_call | solution.py:35
  16.5 0.0 collective-permute-done.2.refs_3_
  16.5 0.0 collective-permute-done.1.refs_2_
  16.5 0.0 collective-permute-done.refs_1_.refs_4_
  16.5 0.1 merge_states.1
  16.6 0.2 collective-permute-done.3.refs_0_
  16.8 0.0 collective-permute-start.5
  16.8 0.5 collective-permute-start.6
  17.3 1.8 %collective-permute-start.7 = (bf16[256,1024]{1,0:T(8,128)(2,1)S(1)}, bf16[256,1024]{1,0:T(8,128)(2,1)S(1)}, u32[]{:S(2)}, u32[]{:S(2)}) collective-permute-start(bf16[256,1024]{1,0:T(8,128)(2,1)S(1)} %gate.6.refs_2_.refs_9_.refs_1_), channel_id=1, source_target_pairs={{0,4},{4,0},{8,12},{12,8},{16,20},{20,16},{24,28},{28,24},{1,5},{5... | collective-permute-start | bytes 1572872 | tf_op jit(solution)/shard_map/ppermute | solution.py:440
  19.1 1.5 %collective-permute-start.8 = (bf16[256,1024]{1,0:T(8,128)(2,1)S(1)}, bf16[256,1024]{1,0:T(8,128)(2,1)S(1)}, u32[]{:S(2)}, u32[]{:S(2)}) collective-permute-start(bf16[256,1024]{1,0:T(8,128)(2,1)S(1)} %get-tuple-element.18.refs_3_), channel_id=1, source_target_pairs={{0,2},{1,3},{2,0},{3,1},{4,6},{5,7},{6,4},{7,5},{8,10},{9,11},{10,... | collective-permute-start | bytes 1572872 | tf_op jit(solution)/shard_map/ppermute | solution.py:440
  20.6 2.6 %collective-permute-start.4 = (bf16[512,128]{1,0:T(8,128)(2,1)S(1)}, bf16[512,128]{1,0:T(8,128)(2,1)S(1)}, u32[]{:S(2)}, u32[]{:S(2)}) collective-permute-start(bf16[512,128]{1,0:T(8,128)(2,1)S(1)} %get-tuple-element.24.refs_1_.refs_7_), channel_id=1, source_target_pairs={{0,16},{4,20},{8,24},{12,28},{16,0},{20,4},{24,8},{28,12},{1,17},{... | collective-permute-start | bytes 393224 | tf_op jit(solution)/shard_map/ppermute | solution.py:440
  23.2 4.3 %local_attention.3.refs_1_ = bf16[2048,512]{1,0:T(8,128)(2,1)S(1)} custom-call(bf16[2048,512]{1,0:T(8,128)(2,1)S(1)} %copy-done, bf16[2048,512]{1,0:T(8,128)(2,1)S(1)} %copy-done.1, bf16[2048,512]{1,0:T(8,128)(2,1)S(1)} %copy-done.3, s32[8,1,256]{2,1,0:T(1,128)S(1)} %bitcast.2, ...), custom_call_target="tpu_custom_call", output_to_operand_aliasing={{}: (6, {})} | custom-call | flops 4000000000 | bytes 12000000 | tf_op jit(solution)/shard_map/local_attention/pallas_call | solution.py:35
  27.5 1.6 %collective-permute-done.4.refs_6_ = bf16[512,128]{1,0:T(8,128)(2,1)S(1)} collective-permute-done((bf16[512,128]{1,0:T(8,128)(2,1)S(1)}, bf16[512,128]{1,0:T(8,128)(2,1)S(1)}, u32[]{:S(2)}, u32[]{:S(2)}) %collective-permute-start.4) | collective-permute-done | bytes 131104 | tf_op jit(solution)/shard_map/ppermute | solution.py:440
  29.1 0.0 collective-permute-done.6.refs_8_.refs_6_.refs_1_
  29.1 0.0 collective-permute-done.5.refs_7_.refs_3_
  29.1 1.0 %finish_rows.6.refs_7_ = bf16[256,512]{1,0:T(8,128)(2,1)S(1)} custom-call(bf16[2048,512]{1,0:T(8,128)(2,1)S(1)} %copy-done, bf16[2048,512]{1,0:T(8,128)(2,1)S(1)} %local_attention.3.refs_1_, s32[8,1,256]{2,1,0:T(1,128)S(1)} %bitcast.3, bf16[48,512]{1,0:T(8,128)(2,1)S(1)} %get-tuple-element.21.refs_4_.refs_3_, ...), custom_call_target="tpu_custom_call" | custom-call | flops 1000000000 | bytes 3000000 | tf_op jit(solution)/shard_map/finish_rows/pallas_call | solution.py:35
  30.2 0.6 collective-permute-start.11
  30.8 0.4 collective-permute-done.7.refs_8_.refs_0_
  31.2 1.0 %finish_rows.7.refs_1_.refs_7_ = bf16[256,512]{1,0:T(8,128)(2,1)S(1)} custom-call(bf16[2048,512]{1,0:T(8,128)(2,1)S(1)} %copy-done, bf16[2048,512]{1,0:T(8,128)(2,1)S(1)} %local_attention.3.refs_1_, s32[8,1,256]{2,1,0:T(1,128)S(1)} %bitcast.4, bf16[48,512]{1,0:T(8,128)(2,1)S(1)} %get-tuple-element.21.refs_4_.refs_3_, ...), custom_call_target="tpu_custom_call" | custom-call | flops 1000000000 | bytes 3000000 | tf_op jit(solution)/shard_map/finish_rows/pallas_call | solution.py:35
  32.2 0.5 collective-permute-start.12
  32.7 0.7 %collective-permute-done.8.refs_0_ = bf16[256,1024]{1,0:T(8,128)(2,1)S(1)} collective-permute-done((bf16[256,1024]{1,0:T(8,128)(2,1)S(1)}, bf16[256,1024]{1,0:T(8,128)(2,1)S(1)}, u32[]{:S(2)}, u32[]{:S(2)}) %collective-permute-start.8) | collective-permute-done | bytes 524320 | tf_op jit(solution)/shard_map/ppermute | solution.py:440
  33.4 0.8 %collective-permute-start.15 = (bf16[256,1024]{1,0:T(8,128)(2,1)S(1)}, bf16[256,1024]{1,0:T(8,128)(2,1)S(1)}, u32[]{:S(2)}, u32[]{:S(2)}) collective-permute-start(bf16[256,1024]{1,0:T(8,128)(2,1)S(1)} %gate.8.refs_8_.refs_2_.refs_3_), channel_id=1, source_target_pairs={{0,4},{4,0},{8,12},{12,8},{16,20},{20,16},{24,28},{28,24},{1,5},{5... | collective-permute-start | bytes 1572872 | tf_op jit(solution)/shard_map/ppermute | solution.py:440
  34.3 1.1 %collective-permute-start.10 = (bf16[256,1024]{1,0:T(8,128)(2,1)S(1)}, bf16[256,1024]{1,0:T(8,128)(2,1)S(1)}, u32[]{:S(2)}, u32[]{:S(2)}) collective-permute-start(bf16[256,1024]{1,0:T(8,128)(2,1)S(1)} %gate.8.refs_8_.refs_2_.refs_3_), channel_id=1, source_target_pairs={{0,1},{1,0},{2,3},{3,2},{4,5},{5,4},{6,7},{7,6},{8,9},{9,8},{10,11... | collective-permute-start | bytes 1572872 | tf_op jit(solution)/shard_map/ppermute | solution.py:440
  35.3 1.0 %finish_rows.8.refs_7_ = bf16[256,512]{1,0:T(8,128)(2,1)S(1)} custom-call(bf16[2048,512]{1,0:T(8,128)(2,1)S(1)} %copy-done, bf16[2048,512]{1,0:T(8,128)(2,1)S(1)} %local_attention.3.refs_1_, s32[8,1,256]{2,1,0:T(1,128)S(1)} %bitcast.5, bf16[48,512]{1,0:T(8,128)(2,1)S(1)} %get-tuple-element.21.refs_4_.refs_3_, ...), custom_call_target="tpu_custom_call" | custom-call | flops 1000000000 | bytes 3000000 | tf_op jit(solution)/shard_map/finish_rows/pallas_call | solution.py:35
  36.4 0.6 %collective-permute-start.13 = (bf16[256,512]{1,0:T(8,128)(2,1)S(1)}, bf16[256,512]{1,0:T(8,128)(2,1)S(1)}, u32[]{:S(2)}, u32[]{:S(2)}) collective-permute-start(bf16[256,512]{1,0:T(8,128)(2,1)S(1)} %finish_rows.8.refs_7_), channel_id=1, source_target_pairs={{0,2},{1,3},{2,0},{3,1},{4,6},{5,7},{6,4},{7,5},{8,10},{9,11},{10,... | collective-permute-start | bytes 786440 | tf_op jit(solution)/shard_map/ppermute | solution.py:440
  37.0 1.0 %finish_rows.9.refs_7_ = bf16[256,512]{1,0:T(8,128)(2,1)S(1)} custom-call(bf16[2048,512]{1,0:T(8,128)(2,1)S(1)} %copy-done, bf16[2048,512]{1,0:T(8,128)(2,1)S(1)} %local_attention.3.refs_1_, s32[8,1,256]{2,1,0:T(1,128)S(1)} %bitcast.6, bf16[48,512]{1,0:T(8,128)(2,1)S(1)} %get-tuple-element.21.refs_4_.refs_3_, ...), custom_call_target="tpu_custom_call" | custom-call | flops 1000000000 | bytes 3000000 | tf_op jit(solution)/shard_map/finish_rows/pallas_call | solution.py:35
  38.1 2.4 %finish_rows.10.refs_7_.refs_0_ = bf16[512,512]{1,0:T(8,128)(2,1)S(1)} custom-call(bf16[2048,512]{1,0:T(8,128)(2,1)S(1)} %copy-done, bf16[2048,512]{1,0:T(8,128)(2,1)S(1)} %local_attention.3.refs_1_, s32[8,1,256]{2,1,0:T(1,128)S(1)} %bitcast.7, bf16[48,512]{1,0:T(8,128)(2,1)S(1)} %get-tuple-element.21.refs_4_.refs_3_, ...), custom_call_target="tpu_custom_call" | custom-call | flops 2000000000 | bytes 6000000 | tf_op jit(solution)/shard_map/finish_rows/pallas_call | solution.py:35
  40.5 2.3 %finish_rows.11.refs_1_.refs_4_ = bf16[512,512]{1,0:T(8,128)(2,1)S(1)} custom-call(bf16[2048,512]{1,0:T(8,128)(2,1)S(1)} %copy-done, bf16[2048,512]{1,0:T(8,128)(2,1)S(1)} %local_attention.3.refs_1_, s32[8,1,256]{2,1,0:T(1,128)S(1)} %bitcast.8, bf16[48,512]{1,0:T(8,128)(2,1)S(1)} %get-tuple-element.21.refs_4_.refs_3_, ...), custom_call_target="tpu_custom_call" | custom-call | flops 2000000000 | bytes 6000000 | tf_op jit(solution)/shard_map/finish_rows/pallas_call | solution.py:35
  42.8 6.7 %collective-permute-done.13.refs_4_.refs_7_.refs_0_ = bf16[256,512]{1,0:T(8,128)(2,1)S(1)} collective-permute-done((bf16[256,512]{1,0:T(8,128)(2,1)S(1)}, bf16[256,512]{1,0:T(8,128)(2,1)S(1)}, u32[]{:S(2)}, u32[]{:S(2)}) %collective-permute-start.13) | collective-permute-done | bytes 262176 | tf_op jit(solution)/shard_map/ppermute | solution.py:440
  49.5 0.0 collective-permute-done.12.refs_3_.refs_6_.refs_1_
  49.5 0.0 collective-permute-done.11.refs_2_.refs_5_.refs_0_
  49.5 0.0 collective-permute-done.10.refs_5_.refs_8_.refs_7_.refs_2_
  49.5 0.0 collective-permute-done.15.refs_0_
  49.5 0.1 collective-permute-start.17
  49.6 0.5 collective-permute-start.16
  50.1 0.1 collective-permute-start.14
  50.2 1.5 %collective-permute-start.9 = (bf16[256,512]{1,0:T(8,128)(2,1)S(1)}, bf16[256,512]{1,0:T(8,128)(2,1)S(1)}, u32[]{:S(2)}, u32[]{:S(2)}) collective-permute-start(bf16[256,512]{1,0:T(8,128)(2,1)S(1)} %finish_rows.9.refs_7_), channel_id=1, source_target_pairs={{0,3},{1,2},{2,1},{3,0},{4,7},{5,6},{6,5},{7,4},{8,11},{9,10},{10,... | collective-permute-start | bytes 786440 | tf_op jit(solution)/shard_map/ppermute | solution.py:440
  51.7 0.0 collective-permute-done.17.refs_1_
  51.7 2.3 %project_start.1 = (f32[256,2048]{1,0:T(8,128)S(1)}, f32[256,2048]{1,0:T(8,128)S(1)}) custom-call(bf16[512,512]{1,0:T(8,128)(2,1)S(1)} %finish_rows.10.refs_7_.refs_0_, bf16[512,512]{1,0:T(8,128)(2,1)S(1)} %collective-permute-done.17.refs_1_, bf16[512,2048]{1,0:T(8,128)(2,1)S(1)} %gate.7.refs_8_.refs_2_, ...), custom_call_target="tpu_custom_call" | custom-call | flops 2400000000 | bytes 7200000 | tf_op jit(solution)/shard_map/project_start/pallas_call | solution.py:35
  54.1 0.9 %project_add.1.refs_5_ = f32[256,2048]{1,0:T(8,128)S(1)} custom-call(bf16[256,512]{1,0:T(8,128)(2,1)S(1)} %collective-permute-done.13.refs_4_.refs_7_.refs_0_, bf16[256,1024]{1,0:T(8,128)(2,1)S(1)} %gate.6.refs_2_.refs_9_.refs_1_, bf16[256,1024]{1,0:T(8,128)(2,1)S(1)} %gate.8.refs_8_.refs_2_.refs_3_, ...), custom_call_target="tpu_custom_call", output_to_operand_aliasing={{}: (5, {})} | custom-call | flops 1000000000 | bytes 3000000 | tf_op jit(solution)/shard_map/project_add/pallas_call | solution.py:35
  55.0 0.0 collective-permute-done.16.refs_9_.refs_4_
  55.0 0.0 collective-permute-done.14.refs_8_.refs_3_
  55.0 2.0 %project_last.2.refs_6_ = bf16[512,2048]{1,0:T(8,128)(2,1)} custom-call(bf16[256,512]{1,0:T(8,128)(2,1)S(1)} %collective-permute-done.11.refs_2_.refs_5_.refs_0_, bf16[256,512]{1,0:T(8,128)(2,1)S(1)} %collective-permute-done.12.refs_3_.refs_6_.refs_1_, bf16[256,1024]{1,0:T(8,128)(2,1)S(1)} %gate.6.refs_2_.refs_9_.refs_1_, ...), custom_call_target="tpu_custom_call" | custom-call | flops 1500000000 | bytes 4500000 | tf_op jit(solution)/shard_map/project_last/pallas_call | solution.py:35
  57.0 1.2 %collective-permute-done.9.refs_0_ = bf16[256,512]{1,0:T(8,128)(2,1)S(1)} collective-permute-done((bf16[256,512]{1,0:T(8,128)(2,1)S(1)}, bf16[256,512]{1,0:T(8,128)(2,1)S(1)}, u32[]{:S(2)}, u32[]{:S(2)}) %collective-permute-start.9) | collective-permute-done | bytes 262176 | tf_op jit(solution)/shard_map/ppermute | solution.py:440
  58.2 1.5 %project_last.3 = bf16[512,2048]{1,0:T(8,128)(2,1)} custom-call(bf16[256,512]{1,0:T(8,128)(2,1)S(1)} %collective-permute-done.9.refs_0_, bf16[256,1024]{1,0:T(8,128)(2,1)S(1)} %collective-permute-done.6.refs_8_.refs_6_.refs_1_, bf16[256,1024]{1,0:T(8,128)(2,1)S(1)} %collective-permute-done.10.refs_5_.refs_8_.refs_7_.refs_2_, ...), custom_call_target="tpu_custom_call", output_to_operand_aliasing={{}: (6, {})} | custom-call | flops 1500000000 | bytes 4500000 | tf_op jit(solution)/shard_map/project_last/pallas_call | solution.py:35
  (10 shorter events, 0.1 us)
Async XLA Ops:
  0.0 4.9 %copy-start.1 = (bf16[2048,512]{1,0:T(8,128)(2,1)S(1)}, bf16[2048,512]{1,0:T(8,128)(2,1)}, u32[]{:S(2)}) copy-start(bf16[2048,512]{1,0:T(8,128)(2,1)} %refs_1_.5) | copy-start | bytes 6291460
  0.0 1.7 %copy-start.5 = (bf16[512,2048]{1,0:T(8,128)(2,1)S(1)}, bf16[512,2048]{1,0:T(8,128)(2,1)}, u32[]{:S(2)}) copy-start(bf16[512,2048]{1,0:T(8,128)(2,1)} %refs_0_.10) | copy-start | bytes 6291460
  1.9 14.9 %collective-permute-start.3 = (bf16[256,1024]{1,0:T(8,128)(2,1)S(1)}, bf16[256,1024]{1,0:T(8,128)(2,1)S(1)}, u32[]{:S(2)}, u32[]{:S(2)}) collective-permute-start(bf16[256,1024]{1,0:T(8,128)(2,1)S(1)} %get-tuple-element.17.refs_2_), channel_id=1, source_target_pairs={{0,2},{1,3},{2,0},{3,1},{4,6},{5,7},{6,4},{7,5},{8,10},{9,11},{10,... | collective-permute-start | bytes 1572872 | tf_op jit(solution)/shard_map/ppermute | solution.py:440
  4.9 1.6 %copy-start.2 = (bf16[2048,512]{1,0:T(8,128)(2,1)S(1)}, bf16[2048,512]{1,0:T(8,128)(2,1)}, u32[]{:S(2)}) copy-start(bf16[2048,512]{1,0:T(8,128)(2,1)} %refs_2_.3) | copy-start | bytes 6291460
  6.5 4.4 %copy-start = (bf16[2048,512]{1,0:T(8,128)(2,1)S(1)}, bf16[2048,512]{1,0:T(8,128)(2,1)}, u32[]{:S(2)}) copy-start(bf16[2048,512]{1,0:T(8,128)(2,1)} %refs_0_.17) | copy-start | bytes 6291460
  6.5 4.4 %copy-start.3 = (bf16[2048,512]{1,0:T(8,128)(2,1)S(1)}, bf16[2048,512]{1,0:T(8,128)(2,1)}, u32[]{:S(2)}) copy-start(bf16[2048,512]{1,0:T(8,128)(2,1)} %refs_2_.3) | copy-start | bytes 6291460
  6.5 4.4 %copy-start.4 = (s32[2048]{0:T(1024)S(1)}, s32[2048]{0:T(1024)}, u32[]{:S(2)}) copy-start(s32[2048]{0:T(1024)} %param.9) | copy-start | bytes 24580
  6.5 4.4 %copy-start.7 = (f32[16,4,20]{2,1,0:T(4,128)S(1)}, f32[16,4,20]{2,1,0:T(4,128)}, u32[]{:S(2)}) copy-start(f32[16,4,20]{2,1,0:T(4,128)} %refs_5_.1) | copy-start | bytes 15364
  7.3 9.2 %collective-permute-start.2 = (bf16[512,128]{1,0:T(8,128)(2,1)S(1)}, bf16[512,128]{1,0:T(8,128)(2,1)S(1)}, u32[]{:S(2)}, u32[]{:S(2)}) collective-permute-start(bf16[512,128]{1,0:T(8,128)(2,1)S(1)} %get-tuple-element.20.refs_7_.refs_0_), channel_id=1, source_target_pairs={{0,12},{4,8},{8,4},{12,0},{16,28},{20,24},{24,20},{28,16},{1,13},{... | collective-permute-start | bytes 393224 | tf_op jit(solution)/shard_map/ppermute | solution.py:440
  9.9 6.6 %collective-permute-start.1 = (bf16[512,128]{1,0:T(8,128)(2,1)S(1)}, bf16[512,128]{1,0:T(8,128)(2,1)S(1)}, u32[]{:S(2)}, u32[]{:S(2)}) collective-permute-start(bf16[512,128]{1,0:T(8,128)(2,1)S(1)} %get-tuple-element.20.refs_7_.refs_0_), channel_id=1, source_target_pairs={{0,8},{4,12},{8,0},{12,4},{16,24},{20,28},{24,16},{28,20},{1,9},{5... | collective-permute-start | bytes 393224 | tf_op jit(solution)/shard_map/ppermute | solution.py:440
  10.3 6.2 %collective-permute-start = (bf16[512,128]{1,0:T(8,128)(2,1)S(1)}, bf16[512,128]{1,0:T(8,128)(2,1)S(1)}, u32[]{:S(2)}, u32[]{:S(2)}) collective-permute-start(bf16[512,128]{1,0:T(8,128)(2,1)S(1)} %get-tuple-element.20.refs_7_.refs_0_), channel_id=1, source_target_pairs={{0,4},{4,0},{8,12},{12,8},{16,20},{20,16},{24,28},{28,24},{1,5},{5... | collective-permute-start | bytes 393224 | tf_op jit(solution)/shard_map/ppermute | solution.py:440
  10.8 1.6 %copy-start.6 = (bf16[512,2048]{1,0:T(8,128)(2,1)S(1)}, bf16[512,2048]{1,0:T(8,128)(2,1)}, u32[]{:S(2)}) copy-start(bf16[512,2048]{1,0:T(8,128)(2,1)} %refs_0_.10) | copy-start | bytes 6291460
  16.8 12.3 %collective-permute-start.5 = (bf16[512,2048]{1,0:T(8,128)(2,1)S(1)}, bf16[512,2048]{1,0:T(8,128)(2,1)S(1)}, u32[]{:S(2)}, u32[]{:S(2)}) collective-permute-start(bf16[512,2048]{1,0:T(8,128)(2,1)S(1)} %gate.7.refs_8_.refs_2_), channel_id=1, source_target_pairs={{0,1},{1,0},{2,3},{3,2},{4,5},{5,4},{6,7},{7,6},{8,9},{9,8},{10,11... | collective-permute-start | bytes 6291464 | tf_op jit(solution)/shard_map/ppermute | solution.py:440
  16.8 12.3 %collective-permute-start.6 = (bf16[256,1024]{1,0:T(8,128)(2,1)S(1)}, bf16[256,1024]{1,0:T(8,128)(2,1)S(1)}, u32[]{:S(2)}, u32[]{:S(2)}) collective-permute-start(bf16[256,1024]{1,0:T(8,128)(2,1)S(1)} %gate.6.refs_2_.refs_9_.refs_1_), channel_id=1, source_target_pairs={{0,1},{1,0},{2,3},{3,2},{4,5},{5,4},{6,7},{7,6},{8,9},{9,8},{10,11... | collective-permute-start | bytes 1572872 | tf_op jit(solution)/shard_map/ppermute | solution.py:440
  17.3 13.9 %collective-permute-start.7 = (bf16[256,1024]{1,0:T(8,128)(2,1)S(1)}, bf16[256,1024]{1,0:T(8,128)(2,1)S(1)}, u32[]{:S(2)}, u32[]{:S(2)}) collective-permute-start(bf16[256,1024]{1,0:T(8,128)(2,1)S(1)} %gate.6.refs_2_.refs_9_.refs_1_), channel_id=1, source_target_pairs={{0,4},{4,0},{8,12},{12,8},{16,20},{20,16},{24,28},{28,24},{1,5},{5... | collective-permute-start | bytes 1572872 | tf_op jit(solution)/shard_map/ppermute | solution.py:440
  19.1 14.3 %collective-permute-start.8 = (bf16[256,1024]{1,0:T(8,128)(2,1)S(1)}, bf16[256,1024]{1,0:T(8,128)(2,1)S(1)}, u32[]{:S(2)}, u32[]{:S(2)}) collective-permute-start(bf16[256,1024]{1,0:T(8,128)(2,1)S(1)} %get-tuple-element.18.refs_3_), channel_id=1, source_target_pairs={{0,2},{1,3},{2,0},{3,1},{4,6},{5,7},{6,4},{7,5},{8,10},{9,11},{10,... | collective-permute-start | bytes 1572872 | tf_op jit(solution)/shard_map/ppermute | solution.py:440
  20.6 8.6 %collective-permute-start.4 = (bf16[512,128]{1,0:T(8,128)(2,1)S(1)}, bf16[512,128]{1,0:T(8,128)(2,1)S(1)}, u32[]{:S(2)}, u32[]{:S(2)}) collective-permute-start(bf16[512,128]{1,0:T(8,128)(2,1)S(1)} %get-tuple-element.24.refs_1_.refs_7_), channel_id=1, source_target_pairs={{0,16},{4,20},{8,24},{12,28},{16,0},{20,4},{24,8},{28,12},{1,17},{... | collective-permute-start | bytes 393224 | tf_op jit(solution)/shard_map/ppermute | solution.py:440
  30.2 19.3 %collective-permute-start.11 = (bf16[256,512]{1,0:T(8,128)(2,1)S(1)}, bf16[256,512]{1,0:T(8,128)(2,1)S(1)}, u32[]{:S(2)}, u32[]{:S(2)}) collective-permute-start(bf16[256,512]{1,0:T(8,128)(2,1)S(1)} %finish_rows.6.refs_7_), channel_id=1, source_target_pairs={{0,2},{1,3},{2,0},{3,1},{4,6},{5,7},{6,4},{7,5},{8,10},{9,11},{10,... | collective-permute-start | bytes 786440 | tf_op jit(solution)/shard_map/ppermute | solution.py:440
  32.2 17.3 %collective-permute-start.12 = (bf16[256,512]{1,0:T(8,128)(2,1)S(1)}, bf16[256,512]{1,0:T(8,128)(2,1)S(1)}, u32[]{:S(2)}, u32[]{:S(2)}) collective-permute-start(bf16[256,512]{1,0:T(8,128)(2,1)S(1)} %finish_rows.7.refs_1_.refs_7_), channel_id=1, source_target_pairs={{0,3},{1,2},{2,1},{3,0},{4,7},{5,6},{6,5},{7,4},{8,11},{9,10},{10,... | collective-permute-start | bytes 786440 | tf_op jit(solution)/shard_map/ppermute | solution.py:440
  33.4 16.1 %collective-permute-start.15 = (bf16[256,1024]{1,0:T(8,128)(2,1)S(1)}, bf16[256,1024]{1,0:T(8,128)(2,1)S(1)}, u32[]{:S(2)}, u32[]{:S(2)}) collective-permute-start(bf16[256,1024]{1,0:T(8,128)(2,1)S(1)} %gate.8.refs_8_.refs_2_.refs_3_), channel_id=1, source_target_pairs={{0,4},{4,0},{8,12},{12,8},{16,20},{20,16},{24,28},{28,24},{1,5},{5... | collective-permute-start | bytes 1572872 | tf_op jit(solution)/shard_map/ppermute | solution.py:440
  34.3 15.2 %collective-permute-start.10 = (bf16[256,1024]{1,0:T(8,128)(2,1)S(1)}, bf16[256,1024]{1,0:T(8,128)(2,1)S(1)}, u32[]{:S(2)}, u32[]{:S(2)}) collective-permute-start(bf16[256,1024]{1,0:T(8,128)(2,1)S(1)} %gate.8.refs_8_.refs_2_.refs_3_), channel_id=1, source_target_pairs={{0,1},{1,0},{2,3},{3,2},{4,5},{5,4},{6,7},{7,6},{8,9},{9,8},{10,11... | collective-permute-start | bytes 1572872 | tf_op jit(solution)/shard_map/ppermute | solution.py:440
  36.4 13.1 %collective-permute-start.13 = (bf16[256,512]{1,0:T(8,128)(2,1)S(1)}, bf16[256,512]{1,0:T(8,128)(2,1)S(1)}, u32[]{:S(2)}, u32[]{:S(2)}) collective-permute-start(bf16[256,512]{1,0:T(8,128)(2,1)S(1)} %finish_rows.8.refs_7_), channel_id=1, source_target_pairs={{0,2},{1,3},{2,0},{3,1},{4,6},{5,7},{6,4},{7,5},{8,10},{9,11},{10,... | collective-permute-start | bytes 786440 | tf_op jit(solution)/shard_map/ppermute | solution.py:440
  49.5 2.2 %collective-permute-start.17 = (bf16[512,512]{1,0:T(8,128)(2,1)S(1)}, bf16[512,512]{1,0:T(8,128)(2,1)S(1)}, u32[]{:S(2)}, u32[]{:S(2)}) collective-permute-start(bf16[512,512]{1,0:T(8,128)(2,1)S(1)} %gate.11), channel_id=1, source_target_pairs={{0,1},{1,0},{2,3},{3,2},{4,5},{5,4},{6,7},{7,6},{8,9},{9,8},{10,11... | collective-permute-start | bytes 1572872 | tf_op jit(solution)/shard_map/ppermute | solution.py:440
  49.6 5.4 %collective-permute-start.16 = (bf16[256,1024]{1,0:T(8,128)(2,1)S(1)}, bf16[256,1024]{1,0:T(8,128)(2,1)S(1)}, u32[]{:S(2)}, u32[]{:S(2)}) collective-permute-start(bf16[256,1024]{1,0:T(8,128)(2,1)S(1)} %gate.10.refs_7_.refs_10_.refs_4_.refs_5_), channel_id=1, source_target_pairs={{0,1},{1,0},{2,3},{3,2},{4,5},{5,4},{6,7},{7,6},{8,9},{9,8},{10,11... | collective-permute-start | bytes 1572872 | tf_op jit(solution)/shard_map/ppermute | solution.py:440
  50.1 4.9 %collective-permute-start.14 = (bf16[256,1024]{1,0:T(8,128)(2,1)S(1)}, bf16[256,1024]{1,0:T(8,128)(2,1)S(1)}, u32[]{:S(2)}, u32[]{:S(2)}) collective-permute-start(bf16[256,1024]{1,0:T(8,128)(2,1)S(1)} %gate.9.refs_6_.refs_9_.refs_3_.refs_4_), channel_id=1, source_target_pairs={{0,1},{1,0},{2,3},{3,2},{4,5},{5,4},{6,7},{7,6},{8,9},{9,8},{10,11... | collective-permute-start | bytes 1572872 | tf_op jit(solution)/shard_map/ppermute | solution.py:440
  50.2 8.0 %collective-permute-start.9 = (bf16[256,512]{1,0:T(8,128)(2,1)S(1)}, bf16[256,512]{1,0:T(8,128)(2,1)S(1)}, u32[]{:S(2)}, u32[]{:S(2)}) collective-permute-start(bf16[256,512]{1,0:T(8,128)(2,1)S(1)} %finish_rows.9.refs_7_), channel_id=1, source_target_pairs={{0,3},{1,2},{2,1},{3,0},{4,7},{5,6},{6,5},{7,4},{8,11},{9,10},{10,... | collective-permute-start | bytes 786440 | tf_op jit(solution)/shard_map/ppermute | solution.py:440

commit v4 on v3

v4 whole, which is shorter than its diff:
```python
import functools

import jax
import jax.numpy as jnp
from jax import lax
from jax.experimental import pallas as pl
from jax.experimental.pallas import tpu as pltpu
from jax.sharding import PartitionSpec as P

STRETCH = 256
LANES = 128
EPSILON = 1e-06
MIB = 1024 * 1024
TILE = 512


SCALE = 5.0


def cost(us):
    return pl.CostEstimate(
        flops=int(us * SCALE * 1e9), bytes_accessed=int(us * SCALE * 3e6), transcendentals=0
    )


def call(kernel, out_shape, name, us, mib, args, after=(), anywhere_in=(), anywhere_out=(), **kw):
    vmem = pl.BlockSpec(memory_space=pltpu.VMEM)
    anywhere = pl.BlockSpec(memory_space=pl.ANY)
    n_in = len(args)

    def run(*refs):
        kernel(*refs[:n_in], *refs[n_in + len(after) :])

    return pl.pallas_call(
        run,
        in_specs=[anywhere if i in anywhere_in else vmem for i in range(n_in)]
        + [anywhere] * len(after),
        out_specs=[anywhere if i in anywhere_out else vmem for i in range(len(out_shape))],
        out_shape=out_shape,
        compiler_params=pltpu.CompilerParams(vmem_limit_bytes=mib * MIB),
        cost_estimate=cost(us),
        name=name,
        **kw,
    )(*args, *after)


def bit_count(n):
    return n.bit_length() - 1


def contract_rows(a, b):
    return lax.dot_general(a, b, (((0,), (0,)), ((), ())), preferred_element_type=jnp.float32)


def dot(a, b):
    return jnp.dot(a, b, preferred_element_type=jnp.float32)


def slice_kernel(w_ref, *refs):
    outs, sem = refs[:-1], refs[-1]
    copies = []
    for c, out in enumerate(outs):
        depth, width = out.shape
        at = lax.rem(lax.axis_index("ctx"), w_ref.shape[0] // depth) * depth
        rows, cols = pl.ds(at, depth), pl.ds(c * width, width)
        copies.append(pltpu.make_async_copy(w_ref.at[rows, cols], out, sem.at[c]))
    for copy in copies:
        copy.start()
    for copy in copies:
        copy.wait()


def slice_weight(weight, sharers):
    depth, width = weight.shape
    n = len(sharers)
    return call(
        slice_kernel,
        [jax.ShapeDtypeStruct((depth // k, width // n), weight.dtype) for k in sharers],
        "slice_weight",
        1,
        4,
        [weight],
        anywhere_in=(0,),
        scratch_shapes=[pltpu.SemaphoreType.DMA((n,))],
    )


def assemble_kernel(*refs):
    pieces, out = refs[:-1], refs[-1]
    me = lax.rem(lax.axis_index("ctx"), len(pieces))
    for i, piece in enumerate(pieces):
        depth = piece.shape[0]
        out[pl.ds(pl.multiple_of((me ^ i) * depth, depth), depth), :] = piece[...]


def assemble(pieces, after):
    depth, width = pieces[0].shape
    return call(
        assemble_kernel,
        [jax.ShapeDtypeStruct((depth * len(pieces), width), pieces[0].dtype)],
        "assemble",
        1,
        4,
        pieces,
        after,
    )[0]


def state_kernel(heads, size, count, k_ref, v_ref, level_ref, own_ref):
    for h in range(heads):
        cols = slice(h * size, (h + 1) * size)
        states = []
        for n in range(count):
            rows = pl.ds(n * STRETCH, STRETCH)
            states.append(contract_rows(k_ref[rows, cols], v_ref[rows, cols]))
        at = 0
        while len(states) > 1:
            for g in range(len(states) // 2):
                level_ref[at, h] = states[2 * g].astype(jnp.bfloat16)
                at += 1
            states = [states[2 * g] + states[2 * g + 1] for g in range(len(states) // 2)]
        own_ref[cols, :] = states[0].astype(jnp.bfloat16)


def block_states(keys, values, heads, size, after):
    count = keys.shape[0] // STRETCH
    return call(
        functools.partial(state_kernel, heads, size, count),
        [
            jax.ShapeDtypeStruct((count - 1, heads, size, size), jnp.bfloat16),
            jax.ShapeDtypeStruct((heads * size, size), jnp.bfloat16),
        ],
        "block_states",
        1,
        6,
        [keys, values],
        after,
    )


def merge_kernel(own_ref, a_ref, b_ref, c_ref, pair_ref, all_ref):
    pair = b_ref[...].astype(jnp.float32) + c_ref[...].astype(jnp.float32)
    pair_ref[...] = pair.astype(jnp.bfloat16)
    own = own_ref[...].astype(jnp.float32) + a_ref[...].astype(jnp.float32)
    all_ref[...] = (own + pair).astype(jnp.bfloat16)


def merge_states(own, near, after):
    return call(
        merge_kernel,
        [jax.ShapeDtypeStruct(own.shape, own.dtype)] * 2,
        "merge_states",
        0.2,
        2,
        [own, *near],
        after,
    )


def gate_kernel(*refs):
    pass


def gate(x, *after):
    (out,) = call(
        gate_kernel,
        [jax.ShapeDtypeStruct(x.shape, x.dtype)],
        "gate",
        0.1,
        1,
        [x],
        after,
        anywhere_in=(0,),
        anywhere_out=(0,),
        input_output_aliases={0: 0},
    )
    return out


def split_table(table_ref):
    plans, heads, levels = table_ref.shape
    lane = lax.broadcasted_iota(jnp.int32, (levels, LANES), 1)
    level = lax.broadcasted_iota(jnp.int32, (levels, LANES), 0)
    place = (lane == level).astype(jnp.float32).astype(jnp.bfloat16)
    columns = []
    for h in range(heads):
        table = table_ref[:, h, :]
        high = table.astype(jnp.bfloat16)
        rest = table - high.astype(jnp.float32)
        middle = rest.astype(jnp.bfloat16)
        low = (rest - middle.astype(jnp.float32)).astype(jnp.bfloat16)
        terms = [dot(term, place).astype(jnp.bfloat16) for term in (high, middle, low)]
        columns.append(jnp.concatenate(terms, axis=0))
    return jnp.concatenate(columns, axis=1)


def spread_weights(index_row, terms):
    plans = terms.shape[0] // 3
    plan = lax.broadcasted_iota(jnp.int32, (plans, index_row.shape[1]), 0)
    onehot = (plan == index_row).astype(jnp.float32).astype(jnp.bfloat16)
    return contract_rows(jnp.concatenate([onehot] * 3, axis=0), terms)


def local_kernel(
    heads, size, count, run, blocks, q_ref, k_ref, v_ref, index_ref, table_ref, level_ref, out_ref
):
    tiles = STRETCH // LANES
    tile_bits = bit_count(LANES)
    block_bits = bit_count(STRETCH)
    row = lax.broadcasted_iota(jnp.int32, (LANES, LANES), 0)
    col = lax.broadcasted_iota(jnp.int32, (LANES, LANES), 1)
    across = row ^ col
    level = jnp.zeros_like(row)
    for b in range(tile_bits):
        level = level + (across >= (1 << b)).astype(jnp.int32)
    level = jnp.where(col <= row, level, LANES - 1)
    for at_block, (offset, part) in enumerate(blocks):
        share = lax.axis_index("mp") ^ offset
        n = share * run + part
        block = pl.ds(pl.multiple_of(n * STRETCH, STRETCH), STRETCH)
        weights = spread_weights(index_ref[n], table_ref[...])
        for h in range(heads):
            cols = slice(h * size, (h + 1) * size)
            q = q_ref[block, cols]
            k = k_ref[block, cols]
            v = v_ref[block, cols]
            w = weights[:, h * LANES : (h + 1) * LANES]
            scores = lax.dot_general(
                q, k, (((1,), (1,)), ((), ())), preferred_element_type=jnp.float32
            )
            parts = []
            for i in range(tiles):
                rows = slice(i * LANES, (i + 1) * LANES)
                w_tile = w[rows]
                pieces = []
                for j in range(i + 1):
                    s = scores[rows, j * LANES : (j + 1) * LANES]
                    if j == i:
                        factor = jnp.take_along_axis(w_tile, level, axis=1)
                    else:
                        at = tile_bits + (i ^ j).bit_length()
                        factor = w_tile[:, at : at + 1]
                    pieces.append((s * factor).astype(jnp.bfloat16))
                weighted = pieces[0] if i == 0 else jnp.concatenate(pieces, axis=1)
                parts.append(dot(weighted, v[: (i + 1) * LANES]))
            total = jnp.concatenate(parts, axis=0)
            first = 0
            for b in range(bit_count(count)):
                at = block_bits + 1 + b
                scale = w[:, at : at + 1]
                low = bit_count(run)
                if b >= low:
                    scale = scale * ((share >> (b - low)) & 1).astype(jnp.float32)
                if b >= low or (part >> b) & 1:
                    total = total + dot(q, level_ref[first + (n >> (b + 1)), h]) * scale
                first += count >> (b + 1)
            out_ref[at_block * STRETCH : (at_block + 1) * STRETCH, cols] = total.astype(out_ref.dtype)


def first_kernel(kernel, w_ref, q_ref, k_ref, v_ref, index_ref, table_ref, level_ref, *refs):
    out_ref, copy_ref, terms_ref, sem = refs
    copy = pltpu.make_async_copy(w_ref, copy_ref, sem)
    copy.start()
    terms_ref[...] = split_table(table_ref)
    kernel(q_ref, k_ref, v_ref, index_ref, terms_ref, level_ref, out_ref)
    copy.wait()


def local_attention(args, parts, blocks, weight=None, after=()):
    queries, levels = args[0], args[-1]
    tokens, width = queries.shape
    count = tokens // STRETCH
    heads, size = levels.shape[1], levels.shape[3]
    kernel = functools.partial(local_kernel, heads, size, count, parts, blocks)
    out_shape = [jax.ShapeDtypeStruct((len(blocks) * STRETCH, width), jnp.bfloat16)]
    if weight is not None:
        return call(
            functools.partial(first_kernel, kernel),
            out_shape
            + [
                jax.ShapeDtypeStruct(weight.shape, weight.dtype),
                jax.ShapeDtypeStruct((3 * args[4].shape[0], heads * LANES), jnp.bfloat16),
            ],
            "local_attention",
            len(blocks),
            8,
            [weight, *args],
            after,
            anywhere_in=(0,),
            scratch_shapes=[pltpu.SemaphoreType.DMA],
        )
    return call(kernel, out_shape, "local_attention", len(blocks), 8, args, after)[0]


def finish_kernel(
    heads, size, first, remotes, offset, part, parts, blocks, row, q_ref, local_ref, index_ref, table_ref, *refs
):
    state_refs, out_ref = refs[:remotes], refs[remotes]
    start = (lax.axis_index("mp") ^ offset) * parts + part
    position = lax.axis_index("ctx")
    for i in range(blocks):
        block = pl.ds(pl.multiple_of((start + i) * STRETCH, STRETCH), STRETCH)
        weights = spread_weights(index_ref[start + i], table_ref[...])
        for h in range(heads):
            cols = slice(h * size, (h + 1) * size)
            q = q_ref[block, cols]
            w = weights[:, h * LANES : (h + 1) * LANES]
            total = local_ref[(row + i) * STRETCH : (row + i + 1) * STRETCH, cols].astype(jnp.float32)
            for b in range(remotes):
                inside = ((position >> b) & 1).astype(jnp.float32)
                reached = dot(q, state_refs[b][cols, :])
                total = total + reached * (w[:, first + b : first + b + 1] * inside)
            scale = lax.rsqrt(jnp.mean(total * total, axis=1, keepdims=True) + EPSILON)
            out_ref[i * STRETCH : (i + 1) * STRETCH, cols] = (total * scale).astype(out_ref.dtype)


def finish_rows(after, offset, part, blocks, row, queries, local, index_rows, table, states, first):
    tokens, width = queries.shape
    size = states[0].shape[1]
    heads = width // size
    parts = tokens // STRETCH // lax.axis_size("mp")
    (out,) = call(
        functools.partial(
            finish_kernel, heads, size, first, len(states), offset, part, parts, blocks, row
        ),
        [jax.ShapeDtypeStruct((blocks * STRETCH, width), jnp.bfloat16)],
        "finish_rows",
        blocks,
        4,
        [queries, local, index_rows, table, *states],
        after,
    )
    return out


def split_refs(groups, refs):
    refs = list(refs)
    a_refs = [refs.pop(0) for _ in groups]
    w_refs = [[[refs.pop(0) for _ in chunk] for chunk in g] for g in groups]
    return a_refs, w_refs, refs


def products(groups, a_refs, w_refs, cols, columns, part):
    total = None
    mine = lax.axis_index("ctx")
    for g, a_ref, chunks in zip(groups, a_refs, w_refs):
        rows = slice(part * STRETCH, (part + 1) * STRETCH) if a_ref.shape[0] > STRETCH else slice(None)
        width = columns // len(chunks)
        for place, ref in zip(g[cols // width], chunks[cols // width]):
            depth = ref.shape[0]
            if depth == a_ref.shape[1]:
                a = a_ref[rows, :]
            else:
                at = lax.rem(mine, a_ref.shape[1] // depth) ^ place
                a = a_ref[rows, pl.ds(pl.multiple_of(at * depth, depth), depth)]
            piece = dot(a, ref[:, cols % width : cols % width + TILE])
            total = piece if total is None else total + piece
    return total


def start_kernel(groups, *refs):
    a_refs, w_refs, outs = split_refs(groups, refs)
    columns = outs[0].shape[1]
    for part, out in enumerate(outs):
        for cols in range(0, columns, TILE):
            out[:, cols : cols + TILE] = products(groups, a_refs, w_refs, cols, columns, part)


def add_kernel(groups, part, *refs):
    a_refs, w_refs, (before, out) = split_refs(groups, refs)
    columns = out.shape[1]
    for cols in range(0, columns, TILE):
        tile = slice(cols, cols + TILE)
        out[:, tile] = before[:, tile] + products(groups, a_refs, w_refs, cols, columns, part)


def last_kernel(groups, part, *refs):
    a_refs, w_refs, rest = split_refs(groups, refs)
    before, (out, tile_ref, sem) = rest[0], rest[-3:]
    columns = out.shape[1]
    copies = []
    for i, cols in enumerate(range(0, columns, TILE)):
        total = before[:, cols : cols + TILE] + products(groups, a_refs, w_refs, cols, columns, part)
        tile_ref[i] = total.astype(tile_ref.dtype)
        to = out.at[pl.ds(part * STRETCH, STRETCH), pl.ds(cols, TILE)]
        copies.append(pltpu.make_async_copy(tile_ref.at[i], to, sem.at[i]))
        copies[-1].start()
    for copy in copies:
        copy.wait()


def operands(pairs):
    groups = [[[place for place, _ in chunk] for chunk in g] for _, g in pairs]
    return groups, [a for a, _ in pairs] + [w for _, g in pairs for chunk in g for _, w in chunk]


def project_start(pairs, parts, columns, after):
    groups, arrays = operands(pairs)
    return call(
        functools.partial(start_kernel, groups),
        [jax.ShapeDtypeStruct((STRETCH, columns), jnp.float32)] * parts,
        "project_start",
        2.4,
        6,
        arrays,
        after,
    )


def project_add(pairs, before, part):
    groups, arrays = operands(pairs)
    return call(
        functools.partial(add_kernel, groups, part),
        [jax.ShapeDtypeStruct(before.shape, before.dtype)],
        "project_add",
        1,
        6,
        [*arrays, before],
        input_output_aliases={len(arrays): 0},
    )[0]


def project_last(pairs, before, out, part, parts):
    groups, arrays = operands(pairs)
    columns = before.shape[1]
    extra = [] if out is None else [out]
    return call(
        functools.partial(last_kernel, groups, part),
        [jax.ShapeDtypeStruct((parts * STRETCH, columns), jnp.bfloat16)],
        "project_last",
        1.5,
        8,
        [*arrays, before, *extra],
        anywhere_in=(len(arrays) + 1,),
        anywhere_out=(0,),
        input_output_aliases={len(arrays) + 1: 0} if extra else {},
        scratch_shapes=[
            pltpu.VMEM((columns // TILE, STRETCH, TILE), jnp.bfloat16),
            pltpu.SemaphoreType.DMA((columns // TILE,)),
        ],
    )[0]


def flip(x, axis, bits):
    n = lax.axis_size(axis)
    return lax.ppermute(x, axis, [(i, i ^ bits) for i in range(n)])


def add_rounded(*arrays):
    total = arrays[0].astype(jnp.float32)
    for a in arrays[1:]:
        total = total + a.astype(jnp.float32)
    return total.astype(jnp.bfloat16)


def body(queries, key_vectors, value_vectors, level_index, level_table, out_weight):
    tokens, width = queries.shape
    heads = level_table.shape[1]
    size = width // heads
    ctx_size, mp_size = lax.axis_size("ctx"), lax.axis_size("mp")
    ctx_bits = bit_count(ctx_size)
    count = tokens // STRETCH
    columns = out_weight.shape[1]
    first = bit_count(STRETCH) + 1 + bit_count(count)

    index_rows = level_index.reshape(count, 1, STRETCH)

    portions = slice_weight(out_weight, [min(2, ctx_size), min(4, ctx_size)])
    evens = list(range(2, mp_size, 2))
    got = {j: [flip(p, "mp", j) for p in portions] for j in evens}

    levels, own = block_states(key_vectors, value_vectors, heads, size, portions)
    near = [flip(own, "ctx", b) for b in range(1, min(4, ctx_size))]

    parts = tokens // mp_size // STRETCH
    far_groups = list(range(2, mp_size))
    far_blocks = [(j, part) for j in far_groups for part in range(parts)]
    own_blocks, mate_blocks = [[(j, part) for part in range(parts)] for j in range(2)]
    args = [queries, key_vectors, value_vectors, index_rows, level_table, levels]
    local, weight, terms = local_attention(args, parts, far_blocks, weight=out_weight, after=[own])
    args[4] = terms

    remote = near[:1]
    ready = near[0] if near else local
    if ctx_bits > 1:
        pair, running = merge_states(own, near, [local])
        remote.append(pair)
        ready = running
    far = None
    for b in range(2, ctx_bits):
        if b > 2:
            running = add_rounded(running, far)
        far = flip(running, "ctx", 1 << b)
        remote.append(far)

    there, over_pair, there_pair = {}, {}, {}
    held = [gate(got[j][0], ready) for j in evens]
    for j, x in zip(evens, held):
        got[j][0] = x
        over_pair[j] = flip(x, "mp", 1)
        if ctx_size > 1:
            there[j] = flip(x, "ctx", 1)
    weight = gate(weight, ready, *held)
    mate = flip(weight, "mp", 1)
    close = local_attention(args, parts, own_blocks, after=[ready, weight] + held)
    done = [close]

    def finished(j, part, blocks, local, places):
        nonlocal done
        out = finish_rows(
            done, j, part, blocks, places.index((j, part)), queries, local, index_rows, terms,
            remote, first,
        )
        done = [out]
        return out

    received = {}
    for j in far_groups[:-1]:
        received[j] = [flip(finished(j, 0, parts, local, far_blocks), "mp", j)] * parts
    done += [mate] + list(over_pair.values())
    last = far_groups[-1]
    received[last] = [
        flip(finished(last, part, 1, local, far_blocks), "mp", last) for part in range(parts - 1)
    ]
    beside = local_attention(args, parts, mate_blocks, after=done)
    done = [beside] + list(there.values())
    pieces = {}
    for j in evens:
        x = gate(got[j][1], *done)
        pieces[j] = [x] + [flip(x, "ctx", b) for b in range(1, min(4, ctx_size))]
        done.append(x)

    final = finished(last, parts - 1, 1, local, far_blocks)
    theirs = finished(1, 0, parts, beside, mate_blocks)
    mine = finished(0, 0, parts, close, own_blocks)

    over = done + [x for xs in received.values() for x in xs]
    for j in evens:
        pieces[j] = assemble(pieces[j], over)
        over.append(pieces[j])
    received[last].append(flip(gate(final, *over), "mp", last))
    theirs = flip(gate(theirs, *over), "mp", 1)
    gathered = {}
    for j in evens:
        gathered[j] = [[(0, got[j][0])], [(0, pieces[j])]]
        gathered[j + 1] = [[(0, over_pair[j])], [(0, flip(pieces[j], "mp", 1))]]
        if there:
            x = gate(there[j], *over)
            gathered[j][0].append((1, x))
            gathered[j + 1][0].append((1, flip(x, "mp", 1)))

    early = [(mine, [[(0, weight)]])]
    early += [(received[j][0], gathered[j]) for j in far_groups[:-1] if j % 2 == 0]
    late = [(j, gathered[j]) for j in far_groups[:-1] if j % 2]
    totals = project_start(early, parts, columns, over)
    out = None
    for part in range(parts):
        total = totals[part]
        pairs = [(theirs, [[(0, mate)]])]
        pairs += [(received[j][part], w) for j, w in late + [(last, gathered[last])]]
        if part + 1 == parts:
            total = project_add(pairs[:-1], total, part)
            pairs = pairs[-1:]
        out = project_last(pairs, total, out, part, parts)
    return out


def solution(mesh):
    placed = (
        P("ctx", "mp"),
        P("ctx", "mp"),
        P("ctx", "mp"),
        P("ctx"),
        P(None, "mp", None),
        P("mp", None),
    )
    return jax.shard_map(
        body, mesh=mesh, in_specs=placed, out_specs=P(("ctx", "mp"), None), check_vma=False
    )
```

time: 60 us -> 58.7 us (0.978)
  local copies, waits for them, and re-layouts: 4.97 us -> 1.62 us
  waiting for transfers between devices: 10.7 us -> 12.3 us
  Pallas kernels: 25 us -> 26.1 us
  starting transfers between devices: 18.8 us -> 18.2 us
    unnamed x17 -> x14, local copies, waits for them, and re-layouts: 4.97 us -> 1.62 us
    ppermute x18, waiting for transfers between devices: 10.7 us -> 12.3 us  [flip(): return lax.ppermute(x, axis, [(i, i ^ bits) for i in range(n)])]
    pallas_call x20 -> x22, Pallas kernels: 24.9 us -> 26.1 us  [call(): pl.pallas_call(run, in_specs=[anywhere if i in anywhere_in else vmem for...]
    ppermute x18, starting transfers between devices: 18.8 us -> 18.2 us  [flip(): return lax.ppermute(x, axis, [(i, i ^ bits) for i in range(n)])]
  transfers between devices with their start and end apart: 18 -> 18, of which waited for: 6 -> 7; matrix products, arithmetic and copies ran while one was open for 0% -> 0% of each run, Pallas kernels for 39% -> 42%
where the time goes in v4:
time: 58.7 us; the launch traced here: 58.6 us
  Pallas kernels  26.1 us (44%)
  starting transfers between devices  18.2 us (31%)
  waiting for transfers between devices  12.3 us (21%)
  local copies, waits for them, and re-layouts  1.62 us (3%)
    pallas_call x22, Pallas kernels, call(): pl.pallas_call(run, in_specs=[anywhere if i in anywhere_in else vmem for...  26.1 us
    ppermute x18, starting transfers between devices, flip(): return lax.ppermute(x, axis, [(i, i ^ bits) for i in range(n)])  18.2 us
    ppermute x18, waiting for transfers between devices, flip(): return lax.ppermute(x, axis, [(i, i ^ bits) for i in range(n)])  12.3 us
    unnamed x14, local copies, waits for them, and re-layouts  1.62 us
  transfers between devices with their start and end apart: 18, of which 7 were waited for; matrix products, arithmetic and copies ran while one was open for 0% of the time, Pallas kernels for 42%

profile of v4, /device:TPU:0, one launch (start us, length us, event | category | flops | bytes accessed | tf_op | source)
XLA Modules:
  0.0 58.6 jit_solution(6561774592928062586)
XLA Ops:
  0.0 0.0 copy-start
  0.0 1.6 %copy-done = bf16[512,2048]{1,0:T(8,128)(2,1)S(1)} copy-done((bf16[512,2048]{1,0:T(8,128)(2,1)S(1)}, bf16[512,2048]{1,0:T(8,128)(2,1)}, u32[]{:S(2)}) %copy-start) | copy-done | bytes 2097176
  1.6 0.0 copy-start.2
  1.6 0.0 copy-start.3
  1.6 0.1 slice_weight.1
  1.7 3.0 %collective-permute-start.4 = (bf16[256,1024]{1,0:T(8,128)(2,1)S(1)}, bf16[256,1024]{1,0:T(8,128)(2,1)S(1)}, u32[]{:S(2)}, u32[]{:S(2)}) collective-permute-start(bf16[256,1024]{1,0:T(8,128)(2,1)S(1)} %get-tuple-element.16.refs_2_), channel_id=1, source_target_pairs={{0,2},{1,3},{2,0},{3,1},{4,6},{5,7},{6,4},{7,5},{8,10},{9,11},{10,... | collective-permute-start | bytes 1572872 | tf_op jit(solution)/shard_map/ppermute | solution.py:446
  4.7 0.0 copy-done.2
  4.7 0.0 copy-done.3
  4.7 0.0 copy-start.5
  4.7 0.0 copy-start.6
  4.7 0.8 %block_states.1 = (bf16[7,4,128,128]{3,2,1,0:T(8,128)(2,1)S(1)}, bf16[512,128]{1,0:T(8,128)(2,1)S(1)}) custom-call(bf16[2048,512]{1,0:T(8,128)(2,1)S(1)} %copy-done.2, bf16[2048,512]{1,0:T(8,128)(2,1)S(1)} %copy-done.3, bf16[256,1024]{1,0:T(8,128)(2,1)S(1)} %get-tuple-element.16.refs_2_, bf16[128,1024]{1,0:T(8,128)(2,1)S(1)} %get-tuple-element.17.refs_3_), custom_call_target="tpu_custom_call" | custom-call | flops 5000000000 | bytes 15000000 | tf_op jit(solution)/shard_map/block_states/pallas_call | solution.py:34
  5.5 3.2 %collective-permute-start.2 = (bf16[512,128]{1,0:T(8,128)(2,1)S(1)}, bf16[512,128]{1,0:T(8,128)(2,1)S(1)}, u32[]{:S(2)}, u32[]{:S(2)}) collective-permute-start(bf16[512,128]{1,0:T(8,128)(2,1)S(1)} %get-tuple-element.19.refs_7_.refs_0_), channel_id=1, source_target_pairs={{0,12},{4,8},{8,4},{12,0},{16,28},{20,24},{24,20},{28,16},{1,13},{... | collective-permute-start | bytes 393224 | tf_op jit(solution)/shard_map/ppermute | solution.py:446
  8.7 0.5 collective-permute-start.1
  9.1 0.2 collective-permute-start
  9.3 0.0 copy-done.1
  9.3 0.0 copy-done.4
  9.3 0.0 copy-done.5
  9.3 0.0 copy-done.6
  9.3 5.1 %local_attention.3 = (bf16[1024,512]{1,0:T(8,128)(2,1)S(1)}, bf16[512,2048]{1,0:T(8,128)(2,1)S(1)}, bf16[48,512]{1,0:T(8,128)(2,1)S(1)}) custom-call(bf16[512,2048]{1,0:T(8,128)(2,1)S(1)} %copy-done.1, bf16[2048,512]{1,0:T(8,128)(2,1)S(1)} %copy-done.4, bf16[2048,512]{1,0:T(8,128)(2,1)S(1)} %copy-done.2, bf16[2048,512]{1,0:T(8,128)(2,1)S(1)} %copy-done.3, ...), custom_call_target="tpu_custom_call" | custom-call | flops 20000000000 | bytes 60000000 | tf_op jit(solution)/shard_map/local_attention/pallas_call | solution.py:34
  14.4 0.0 collective-permute-done.2.refs_3_
  14.4 0.7 %collective-permute-done.1.refs_2_ = bf16[512,128]{1,0:T(8,128)(2,1)S(1)} collective-permute-done((bf16[512,128]{1,0:T(8,128)(2,1)S(1)}, bf16[512,128]{1,0:T(8,128)(2,1)S(1)}, u32[]{:S(2)}, u32[]{:S(2)}) %collective-permute-start.1) | collective-permute-done | bytes 131104 | tf_op jit(solution)/shard_map/ppermute | solution.py:446
  15.1 0.0 collective-permute-done.refs_1_.refs_4_
  15.1 0.1 merge_states.1
  15.2 1.4 %collective-permute-done.4.refs_0_ = bf16[256,1024]{1,0:T(8,128)(2,1)S(1)} collective-permute-done((bf16[256,1024]{1,0:T(8,128)(2,1)S(1)}, bf16[256,1024]{1,0:T(8,128)(2,1)S(1)}, u32[]{:S(2)}, u32[]{:S(2)}) %collective-permute-start.4) | collective-permute-done | bytes 524320 | tf_op jit(solution)/shard_map/ppermute | solution.py:446
  16.6 0.0 collective-permute-start.5
  16.6 1.7 %collective-permute-start.8 = (bf16[128,1024]{1,0:T(8,128)(2,1)S(1)}, bf16[128,1024]{1,0:T(8,128)(2,1)S(1)}, u32[]{:S(2)}, u32[]{:S(2)}) collective-permute-start(bf16[128,1024]{1,0:T(8,128)(2,1)S(1)} %get-tuple-element.17.refs_3_), channel_id=1, source_target_pairs={{0,2},{1,3},{2,0},{3,1},{4,6},{5,7},{6,4},{7,5},{8,10},{9,11},{10,... | collective-permute-start | bytes 786440 | tf_op jit(solution)/shard_map/ppermute | solution.py:446
  18.4 2.6 %collective-permute-start.3 = (bf16[512,128]{1,0:T(8,128)(2,1)S(1)}, bf16[512,128]{1,0:T(8,128)(2,1)S(1)}, u32[]{:S(2)}, u32[]{:S(2)}) collective-permute-start(bf16[512,128]{1,0:T(8,128)(2,1)S(1)} %get-tuple-element.23.refs_1_.refs_6_), channel_id=1, source_target_pairs={{0,16},{4,20},{8,24},{12,28},{16,0},{20,4},{24,8},{28,12},{1,17},{... | collective-permute-start | bytes 393224 | tf_op jit(solution)/shard_map/ppermute | solution.py:446
  20.9 1.5 %collective-permute-start.7 = (bf16[256,1024]{1,0:T(8,128)(2,1)S(1)}, bf16[256,1024]{1,0:T(8,128)(2,1)S(1)}, u32[]{:S(2)}, u32[]{:S(2)}) collective-permute-start(bf16[256,1024]{1,0:T(8,128)(2,1)S(1)} %gate.6.refs_2_.refs_8_.refs_3_), channel_id=1, source_target_pairs={{0,4},{4,0},{8,12},{12,8},{16,20},{20,16},{24,28},{28,24},{1,5},{5... | collective-permute-start | bytes 1572872 | tf_op jit(solution)/shard_map/ppermute | solution.py:446
  22.5 0.0 collective-permute-start.6
  22.5 2.2 %local_attention.4.refs_7_.refs_1_ = bf16[512,512]{1,0:T(8,128)(2,1)S(1)} custom-call(bf16[2048,512]{1,0:T(8,128)(2,1)S(1)} %copy-done.4, bf16[2048,512]{1,0:T(8,128)(2,1)S(1)} %copy-done.2, bf16[2048,512]{1,0:T(8,128)(2,1)S(1)} %copy-done.3, s32[8,1,256]{2,1,0:T(1,128)S(1)} %bitcast.2, bf16[48,512]{1,0:T(8,128)(2,1)S(1)} %get-tuple-element.21.refs_4_.refs_3_, ...), custom_call_target="tpu_custom_call" | custom-call | flops 10000000000 | bytes 30000000 | tf_op jit(solution)/shard_map/local_attention/pallas_call | solution.py:34
  24.7 3.0 %collective-permute-done.3.refs_6_ = bf16[512,128]{1,0:T(8,128)(2,1)S(1)} collective-permute-done((bf16[512,128]{1,0:T(8,128)(2,1)S(1)}, bf16[512,128]{1,0:T(8,128)(2,1)S(1)}, u32[]{:S(2)}, u32[]{:S(2)}) %collective-permute-start.3) | collective-permute-done | bytes 131104 | tf_op jit(solution)/shard_map/ppermute | solution.py:446
  27.7 2.3 %finish_rows.5.refs_7_ = bf16[512,512]{1,0:T(8,128)(2,1)S(1)} custom-call(bf16[2048,512]{1,0:T(8,128)(2,1)S(1)} %copy-done.4, bf16[1024,512]{1,0:T(8,128)(2,1)S(1)} %get-tuple-element.20.refs_4_.refs_1_, s32[8,1,256]{2,1,0:T(1,128)S(1)} %bitcast.3, bf16[48,512]{1,0:T(8,128)(2,1)S(1)} %get-tuple-element.21.refs_4_.refs_3_, ...), custom_call_target="tpu_custom_call" | custom-call | flops 10000000000 | bytes 30000000 | tf_op jit(solution)/shard_map/finish_rows/pallas_call | solution.py:34
  30.0 0.5 collective-permute-start.9
  30.5 0.0 collective-permute-done.6.refs_9_.refs_3_.refs_1_
  30.5 0.0 collective-permute-done.5.refs_8_.refs_1_.refs_2_
  30.5 1.0 %finish_rows.6.refs_6_ = bf16[256,512]{1,0:T(8,128)(2,1)S(1)} custom-call(bf16[2048,512]{1,0:T(8,128)(2,1)S(1)} %copy-done.4, bf16[1024,512]{1,0:T(8,128)(2,1)S(1)} %get-tuple-element.20.refs_4_.refs_1_, s32[8,1,256]{2,1,0:T(1,128)S(1)} %bitcast.4, bf16[48,512]{1,0:T(8,128)(2,1)S(1)} %get-tuple-element.21.refs_4_.refs_3_, ...), custom_call_target="tpu_custom_call" | custom-call | flops 5000000000 | bytes 15000000 | tf_op jit(solution)/shard_map/finish_rows/pallas_call | solution.py:34
  31.6 2.2 %local_attention.5.refs_1_.refs_7_ = bf16[512,512]{1,0:T(8,128)(2,1)S(1)} custom-call(bf16[2048,512]{1,0:T(8,128)(2,1)S(1)} %copy-done.4, bf16[2048,512]{1,0:T(8,128)(2,1)S(1)} %copy-done.2, bf16[2048,512]{1,0:T(8,128)(2,1)S(1)} %copy-done.3, s32[8,1,256]{2,1,0:T(1,128)S(1)} %bitcast.5, bf16[48,512]{1,0:T(8,128)(2,1)S(1)} %get-tuple-element.21.refs_4_.refs_3_, ...), custom_call_target="tpu_custom_call" | custom-call | flops 10000000000 | bytes 30000000 | tf_op jit(solution)/shard_map/local_attention/pallas_call | solution.py:34
  33.8 0.0 collective-permute-done.8.refs_0_
  33.8 0.9 %collective-permute-done.7.refs_2_.refs_8_.refs_0_ = bf16[256,1024]{1,0:T(8,128)(2,1)S(1)} collective-permute-done((bf16[256,1024]{1,0:T(8,128)(2,1)S(1)}, bf16[256,1024]{1,0:T(8,128)(2,1)S(1)}, u32[]{:S(2)}, u32[]{:S(2)}) %collective-permute-start.7) | collective-permute-done | bytes 524320 | tf_op jit(solution)/shard_map/ppermute | solution.py:446
  34.7 2.5 %collective-permute-start.13 = (bf16[128,1024]{1,0:T(8,128)(2,1)S(1)}, bf16[128,1024]{1,0:T(8,128)(2,1)S(1)}, u32[]{:S(2)}, u32[]{:S(2)}) collective-permute-start(bf16[128,1024]{1,0:T(8,128)(2,1)S(1)} %gate.8.refs_9_.refs_0_), channel_id=1, source_target_pairs={{0,12},{4,8},{8,4},{12,0},{16,28},{20,24},{24,20},{28,16},{1,13},{... | collective-permute-start | bytes 786440 | tf_op jit(solution)/shard_map/ppermute | solution.py:446
  37.3 0.5 collective-permute-start.12
  37.7 0.5 collective-permute-start.11
  38.2 0.0 collective-permute-start.10
  38.2 1.0 %finish_rows.7.refs_7_.refs_0_ = bf16[256,512]{1,0:T(8,128)(2,1)S(1)} custom-call(bf16[2048,512]{1,0:T(8,128)(2,1)S(1)} %copy-done.4, bf16[1024,512]{1,0:T(8,128)(2,1)S(1)} %get-tuple-element.20.refs_4_.refs_1_, s32[8,1,256]{2,1,0:T(1,128)S(1)} %bitcast.6, bf16[48,512]{1,0:T(8,128)(2,1)S(1)} %get-tuple-element.21.refs_4_.refs_3_, ...), custom_call_target="tpu_custom_call" | custom-call | flops 5000000000 | bytes 15000000 | tf_op jit(solution)/shard_map/finish_rows/pallas_call | solution.py:34
  39.3 2.3 %finish_rows.8.refs_7_.refs_0_ = bf16[512,512]{1,0:T(8,128)(2,1)S(1)} custom-call(bf16[2048,512]{1,0:T(8,128)(2,1)S(1)} %copy-done.4, bf16[512,512]{1,0:T(8,128)(2,1)S(1)} %local_attention.5.refs_1_.refs_7_, s32[8,1,256]{2,1,0:T(1,128)S(1)} %bitcast.7, bf16[48,512]{1,0:T(8,128)(2,1)S(1)} %get-tuple-element.21.refs_4_.refs_3_, ...), custom_call_target="tpu_custom_call" | custom-call | flops 10000000000 | bytes 30000000 | tf_op jit(solution)/shard_map/finish_rows/pallas_call | solution.py:34
  41.5 2.3 %finish_rows.9.refs_4_.refs_1_.refs_0_.refs_6_ = bf16[512,512]{1,0:T(8,128)(2,1)S(1)} custom-call(bf16[2048,512]{1,0:T(8,128)(2,1)S(1)} %copy-done.4, bf16[512,512]{1,0:T(8,128)(2,1)S(1)} %local_attention.4.refs_7_.refs_1_, s32[8,1,256]{2,1,0:T(1,128)S(1)} %bitcast.8, bf16[48,512]{1,0:T(8,128)(2,1)S(1)} %get-tuple-element.21.refs_4_.refs_3_, ...), custom_call_target="tpu_custom_call" | custom-call | flops 10000000000 | bytes 30000000 | tf_op jit(solution)/shard_map/finish_rows/pallas_call | solution.py:34
  43.8 1.1 %collective-permute-done.9.refs_5_.refs_6_.refs_2_.refs_3_.refs_1_.refs_7_.refs_8_ = bf16[512,512]{1,0:T(8,128)(2,1)S(1)} collective-permute-done((bf16[512,512]{1,0:T(8,128)(2,1)S(1)}, bf16[512,512]{1,0:T(8,128)(2,1)S(1)}, u32[]{:S(2)}, u32[]{:S(2)}) %collective-permute-start.9) | collective-permute-done | bytes 524320 | tf_op jit(solution)/shard_map/ppermute | solution.py:446
  44.9 0.0 collective-permute-done.13.refs_3_
  44.9 3.7 %collective-permute-done.12.refs_2_ = bf16[128,1024]{1,0:T(8,128)(2,1)S(1)} collective-permute-done((bf16[128,1024]{1,0:T(8,128)(2,1)S(1)}, bf16[128,1024]{1,0:T(8,128)(2,1)S(1)}, u32[]{:S(2)}, u32[]{:S(2)}) %collective-permute-start.12) | collective-permute-done | bytes 262176 | tf_op jit(solution)/shard_map/ppermute | solution.py:446
  48.6 0.0 collective-permute-done.11.refs_1_
  48.6 0.0 collective-permute-done.10.refs_7_.refs_4_.refs_9_.refs_1_
  48.6 0.1 assemble.1.refs_5_.refs_10_
  48.7 0.2 collective-permute-start.16
  48.9 0.8 %collective-permute-start.14 = (bf16[256,512]{1,0:T(8,128)(2,1)S(1)}, bf16[256,512]{1,0:T(8,128)(2,1)S(1)}, u32[]{:S(2)}, u32[]{:S(2)}) collective-permute-start(bf16[256,512]{1,0:T(8,128)(2,1)S(1)} %gate.9), channel_id=1, source_target_pairs={{0,3},{1,2},{2,1},{3,0},{4,7},{5,6},{6,5},{7,4},{8,11},{9,10},{10,... | collective-permute-start | bytes 786440 | tf_op jit(solution)/shard_map/ppermute | solution.py:446
  49.7 0.1 collective-permute-start.17
  49.8 0.4 collective-permute-start.15
  50.2 2.3 %project_start.1 = (f32[256,2048]{1,0:T(8,128)S(1)}, f32[256,2048]{1,0:T(8,128)S(1)}) custom-call(bf16[512,512]{1,0:T(8,128)(2,1)S(1)} %finish_rows.9.refs_4_.refs_1_.refs_0_.refs_6_, bf16[512,512]{1,0:T(8,128)(2,1)S(1)} %collective-permute-done.9.refs_5_.refs_6_.refs_2_.refs_3_.refs_1_.refs_7_.refs_8_, bf16[512,2048]{1,0:T(8,128)(2,1)S(1)} %gate.7.refs_7_.refs_2_, ...), custom_call_target="tpu_custom_call" | custom-call | flops 12000000000 | bytes 36000000 | tf_op jit(solution)/shard_map/project_start/pallas_call | solution.py:34
  52.6 0.0 collective-permute-done.17.refs_0_
  52.6 0.9 %project_add.1.refs_4_ = f32[256,2048]{1,0:T(8,128)S(1)} custom-call(bf16[512,512]{1,0:T(8,128)(2,1)S(1)} %collective-permute-done.17.refs_0_, bf16[512,2048]{1,0:T(8,128)(2,1)S(1)} %collective-permute-done.5.refs_8_.refs_1_.refs_2_, f32[256,2048]{1,0:T(8,128)S(1)} %get-tuple-element.25.refs_2_), custom_call_target="tpu_custom_call", output_to_operand_aliasing={{}: (2, {})} | custom-call | flops 5000000000 | bytes 15000000 | tf_op jit(solution)/shard_map/project_add/pallas_call | solution.py:34
  53.4 0.0 collective-permute-done.15.refs_4_.refs_2_
  53.5 0.0 collective-permute-done.16.refs_5_.refs_3_
  53.5 2.0 %project_last.2.refs_5_ = bf16[512,2048]{1,0:T(8,128)(2,1)} custom-call(bf16[512,512]{1,0:T(8,128)(2,1)S(1)} %collective-permute-done.17.refs_0_, bf16[256,512]{1,0:T(8,128)(2,1)S(1)} %collective-permute-done.10.refs_7_.refs_4_.refs_9_.refs_1_, bf16[512,2048]{1,0:T(8,128)(2,1)S(1)} %collective-permute-done.5.refs_8_.refs_1_.refs_2_, ...), custom_call_target="tpu_custom_call" | custom-call | flops 7500000256 | bytes 22500000 | tf_op jit(solution)/shard_map/project_last/pallas_call | solution.py:34
  55.5 1.5 %collective-permute-done.14.refs_0_ = bf16[256,512]{1,0:T(8,128)(2,1)S(1)} collective-permute-done((bf16[256,512]{1,0:T(8,128)(2,1)S(1)}, bf16[256,512]{1,0:T(8,128)(2,1)S(1)}, u32[]{:S(2)}, u32[]{:S(2)}) %collective-permute-start.14) | collective-permute-done | bytes 262176 | tf_op jit(solution)/shard_map/ppermute | solution.py:446
  57.0 1.5 %project_last.3 = bf16[512,2048]{1,0:T(8,128)(2,1)} custom-call(bf16[256,512]{1,0:T(8,128)(2,1)S(1)} %collective-permute-done.14.refs_0_, bf16[256,1024]{1,0:T(8,128)(2,1)S(1)} %collective-permute-done.6.refs_9_.refs_3_.refs_1_, bf16[256,1024]{1,0:T(8,128)(2,1)S(1)} %collective-permute-done.15.refs_4_.refs_2_, ...), custom_call_target="tpu_custom_call", output_to_operand_aliasing={{}: (5, {})} | custom-call | flops 7500000256 | bytes 22500000 | tf_op jit(solution)/shard_map/project_last/pallas_call | solution.py:34
  (8 shorter events, 0.0 us)
Async XLA Ops:
  0.0 1.6 %copy-start = (bf16[512,2048]{1,0:T(8,128)(2,1)S(1)}, bf16[512,2048]{1,0:T(8,128)(2,1)}, u32[]{:S(2)}) copy-start(bf16[512,2048]{1,0:T(8,128)(2,1)} %refs_0_.12) | copy-start | bytes 6291460
  1.6 3.1 %copy-start.2 = (bf16[2048,512]{1,0:T(8,128)(2,1)S(1)}, bf16[2048,512]{1,0:T(8,128)(2,1)}, u32[]{:S(2)}) copy-start(bf16[2048,512]{1,0:T(8,128)(2,1)} %refs_1_.7) | copy-start | bytes 6291460
  1.6 3.1 %copy-start.3 = (bf16[2048,512]{1,0:T(8,128)(2,1)S(1)}, bf16[2048,512]{1,0:T(8,128)(2,1)}, u32[]{:S(2)}) copy-start(bf16[2048,512]{1,0:T(8,128)(2,1)} %refs_2_.5) | copy-start | bytes 6291460
  1.7 14.9 %collective-permute-start.4 = (bf16[256,1024]{1,0:T(8,128)(2,1)S(1)}, bf16[256,1024]{1,0:T(8,128)(2,1)S(1)}, u32[]{:S(2)}, u32[]{:S(2)}) collective-permute-start(bf16[256,1024]{1,0:T(8,128)(2,1)S(1)} %get-tuple-element.16.refs_2_), channel_id=1, source_target_pairs={{0,2},{1,3},{2,0},{3,1},{4,6},{5,7},{6,4},{7,5},{8,10},{9,11},{10,... | collective-permute-start | bytes 1572872 | tf_op jit(solution)/shard_map/ppermute | solution.py:446
  4.7 4.6 %copy-start.1 = (bf16[512,2048]{1,0:T(8,128)(2,1)S(1)}, bf16[512,2048]{1,0:T(8,128)(2,1)}, u32[]{:S(2)}) copy-start(bf16[512,2048]{1,0:T(8,128)(2,1)} %refs_0_.12) | copy-start | bytes 6291460
  4.7 4.6 %copy-start.4 = (bf16[2048,512]{1,0:T(8,128)(2,1)S(1)}, bf16[2048,512]{1,0:T(8,128)(2,1)}, u32[]{:S(2)}) copy-start(bf16[2048,512]{1,0:T(8,128)(2,1)} %refs_0_.19) | copy-start | bytes 6291460
  4.7 4.6 %copy-start.5 = (f32[16,4,20]{2,1,0:T(4,128)S(1)}, f32[16,4,20]{2,1,0:T(4,128)}, u32[]{:S(2)}) copy-start(f32[16,4,20]{2,1,0:T(4,128)} %refs_5_.1) | copy-start | bytes 15364
  4.7 4.6 %copy-start.6 = (s32[2048]{0:T(1024)S(1)}, s32[2048]{0:T(1024)}, u32[]{:S(2)}) copy-start(s32[2048]{0:T(1024)} %param.9) | copy-start | bytes 24580
  5.5 8.9 %collective-permute-start.2 = (bf16[512,128]{1,0:T(8,128)(2,1)S(1)}, bf16[512,128]{1,0:T(8,128)(2,1)S(1)}, u32[]{:S(2)}, u32[]{:S(2)}) collective-permute-start(bf16[512,128]{1,0:T(8,128)(2,1)S(1)} %get-tuple-element.19.refs_7_.refs_0_), channel_id=1, source_target_pairs={{0,12},{4,8},{8,4},{12,0},{16,28},{20,24},{24,20},{28,16},{1,13},{... | collective-permute-start | bytes 393224 | tf_op jit(solution)/shard_map/ppermute | solution.py:446
  8.7 6.5 %collective-permute-start.1 = (bf16[512,128]{1,0:T(8,128)(2,1)S(1)}, bf16[512,128]{1,0:T(8,128)(2,1)S(1)}, u32[]{:S(2)}, u32[]{:S(2)}) collective-permute-start(bf16[512,128]{1,0:T(8,128)(2,1)S(1)} %get-tuple-element.19.refs_7_.refs_0_), channel_id=1, source_target_pairs={{0,8},{4,12},{8,0},{12,4},{16,24},{20,28},{24,16},{28,20},{1,9},{5... | collective-permute-start | bytes 393224 | tf_op jit(solution)/shard_map/ppermute | solution.py:446
  9.1 6.0 %collective-permute-start = (bf16[512,128]{1,0:T(8,128)(2,1)S(1)}, bf16[512,128]{1,0:T(8,128)(2,1)S(1)}, u32[]{:S(2)}, u32[]{:S(2)}) collective-permute-start(bf16[512,128]{1,0:T(8,128)(2,1)S(1)} %get-tuple-element.19.refs_7_.refs_0_), channel_id=1, source_target_pairs={{0,4},{4,0},{8,12},{12,8},{16,20},{20,16},{24,28},{28,24},{1,5},{5... | collective-permute-start | bytes 393224 | tf_op jit(solution)/shard_map/ppermute | solution.py:446
  16.6 13.9 %collective-permute-start.5 = (bf16[512,2048]{1,0:T(8,128)(2,1)S(1)}, bf16[512,2048]{1,0:T(8,128)(2,1)S(1)}, u32[]{:S(2)}, u32[]{:S(2)}) collective-permute-start(bf16[512,2048]{1,0:T(8,128)(2,1)S(1)} %gate.7.refs_7_.refs_2_), channel_id=1, source_target_pairs={{0,1},{1,0},{2,3},{3,2},{4,5},{5,4},{6,7},{7,6},{8,9},{9,8},{10,11... | collective-permute-start | bytes 6291464 | tf_op jit(solution)/shard_map/ppermute | solution.py:446
  16.6 17.2 %collective-permute-start.8 = (bf16[128,1024]{1,0:T(8,128)(2,1)S(1)}, bf16[128,1024]{1,0:T(8,128)(2,1)S(1)}, u32[]{:S(2)}, u32[]{:S(2)}) collective-permute-start(bf16[128,1024]{1,0:T(8,128)(2,1)S(1)} %get-tuple-element.17.refs_3_), channel_id=1, source_target_pairs={{0,2},{1,3},{2,0},{3,1},{4,6},{5,7},{6,4},{7,5},{8,10},{9,11},{10,... | collective-permute-start | bytes 786440 | tf_op jit(solution)/shard_map/ppermute | solution.py:446
  18.4 9.3 %collective-permute-start.3 = (bf16[512,128]{1,0:T(8,128)(2,1)S(1)}, bf16[512,128]{1,0:T(8,128)(2,1)S(1)}, u32[]{:S(2)}, u32[]{:S(2)}) collective-permute-start(bf16[512,128]{1,0:T(8,128)(2,1)S(1)} %get-tuple-element.23.refs_1_.refs_6_), channel_id=1, source_target_pairs={{0,16},{4,20},{8,24},{12,28},{16,0},{20,4},{24,8},{28,12},{1,17},{... | collective-permute-start | bytes 393224 | tf_op jit(solution)/shard_map/ppermute | solution.py:446
  20.9 13.8 %collective-permute-start.7 = (bf16[256,1024]{1,0:T(8,128)(2,1)S(1)}, bf16[256,1024]{1,0:T(8,128)(2,1)S(1)}, u32[]{:S(2)}, u32[]{:S(2)}) collective-permute-start(bf16[256,1024]{1,0:T(8,128)(2,1)S(1)} %gate.6.refs_2_.refs_8_.refs_3_), channel_id=1, source_target_pairs={{0,4},{4,0},{8,12},{12,8},{16,20},{20,16},{24,28},{28,24},{1,5},{5... | collective-permute-start | bytes 1572872 | tf_op jit(solution)/shard_map/ppermute | solution.py:446
  22.5 8.1 %collective-permute-start.6 = (bf16[256,1024]{1,0:T(8,128)(2,1)S(1)}, bf16[256,1024]{1,0:T(8,128)(2,1)S(1)}, u32[]{:S(2)}, u32[]{:S(2)}) collective-permute-start(bf16[256,1024]{1,0:T(8,128)(2,1)S(1)} %gate.6.refs_2_.refs_8_.refs_3_), channel_id=1, source_target_pairs={{0,1},{1,0},{2,3},{3,2},{4,5},{5,4},{6,7},{7,6},{8,9},{9,8},{10,11... | collective-permute-start | bytes 1572872 | tf_op jit(solution)/shard_map/ppermute | solution.py:446
  30.0 14.9 %collective-permute-start.9 = (bf16[512,512]{1,0:T(8,128)(2,1)S(1)}, bf16[512,512]{1,0:T(8,128)(2,1)S(1)}, u32[]{:S(2)}, u32[]{:S(2)}) collective-permute-start(bf16[512,512]{1,0:T(8,128)(2,1)S(1)} %finish_rows.5.refs_7_), channel_id=1, source_target_pairs={{0,2},{1,3},{2,0},{3,1},{4,6},{5,7},{6,4},{7,5},{8,10},{9,11},{10,... | collective-permute-start | bytes 1572872 | tf_op jit(solution)/shard_map/ppermute | solution.py:446
  34.7 10.2 %collective-permute-start.13 = (bf16[128,1024]{1,0:T(8,128)(2,1)S(1)}, bf16[128,1024]{1,0:T(8,128)(2,1)S(1)}, u32[]{:S(2)}, u32[]{:S(2)}) collective-permute-start(bf16[128,1024]{1,0:T(8,128)(2,1)S(1)} %gate.8.refs_9_.refs_0_), channel_id=1, source_target_pairs={{0,12},{4,8},{8,4},{12,0},{16,28},{20,24},{24,20},{28,16},{1,13},{... | collective-permute-start | bytes 786440 | tf_op jit(solution)/shard_map/ppermute | solution.py:446
  37.3 11.4 %collective-permute-start.12 = (bf16[128,1024]{1,0:T(8,128)(2,1)S(1)}, bf16[128,1024]{1,0:T(8,128)(2,1)S(1)}, u32[]{:S(2)}, u32[]{:S(2)}) collective-permute-start(bf16[128,1024]{1,0:T(8,128)(2,1)S(1)} %gate.8.refs_9_.refs_0_), channel_id=1, source_target_pairs={{0,8},{4,12},{8,0},{12,4},{16,24},{20,28},{24,16},{28,20},{1,9},{5... | collective-permute-start | bytes 786440 | tf_op jit(solution)/shard_map/ppermute | solution.py:446
  37.7 10.9 %collective-permute-start.11 = (bf16[128,1024]{1,0:T(8,128)(2,1)S(1)}, bf16[128,1024]{1,0:T(8,128)(2,1)S(1)}, u32[]{:S(2)}, u32[]{:S(2)}) collective-permute-start(bf16[128,1024]{1,0:T(8,128)(2,1)S(1)} %gate.8.refs_9_.refs_0_), channel_id=1, source_target_pairs={{0,4},{4,0},{8,12},{12,8},{16,20},{20,16},{24,28},{28,24},{1,5},{5... | collective-permute-start | bytes 786440 | tf_op jit(solution)/shard_map/ppermute | solution.py:446
  38.2 10.4 %collective-permute-start.10 = (bf16[256,512]{1,0:T(8,128)(2,1)S(1)}, bf16[256,512]{1,0:T(8,128)(2,1)S(1)}, u32[]{:S(2)}, u32[]{:S(2)}) collective-permute-start(bf16[256,512]{1,0:T(8,128)(2,1)S(1)} %finish_rows.6.refs_6_), channel_id=1, source_target_pairs={{0,3},{1,2},{2,1},{3,0},{4,7},{5,6},{6,5},{7,4},{8,11},{9,10},{10,... | collective-permute-start | bytes 786440 | tf_op jit(solution)/shard_map/ppermute | solution.py:446
  48.7 4.7 %collective-permute-start.16 = (bf16[512,1024]{1,0:T(8,128)(2,1)S(1)}, bf16[512,1024]{1,0:T(8,128)(2,1)S(1)}, u32[]{:S(2)}, u32[]{:S(2)}) collective-permute-start(bf16[512,1024]{1,0:T(8,128)(2,1)S(1)} %assemble.1.refs_5_.refs_10_), channel_id=1, source_target_pairs={{0,1},{1,0},{2,3},{3,2},{4,5},{5,4},{6,7},{7,6},{8,9},{9,8},{10,11... | collective-permute-start | bytes 3145736 | tf_op jit(solution)/shard_map/ppermute | solution.py:446
  48.9 8.1 %collective-permute-start.14 = (bf16[256,512]{1,0:T(8,128)(2,1)S(1)}, bf16[256,512]{1,0:T(8,128)(2,1)S(1)}, u32[]{:S(2)}, u32[]{:S(2)}) collective-permute-start(bf16[256,512]{1,0:T(8,128)(2,1)S(1)} %gate.9), channel_id=1, source_target_pairs={{0,3},{1,2},{2,1},{3,0},{4,7},{5,6},{6,5},{7,4},{8,11},{9,10},{10,... | collective-permute-start | bytes 786440 | tf_op jit(solution)/shard_map/ppermute | solution.py:446
  49.7 2.9 %collective-permute-start.17 = (bf16[512,512]{1,0:T(8,128)(2,1)S(1)}, bf16[512,512]{1,0:T(8,128)(2,1)S(1)}, u32[]{:S(2)}, u32[]{:S(2)}) collective-permute-start(bf16[512,512]{1,0:T(8,128)(2,1)S(1)} %gate.11), channel_id=1, source_target_pairs={{0,1},{1,0},{2,3},{3,2},{4,5},{5,4},{6,7},{7,6},{8,9},{9,8},{10,11... | collective-permute-start | bytes 1572872 | tf_op jit(solution)/shard_map/ppermute | solution.py:446
  49.8 3.7 %collective-permute-start.15 = (bf16[256,1024]{1,0:T(8,128)(2,1)S(1)}, bf16[256,1024]{1,0:T(8,128)(2,1)S(1)}, u32[]{:S(2)}, u32[]{:S(2)}) collective-permute-start(bf16[256,1024]{1,0:T(8,128)(2,1)S(1)} %gate.10.refs_4_), channel_id=1, source_target_pairs={{0,1},{1,0},{2,3},{3,2},{4,5},{5,4},{6,7},{7,6},{8,9},{9,8},{10,11... | collective-permute-start | bytes 1572872 | tf_op jit(solution)/shard_map/ppermute | solution.py:446

commit v5 on v4

--- a/solution.py
+++ b/solution.py
@@ -14,7 +14,9 @@
 TILE = 512
 
 
-SCALE = 5.0
+SCALE = 8.0
+SHORT = 0.02
+LONG = 3
 
 
 def cost(us):
@@ -161,12 +163,12 @@
     pass
 
 
-def gate(x, *after):
+def gate(x, *after, us=0.1):
     (out,) = call(
         gate_kernel,
         [jax.ShapeDtypeStruct(x.shape, x.dtype)],
         "gate",
-        0.1,
+        us,
         1,
         [x],
         after,
@@ -266,7 +268,7 @@
     copy.wait()
 
 
-def local_attention(args, parts, blocks, weight=None, after=()):
+def local_attention(args, parts, blocks, weight=None, after=(), us=None):
     queries, levels = args[0], args[-1]
     tokens, width = queries.shape
     count = tokens // STRETCH
@@ -289,7 +291,8 @@
             anywhere_in=(0,),
             scratch_shapes=[pltpu.SemaphoreType.DMA],
         )
-    return call(kernel, out_shape, "local_attention", len(blocks), 8, args, after)[0]
+    us = len(blocks) if us is None else us
+    return call(kernel, out_shape, "local_attention", us, 8, args, after)[0]
 
 
 def finish_kernel(
@@ -471,6 +474,7 @@
 
     levels, own = block_states(key_vectors, value_vectors, heads, size, portions)
     near = [flip(own, "ctx", b) for b in range(1, min(4, ctx_size))]
+    mate = flip(out_weight, "mp", 1)
 
     parts = tokens // mp_size // STRETCH
     far_groups = list(range(2, mp_size))
@@ -483,7 +487,7 @@
     remote = near[:1]
     ready = near[0] if near else local
     if ctx_bits > 1:
-        pair, running = merge_states(own, near, [local])
+        pair, running = merge_states(own, near, [local, mate])
         remote.append(pair)
         ready = running
     far = None
@@ -500,9 +504,7 @@
         over_pair[j] = flip(x, "mp", 1)
         if ctx_size > 1:
             there[j] = flip(x, "ctx", 1)
-    weight = gate(weight, ready, *held)
-    mate = flip(weight, "mp", 1)
-    close = local_attention(args, parts, own_blocks, after=[ready, weight] + held)
+    close = local_attention(args, parts, own_blocks, after=[ready] + held, us=SHORT)
     done = [close]
 
     def finished(j, part, blocks, local, places):
@@ -517,13 +519,16 @@
     received = {}
     for j in far_groups[:-1]:
         received[j] = [flip(finished(j, 0, parts, local, far_blocks), "mp", j)] * parts
-    done += [mate] + list(over_pair.values())
+    done += list(over_pair.values())
     last = far_groups[-1]
     received[last] = [
         flip(finished(last, part, 1, local, far_blocks), "mp", last) for part in range(parts - 1)
     ]
-    beside = local_attention(args, parts, mate_blocks, after=done)
-    done = [beside] + list(there.values())
+    beside = local_attention(args, parts, mate_blocks, after=done, us=SHORT)
+    done = [beside]
+    for j in there:
+        there[j] = gate(there[j], *done, us=LONG)
+        done.append(there[j])
     pieces = {}
     for j in evens:
         x = gate(got[j][1], *done)

time: 58.7 us -> 55.4 us (0.944)
  waiting for transfers between devices: 12.3 us -> 8.58 us
    ppermute x18, waiting for transfers between devices: 12.3 us -> 8.58 us  [flip(): return lax.ppermute(x, axis, [(i, i ^ bits) for i in range(n)])]
  transfers between devices with their start and end apart: 18 -> 18, of which waited for: 7 -> 7; matrix products, arithmetic and copies ran while one was open for 0% -> 0% of each run, Pallas kernels for 42% -> 44%
where the time goes in v5:
time: 55.4 us; the launch traced here: 55.3 us
  Pallas kernels  26.1 us (47%)
  starting transfers between devices  18.5 us (33%)
  waiting for transfers between devices  8.58 us (15%)
  local copies, waits for them, and re-layouts  1.77 us (3%)
    pallas_call x22, Pallas kernels, call(): pl.pallas_call(run, in_specs=[anywhere if i in anywhere_in else vmem for...  26.1 us
    ppermute x18, starting transfers between devices, flip(): return lax.ppermute(x, axis, [(i, i ^ bits) for i in range(n)])  18.5 us
    ppermute x18, waiting for transfers between devices, flip(): return lax.ppermute(x, axis, [(i, i ^ bits) for i in range(n)])  8.58 us
    unnamed x14, local copies, waits for them, and re-layouts  1.77 us
  transfers between devices with their start and end apart: 18, of which 7 were waited for; matrix products, arithmetic and copies ran while one was open for 0% of the time, Pallas kernels for 44%

profile of v5, /device:TPU:0, one launch (start us, length us, event | category | flops | bytes accessed | tf_op | source)
XLA Modules:
  0.0 55.3 jit_solution(11032873767090818652)
XLA Ops:
  0.0 0.0 copy-start.1
  0.0 0.0 copy-start
  0.0 0.0 copy-start.4
  0.0 1.7 %copy-done.4 = bf16[512,2048]{1,0:T(8,128)(2,1)S(1)} copy-done((bf16[512,2048]{1,0:T(8,128)(2,1)S(1)}, bf16[512,2048]{1,0:T(8,128)(2,1)}, u32[]{:S(2)}) %copy-start.4) | copy-done | bytes 2097176
  1.7 0.1 slice_weight.1
  1.8 3.0 %collective-permute-start.5 = (bf16[256,1024]{1,0:T(8,128)(2,1)S(1)}, bf16[256,1024]{1,0:T(8,128)(2,1)S(1)}, u32[]{:S(2)}, u32[]{:S(2)}) collective-permute-start(bf16[256,1024]{1,0:T(8,128)(2,1)S(1)} %get-tuple-element.16.refs_2_), channel_id=1, source_target_pairs={{0,2},{1,3},{2,0},{3,1},{4,6},{5,7},{6,4},{7,5},{8,10},{9,11},{10,... | collective-permute-start | bytes 1572872 | tf_op jit(solution)/shard_map/ppermute | solution.py:449
  4.8 0.0 copy-done.1
  4.8 0.0 copy-done
  4.9 0.0 copy-start.3
  4.9 0.0 copy-start.6
  4.9 0.8 %block_states.1 = (bf16[7,4,128,128]{3,2,1,0:T(8,128)(2,1)S(1)}, bf16[512,128]{1,0:T(8,128)(2,1)S(1)}) custom-call(bf16[2048,512]{1,0:T(8,128)(2,1)S(1)} %copy-done, bf16[2048,512]{1,0:T(8,128)(2,1)S(1)} %copy-done.1, bf16[256,1024]{1,0:T(8,128)(2,1)S(1)} %get-tuple-element.16.refs_2_, bf16[128,1024]{1,0:T(8,128)(2,1)S(1)} %get-tuple-element.17.refs_3_), custom_call_target="tpu_custom_call" | custom-call | flops 8000000000 | bytes 24000000 | tf_op jit(solution)/shard_map/block_states/pallas_call | solution.py:36
  5.7 2.6 %collective-permute-start.2 = (bf16[512,128]{1,0:T(8,128)(2,1)S(1)}, bf16[512,128]{1,0:T(8,128)(2,1)S(1)}, u32[]{:S(2)}, u32[]{:S(2)}) collective-permute-start(bf16[512,128]{1,0:T(8,128)(2,1)S(1)} %get-tuple-element.19.refs_7_.refs_0_), channel_id=1, source_target_pairs={{0,12},{4,8},{8,4},{12,0},{16,28},{20,24},{24,20},{28,16},{1,13},{... | collective-permute-start | bytes 393224 | tf_op jit(solution)/shard_map/ppermute | solution.py:449
  8.3 0.5 collective-permute-start.1
  8.7 0.5 collective-permute-start
  9.2 0.0 copy-done.5
  9.2 0.0 collective-permute-start.3
  9.2 0.0 copy-done.2
  9.2 0.0 copy-done.3
  9.3 0.0 copy-done.6
  9.3 5.1 %local_attention.3 = (bf16[1024,512]{1,0:T(8,128)(2,1)S(1)}, bf16[512,2048]{1,0:T(8,128)(2,1)S(1)}, bf16[48,512]{1,0:T(8,128)(2,1)S(1)}) custom-call(bf16[512,2048]{1,0:T(8,128)(2,1)S(1)} %copy-done.5, bf16[2048,512]{1,0:T(8,128)(2,1)S(1)} %copy-done.2, bf16[2048,512]{1,0:T(8,128)(2,1)S(1)} %copy-done, bf16[2048,512]{1,0:T(8,128)(2,1)S(1)} %copy-done.1, ...), custom_call_target="tpu_custom_call" | custom-call | flops 32000000000 | bytes 96000000 | tf_op jit(solution)/shard_map/local_attention/pallas_call | solution.py:36
  14.3 0.0 collective-permute-done.2.refs_3_
  14.3 0.1 collective-permute-done.1.refs_2_
  14.5 0.0 collective-permute-done.refs_1_.refs_4_
  14.5 0.0 collective-permute-done.3.refs_5_.refs_1_.refs_2_
  14.5 0.1 merge_states.1
  14.6 2.7 %collective-permute-start.4 = (bf16[512,128]{1,0:T(8,128)(2,1)S(1)}, bf16[512,128]{1,0:T(8,128)(2,1)S(1)}, u32[]{:S(2)}, u32[]{:S(2)}) collective-permute-start(bf16[512,128]{1,0:T(8,128)(2,1)S(1)} %get-tuple-element.23.refs_1_.refs_6_), channel_id=1, source_target_pairs={{0,16},{4,20},{8,24},{12,28},{16,0},{20,4},{24,8},{28,12},{1,17},{... | collective-permute-start | bytes 393224 | tf_op jit(solution)/shard_map/ppermute | solution.py:449
  17.2 1.2 %collective-permute-start.8 = (bf16[128,1024]{1,0:T(8,128)(2,1)S(1)}, bf16[128,1024]{1,0:T(8,128)(2,1)S(1)}, u32[]{:S(2)}, u32[]{:S(2)}) collective-permute-start(bf16[128,1024]{1,0:T(8,128)(2,1)S(1)} %get-tuple-element.17.refs_3_), channel_id=1, source_target_pairs={{0,2},{1,3},{2,0},{3,1},{4,6},{5,7},{6,4},{7,5},{8,10},{9,11},{10,... | collective-permute-start | bytes 786440 | tf_op jit(solution)/shard_map/ppermute | solution.py:449
  18.4 0.0 collective-permute-done.5.refs_0_
  18.4 1.5 %collective-permute-start.7 = (bf16[256,1024]{1,0:T(8,128)(2,1)S(1)}, bf16[256,1024]{1,0:T(8,128)(2,1)S(1)}, u32[]{:S(2)}, u32[]{:S(2)}) collective-permute-start(bf16[256,1024]{1,0:T(8,128)(2,1)S(1)} %gate.6.refs_7_.refs_3_), channel_id=1, source_target_pairs={{0,4},{4,0},{8,12},{12,8},{16,20},{20,16},{24,28},{28,24},{1,5},{5... | collective-permute-start | bytes 1572872 | tf_op jit(solution)/shard_map/ppermute | solution.py:449
  19.9 0.0 collective-permute-start.6
  19.9 2.2 %local_attention.4.refs_7_.refs_1_ = bf16[512,512]{1,0:T(8,128)(2,1)S(1)} custom-call(bf16[2048,512]{1,0:T(8,128)(2,1)S(1)} %copy-done.2, bf16[2048,512]{1,0:T(8,128)(2,1)S(1)} %copy-done, bf16[2048,512]{1,0:T(8,128)(2,1)S(1)} %copy-done.1, s32[8,1,256]{2,1,0:T(1,128)S(1)} %bitcast.2, bf16[48,512]{1,0:T(8,128)(2,1)S(1)} %get-tuple-element.21.refs_4_.refs_3_, ...), custom_call_target="tpu_custom_call" | custom-call | flops 160000000 | bytes 480000 | tf_op jit(solution)/shard_map/local_attention/pallas_call | solution.py:36
  22.1 2.0 %collective-permute-done.4.refs_6_ = bf16[512,128]{1,0:T(8,128)(2,1)S(1)} collective-permute-done((bf16[512,128]{1,0:T(8,128)(2,1)S(1)}, bf16[512,128]{1,0:T(8,128)(2,1)S(1)}, u32[]{:S(2)}, u32[]{:S(2)}) %collective-permute-start.4) | collective-permute-done | bytes 131104 | tf_op jit(solution)/shard_map/ppermute | solution.py:449
  24.1 2.3 %finish_rows.5.refs_7_ = bf16[512,512]{1,0:T(8,128)(2,1)S(1)} custom-call(bf16[2048,512]{1,0:T(8,128)(2,1)S(1)} %copy-done.2, bf16[1024,512]{1,0:T(8,128)(2,1)S(1)} %get-tuple-element.20.refs_4_.refs_1_, s32[8,1,256]{2,1,0:T(1,128)S(1)} %bitcast.3, bf16[48,512]{1,0:T(8,128)(2,1)S(1)} %get-tuple-element.21.refs_4_.refs_3_, ...), custom_call_target="tpu_custom_call" | custom-call | flops 16000000000 | bytes 48000000 | tf_op jit(solution)/shard_map/finish_rows/pallas_call | solution.py:36
  26.4 1.0 %collective-permute-start.9 = (bf16[512,512]{1,0:T(8,128)(2,1)S(1)}, bf16[512,512]{1,0:T(8,128)(2,1)S(1)}, u32[]{:S(2)}, u32[]{:S(2)}) collective-permute-start(bf16[512,512]{1,0:T(8,128)(2,1)S(1)} %finish_rows.5.refs_7_), channel_id=1, source_target_pairs={{0,2},{1,3},{2,0},{3,1},{4,6},{5,7},{6,4},{7,5},{8,10},{9,11},{10,... | collective-permute-start | bytes 1572872 | tf_op jit(solution)/shard_map/ppermute | solution.py:449
  27.4 0.0 collective-permute-done.6.refs_8_.refs_3_.refs_1_
  27.4 1.0 %finish_rows.6.refs_6_ = bf16[256,512]{1,0:T(8,128)(2,1)S(1)} custom-call(bf16[2048,512]{1,0:T(8,128)(2,1)S(1)} %copy-done.2, bf16[1024,512]{1,0:T(8,128)(2,1)S(1)} %get-tuple-element.20.refs_4_.refs_1_, s32[8,1,256]{2,1,0:T(1,128)S(1)} %bitcast.4, bf16[48,512]{1,0:T(8,128)(2,1)S(1)} %get-tuple-element.21.refs_4_.refs_3_, ...), custom_call_target="tpu_custom_call" | custom-call | flops 8000000000 | bytes 24000000 | tf_op jit(solution)/shard_map/finish_rows/pallas_call | solution.py:36
  28.4 2.2 %local_attention.5.refs_1_.refs_7_ = bf16[512,512]{1,0:T(8,128)(2,1)S(1)} custom-call(bf16[2048,512]{1,0:T(8,128)(2,1)S(1)} %copy-done.2, bf16[2048,512]{1,0:T(8,128)(2,1)S(1)} %copy-done, bf16[2048,512]{1,0:T(8,128)(2,1)S(1)} %copy-done.1, s32[8,1,256]{2,1,0:T(1,128)S(1)} %bitcast.5, bf16[48,512]{1,0:T(8,128)(2,1)S(1)} %get-tuple-element.21.refs_4_.refs_3_, ...), custom_call_target="tpu_custom_call" | custom-call | flops 160000000 | bytes 480000 | tf_op jit(solution)/shard_map/local_attention/pallas_call | solution.py:36
  30.7 1.1 %collective-permute-done.7.refs_0_ = bf16[256,1024]{1,0:T(8,128)(2,1)S(1)} collective-permute-done((bf16[256,1024]{1,0:T(8,128)(2,1)S(1)}, bf16[256,1024]{1,0:T(8,128)(2,1)S(1)}, u32[]{:S(2)}, u32[]{:S(2)}) %collective-permute-start.7) | collective-permute-done | bytes 524320 | tf_op jit(solution)/shard_map/ppermute | solution.py:449
  31.8 0.0 collective-permute-done.8.refs_0_
  31.8 2.5 %collective-permute-start.13 = (bf16[128,1024]{1,0:T(8,128)(2,1)S(1)}, bf16[128,1024]{1,0:T(8,128)(2,1)S(1)}, u32[]{:S(2)}, u32[]{:S(2)}) collective-permute-start(bf16[128,1024]{1,0:T(8,128)(2,1)S(1)} %gate.8.refs_9_.refs_0_), channel_id=1, source_target_pairs={{0,12},{4,8},{8,4},{12,0},{16,28},{20,24},{24,20},{28,16},{1,13},{... | collective-permute-start | bytes 786440 | tf_op jit(solution)/shard_map/ppermute | solution.py:449
  34.3 0.5 collective-permute-start.12
  34.8 0.5 collective-permute-start.11
  35.3 0.0 collective-permute-start.10
  35.3 1.0 %finish_rows.7.refs_7_.refs_0_ = bf16[256,512]{1,0:T(8,128)(2,1)S(1)} custom-call(bf16[2048,512]{1,0:T(8,128)(2,1)S(1)} %copy-done.2, bf16[1024,512]{1,0:T(8,128)(2,1)S(1)} %get-tuple-element.20.refs_4_.refs_1_, s32[8,1,256]{2,1,0:T(1,128)S(1)} %bitcast.6, bf16[48,512]{1,0:T(8,128)(2,1)S(1)} %get-tuple-element.21.refs_4_.refs_3_, ...), custom_call_target="tpu_custom_call" | custom-call | flops 8000000000 | bytes 24000000 | tf_op jit(solution)/shard_map/finish_rows/pallas_call | solution.py:36
  36.3 2.3 %finish_rows.8.refs_7_.refs_0_ = bf16[512,512]{1,0:T(8,128)(2,1)S(1)} custom-call(bf16[2048,512]{1,0:T(8,128)(2,1)S(1)} %copy-done.2, bf16[512,512]{1,0:T(8,128)(2,1)S(1)} %local_attention.5.refs_1_.refs_7_, s32[8,1,256]{2,1,0:T(1,128)S(1)} %bitcast.7, bf16[48,512]{1,0:T(8,128)(2,1)S(1)} %get-tuple-element.21.refs_4_.refs_3_, ...), custom_call_target="tpu_custom_call" | custom-call | flops 16000000000 | bytes 48000000 | tf_op jit(solution)/shard_map/finish_rows/pallas_call | solution.py:36
  38.6 2.3 %finish_rows.9.refs_4_.refs_1_.refs_0_.refs_6_ = bf16[512,512]{1,0:T(8,128)(2,1)S(1)} custom-call(bf16[2048,512]{1,0:T(8,128)(2,1)S(1)} %copy-done.2, bf16[512,512]{1,0:T(8,128)(2,1)S(1)} %local_attention.4.refs_7_.refs_1_, s32[8,1,256]{2,1,0:T(1,128)S(1)} %bitcast.8, bf16[48,512]{1,0:T(8,128)(2,1)S(1)} %get-tuple-element.21.refs_4_.refs_3_, ...), custom_call_target="tpu_custom_call" | custom-call | flops 16000000000 | bytes 48000000 | tf_op jit(solution)/shard_map/finish_rows/pallas_call | solution.py:36
  40.9 0.4 collective-permute-done.9.refs_5_.refs_6_.refs_2_.refs_3_.refs_1_.refs_7_.refs_8_
  41.3 0.6 %collective-permute-done.13.refs_3_ = bf16[128,1024]{1,0:T(8,128)(2,1)S(1)} collective-permute-done((bf16[128,1024]{1,0:T(8,128)(2,1)S(1)}, bf16[128,1024]{1,0:T(8,128)(2,1)S(1)}, u32[]{:S(2)}, u32[]{:S(2)}) %collective-permute-start.13) | collective-permute-done | bytes 262176 | tf_op jit(solution)/shard_map/ppermute | solution.py:449
  42.0 3.4 %collective-permute-done.12.refs_2_ = bf16[128,1024]{1,0:T(8,128)(2,1)S(1)} collective-permute-done((bf16[128,1024]{1,0:T(8,128)(2,1)S(1)}, bf16[128,1024]{1,0:T(8,128)(2,1)S(1)}, u32[]{:S(2)}, u32[]{:S(2)}) %collective-permute-start.12) | collective-permute-done | bytes 262176 | tf_op jit(solution)/shard_map/ppermute | solution.py:449
  45.3 0.0 collective-permute-done.11.refs_1_
  45.3 0.0 collective-permute-done.10.refs_7_.refs_4_.refs_9_.refs_1_
  45.3 0.1 assemble.1.refs_5_.refs_10_
  45.4 0.2 collective-permute-start.16
  45.6 1.5 %collective-permute-start.14 = (bf16[256,512]{1,0:T(8,128)(2,1)S(1)}, bf16[256,512]{1,0:T(8,128)(2,1)S(1)}, u32[]{:S(2)}, u32[]{:S(2)}) collective-permute-start(bf16[256,512]{1,0:T(8,128)(2,1)S(1)} %gate.9), channel_id=1, source_target_pairs={{0,3},{1,2},{2,1},{3,0},{4,7},{5,6},{6,5},{7,4},{8,11},{9,10},{10,... | collective-permute-start | bytes 786440 | tf_op jit(solution)/shard_map/ppermute | solution.py:449
  47.1 0.1 collective-permute-start.17
  47.1 0.4 collective-permute-start.15
  47.6 2.3 %project_start.1 = (f32[256,2048]{1,0:T(8,128)S(1)}, f32[256,2048]{1,0:T(8,128)S(1)}) custom-call(bf16[512,512]{1,0:T(8,128)(2,1)S(1)} %finish_rows.9.refs_4_.refs_1_.refs_0_.refs_6_, bf16[512,512]{1,0:T(8,128)(2,1)S(1)} %collective-permute-done.9.refs_5_.refs_6_.refs_2_.refs_3_.refs_1_.refs_7_.refs_8_, bf16[512,2048]{1,0:T(8,128)(2,1)S(1)} %get-tuple-element.24.refs_2_, ...), custom_call_target="tpu_custom_call" | custom-call | flops 19200000000 | bytes 57600000 | tf_op jit(solution)/shard_map/project_start/pallas_call | solution.py:36
  49.9 0.0 collective-permute-done.17.refs_0_
  49.9 0.9 %project_add.1.refs_4_ = f32[256,2048]{1,0:T(8,128)S(1)} custom-call(bf16[512,512]{1,0:T(8,128)(2,1)S(1)} %collective-permute-done.17.refs_0_, bf16[512,2048]{1,0:T(8,128)(2,1)S(1)} %collective-permute-done.3.refs_5_.refs_1_.refs_2_, f32[256,2048]{1,0:T(8,128)S(1)} %get-tuple-element.25.refs_2_), custom_call_target="tpu_custom_call", output_to_operand_aliasing={{}: (2, {})} | custom-call | flops 8000000000 | bytes 24000000 | tf_op jit(solution)/shard_map/project_add/pallas_call | solution.py:36
  50.8 0.0 collective-permute-done.15.refs_4_.refs_2_
  50.8 0.0 collective-permute-done.16.refs_5_.refs_3_
  50.8 2.0 %project_last.2.refs_5_ = bf16[512,2048]{1,0:T(8,128)(2,1)} custom-call(bf16[512,512]{1,0:T(8,128)(2,1)S(1)} %collective-permute-done.17.refs_0_, bf16[256,512]{1,0:T(8,128)(2,1)S(1)} %collective-permute-done.10.refs_7_.refs_4_.refs_9_.refs_1_, bf16[512,2048]{1,0:T(8,128)(2,1)S(1)} %collective-permute-done.3.refs_5_.refs_1_.refs_2_, ...), custom_call_target="tpu_custom_call" | custom-call | flops 12000000000 | bytes 36000000 | tf_op jit(solution)/shard_map/project_last/pallas_call | solution.py:36
  52.9 0.8 %collective-permute-done.14.refs_0_ = bf16[256,512]{1,0:T(8,128)(2,1)S(1)} collective-permute-done((bf16[256,512]{1,0:T(8,128)(2,1)S(1)}, bf16[256,512]{1,0:T(8,128)(2,1)S(1)}, u32[]{:S(2)}, u32[]{:S(2)}) %collective-permute-start.14) | collective-permute-done | bytes 262176 | tf_op jit(solution)/shard_map/ppermute | solution.py:449
  53.7 1.5 %project_last.3 = bf16[512,2048]{1,0:T(8,128)(2,1)} custom-call(bf16[256,512]{1,0:T(8,128)(2,1)S(1)} %collective-permute-done.14.refs_0_, bf16[256,1024]{1,0:T(8,128)(2,1)S(1)} %collective-permute-done.6.refs_8_.refs_3_.refs_1_, bf16[256,1024]{1,0:T(8,128)(2,1)S(1)} %collective-permute-done.15.refs_4_.refs_2_, ...), custom_call_target="tpu_custom_call", output_to_operand_aliasing={{}: (5, {})} | custom-call | flops 12000000000 | bytes 36000000 | tf_op jit(solution)/shard_map/project_last/pallas_call | solution.py:36
  (8 shorter events, 0.0 us)
Async XLA Ops:
  0.0 4.8 %copy-start.1 = (bf16[2048,512]{1,0:T(8,128)(2,1)S(1)}, bf16[2048,512]{1,0:T(8,128)(2,1)}, u32[]{:S(2)}) copy-start(bf16[2048,512]{1,0:T(8,128)(2,1)} %refs_2_.5) | copy-start | bytes 6291460
  0.0 4.8 %copy-start = (bf16[2048,512]{1,0:T(8,128)(2,1)S(1)}, bf16[2048,512]{1,0:T(8,128)(2,1)}, u32[]{:S(2)}) copy-start(bf16[2048,512]{1,0:T(8,128)(2,1)} %refs_1_.7) | copy-start | bytes 6291460
  0.0 1.7 %copy-start.4 = (bf16[512,2048]{1,0:T(8,128)(2,1)S(1)}, bf16[512,2048]{1,0:T(8,128)(2,1)}, u32[]{:S(2)}) copy-start(bf16[512,2048]{1,0:T(8,128)(2,1)} %refs_0_.12) | copy-start | bytes 6291460
  1.8 16.6 %collective-permute-start.5 = (bf16[256,1024]{1,0:T(8,128)(2,1)S(1)}, bf16[256,1024]{1,0:T(8,128)(2,1)S(1)}, u32[]{:S(2)}, u32[]{:S(2)}) collective-permute-start(bf16[256,1024]{1,0:T(8,128)(2,1)S(1)} %get-tuple-element.16.refs_2_), channel_id=1, source_target_pairs={{0,2},{1,3},{2,0},{3,1},{4,6},{5,7},{6,4},{7,5},{8,10},{9,11},{10,... | collective-permute-start | bytes 1572872 | tf_op jit(solution)/shard_map/ppermute | solution.py:449
  4.8 4.4 %copy-start.5 = (bf16[512,2048]{1,0:T(8,128)(2,1)S(1)}, bf16[512,2048]{1,0:T(8,128)(2,1)}, u32[]{:S(2)}) copy-start(bf16[512,2048]{1,0:T(8,128)(2,1)} %refs_0_.12) | copy-start | bytes 6291460
  4.9 4.4 %copy-start.2 = (bf16[2048,512]{1,0:T(8,128)(2,1)S(1)}, bf16[2048,512]{1,0:T(8,128)(2,1)}, u32[]{:S(2)}) copy-start(bf16[2048,512]{1,0:T(8,128)(2,1)} %refs_0_.19) | copy-start | bytes 6291460
  4.9 4.4 %copy-start.3 = (s32[2048]{0:T(1024)S(1)}, s32[2048]{0:T(1024)}, u32[]{:S(2)}) copy-start(s32[2048]{0:T(1024)} %param.9) | copy-start | bytes 24580
  4.9 4.4 %copy-start.6 = (f32[16,4,20]{2,1,0:T(4,128)S(1)}, f32[16,4,20]{2,1,0:T(4,128)}, u32[]{:S(2)}) copy-start(f32[16,4,20]{2,1,0:T(4,128)} %refs_5_.1) | copy-start | bytes 15364
  5.7 8.7 %collective-permute-start.2 = (bf16[512,128]{1,0:T(8,128)(2,1)S(1)}, bf16[512,128]{1,0:T(8,128)(2,1)S(1)}, u32[]{:S(2)}, u32[]{:S(2)}) collective-permute-start(bf16[512,128]{1,0:T(8,128)(2,1)S(1)} %get-tuple-element.19.refs_7_.refs_0_), channel_id=1, source_target_pairs={{0,12},{4,8},{8,4},{12,0},{16,28},{20,24},{24,20},{28,16},{1,13},{... | collective-permute-start | bytes 393224 | tf_op jit(solution)/shard_map/ppermute | solution.py:449
  8.3 6.2 %collective-permute-start.1 = (bf16[512,128]{1,0:T(8,128)(2,1)S(1)}, bf16[512,128]{1,0:T(8,128)(2,1)S(1)}, u32[]{:S(2)}, u32[]{:S(2)}) collective-permute-start(bf16[512,128]{1,0:T(8,128)(2,1)S(1)} %get-tuple-element.19.refs_7_.refs_0_), channel_id=1, source_target_pairs={{0,8},{4,12},{8,0},{12,4},{16,24},{20,28},{24,16},{28,20},{1,9},{5... | collective-permute-start | bytes 393224 | tf_op jit(solution)/shard_map/ppermute | solution.py:449
  8.7 5.8 %collective-permute-start = (bf16[512,128]{1,0:T(8,128)(2,1)S(1)}, bf16[512,128]{1,0:T(8,128)(2,1)S(1)}, u32[]{:S(2)}, u32[]{:S(2)}) collective-permute-start(bf16[512,128]{1,0:T(8,128)(2,1)S(1)} %get-tuple-element.19.refs_7_.refs_0_), channel_id=1, source_target_pairs={{0,4},{4,0},{8,12},{12,8},{16,20},{20,16},{24,28},{28,24},{1,5},{5... | collective-permute-start | bytes 393224 | tf_op jit(solution)/shard_map/ppermute | solution.py:449
  9.2 5.3 %collective-permute-start.3 = (bf16[512,2048]{1,0:T(8,128)(2,1)S(1)}, bf16[512,2048]{1,0:T(8,128)(2,1)S(1)}, u32[]{:S(2)}, u32[]{:S(2)}) collective-permute-start(bf16[512,2048]{1,0:T(8,128)(2,1)S(1)} %copy-done.5), channel_id=1, source_target_pairs={{0,1},{1,0},{2,3},{3,2},{4,5},{5,4},{6,7},{7,6},{8,9},{9,8},{10,11... | collective-permute-start | bytes 6291464 | tf_op jit(solution)/shard_map/ppermute | solution.py:449
  14.6 9.5 %collective-permute-start.4 = (bf16[512,128]{1,0:T(8,128)(2,1)S(1)}, bf16[512,128]{1,0:T(8,128)(2,1)S(1)}, u32[]{:S(2)}, u32[]{:S(2)}) collective-permute-start(bf16[512,128]{1,0:T(8,128)(2,1)S(1)} %get-tuple-element.23.refs_1_.refs_6_), channel_id=1, source_target_pairs={{0,16},{4,20},{8,24},{12,28},{16,0},{20,4},{24,8},{28,12},{1,17},{... | collective-permute-start | bytes 393224 | tf_op jit(solution)/shard_map/ppermute | solution.py:449
  17.2 14.6 %collective-permute-start.8 = (bf16[128,1024]{1,0:T(8,128)(2,1)S(1)}, bf16[128,1024]{1,0:T(8,128)(2,1)S(1)}, u32[]{:S(2)}, u32[]{:S(2)}) collective-permute-start(bf16[128,1024]{1,0:T(8,128)(2,1)S(1)} %get-tuple-element.17.refs_3_), channel_id=1, source_target_pairs={{0,2},{1,3},{2,0},{3,1},{4,6},{5,7},{6,4},{7,5},{8,10},{9,11},{10,... | collective-permute-start | bytes 786440 | tf_op jit(solution)/shard_map/ppermute | solution.py:449
  18.4 13.4 %collective-permute-start.7 = (bf16[256,1024]{1,0:T(8,128)(2,1)S(1)}, bf16[256,1024]{1,0:T(8,128)(2,1)S(1)}, u32[]{:S(2)}, u32[]{:S(2)}) collective-permute-start(bf16[256,1024]{1,0:T(8,128)(2,1)S(1)} %gate.6.refs_7_.refs_3_), channel_id=1, source_target_pairs={{0,4},{4,0},{8,12},{12,8},{16,20},{20,16},{24,28},{28,24},{1,5},{5... | collective-permute-start | bytes 1572872 | tf_op jit(solution)/shard_map/ppermute | solution.py:449
  19.9 7.5 %collective-permute-start.6 = (bf16[256,1024]{1,0:T(8,128)(2,1)S(1)}, bf16[256,1024]{1,0:T(8,128)(2,1)S(1)}, u32[]{:S(2)}, u32[]{:S(2)}) collective-permute-start(bf16[256,1024]{1,0:T(8,128)(2,1)S(1)} %gate.6.refs_7_.refs_3_), channel_id=1, source_target_pairs={{0,1},{1,0},{2,3},{3,2},{4,5},{5,4},{6,7},{7,6},{8,9},{9,8},{10,11... | collective-permute-start | bytes 1572872 | tf_op jit(solution)/shard_map/ppermute | solution.py:449
  26.4 14.9 %collective-permute-start.9 = (bf16[512,512]{1,0:T(8,128)(2,1)S(1)}, bf16[512,512]{1,0:T(8,128)(2,1)S(1)}, u32[]{:S(2)}, u32[]{:S(2)}) collective-permute-start(bf16[512,512]{1,0:T(8,128)(2,1)S(1)} %finish_rows.5.refs_7_), channel_id=1, source_target_pairs={{0,2},{1,3},{2,0},{3,1},{4,6},{5,7},{6,4},{7,5},{8,10},{9,11},{10,... | collective-permute-start | bytes 1572872 | tf_op jit(solution)/shard_map/ppermute | solution.py:449
  31.8 10.2 %collective-permute-start.13 = (bf16[128,1024]{1,0:T(8,128)(2,1)S(1)}, bf16[128,1024]{1,0:T(8,128)(2,1)S(1)}, u32[]{:S(2)}, u32[]{:S(2)}) collective-permute-start(bf16[128,1024]{1,0:T(8,128)(2,1)S(1)} %gate.8.refs_9_.refs_0_), channel_id=1, source_target_pairs={{0,12},{4,8},{8,4},{12,0},{16,28},{20,24},{24,20},{28,16},{1,13},{... | collective-permute-start | bytes 786440 | tf_op jit(solution)/shard_map/ppermute | solution.py:449
  34.3 11.0 %collective-permute-start.12 = (bf16[128,1024]{1,0:T(8,128)(2,1)S(1)}, bf16[128,1024]{1,0:T(8,128)(2,1)S(1)}, u32[]{:S(2)}, u32[]{:S(2)}) collective-permute-start(bf16[128,1024]{1,0:T(8,128)(2,1)S(1)} %gate.8.refs_9_.refs_0_), channel_id=1, source_target_pairs={{0,8},{4,12},{8,0},{12,4},{16,24},{20,28},{24,16},{28,20},{1,9},{5... | collective-permute-start | bytes 786440 | tf_op jit(solution)/shard_map/ppermute | solution.py:449
  34.8 10.6 %collective-permute-start.11 = (bf16[128,1024]{1,0:T(8,128)(2,1)S(1)}, bf16[128,1024]{1,0:T(8,128)(2,1)S(1)}, u32[]{:S(2)}, u32[]{:S(2)}) collective-permute-start(bf16[128,1024]{1,0:T(8,128)(2,1)S(1)} %gate.8.refs_9_.refs_0_), channel_id=1, source_target_pairs={{0,4},{4,0},{8,12},{12,8},{16,20},{20,16},{24,28},{28,24},{1,5},{5... | collective-permute-start | bytes 786440 | tf_op jit(solution)/shard_map/ppermute | solution.py:449
  35.3 10.1 %collective-permute-start.10 = (bf16[256,512]{1,0:T(8,128)(2,1)S(1)}, bf16[256,512]{1,0:T(8,128)(2,1)S(1)}, u32[]{:S(2)}, u32[]{:S(2)}) collective-permute-start(bf16[256,512]{1,0:T(8,128)(2,1)S(1)} %finish_rows.6.refs_6_), channel_id=1, source_target_pairs={{0,3},{1,2},{2,1},{3,0},{4,7},{5,6},{6,5},{7,4},{8,11},{9,10},{10,... | collective-permute-start | bytes 786440 | tf_op jit(solution)/shard_map/ppermute | solution.py:449
  45.4 5.4 %collective-permute-start.16 = (bf16[512,1024]{1,0:T(8,128)(2,1)S(1)}, bf16[512,1024]{1,0:T(8,128)(2,1)S(1)}, u32[]{:S(2)}, u32[]{:S(2)}) collective-permute-start(bf16[512,1024]{1,0:T(8,128)(2,1)S(1)} %assemble.1.refs_5_.refs_10_), channel_id=1, source_target_pairs={{0,1},{1,0},{2,3},{3,2},{4,5},{5,4},{6,7},{7,6},{8,9},{9,8},{10,11... | collective-permute-start | bytes 3145736 | tf_op jit(solution)/shard_map/ppermute | solution.py:449
  45.6 8.1 %collective-permute-start.14 = (bf16[256,512]{1,0:T(8,128)(2,1)S(1)}, bf16[256,512]{1,0:T(8,128)(2,1)S(1)}, u32[]{:S(2)}, u32[]{:S(2)}) collective-permute-start(bf16[256,512]{1,0:T(8,128)(2,1)S(1)} %gate.9), channel_id=1, source_target_pairs={{0,3},{1,2},{2,1},{3,0},{4,7},{5,6},{6,5},{7,4},{8,11},{9,10},{10,... | collective-permute-start | bytes 786440 | tf_op jit(solution)/shard_map/ppermute | solution.py:449
  47.1 2.9 %collective-permute-start.17 = (bf16[512,512]{1,0:T(8,128)(2,1)S(1)}, bf16[512,512]{1,0:T(8,128)(2,1)S(1)}, u32[]{:S(2)}, u32[]{:S(2)}) collective-permute-start(bf16[512,512]{1,0:T(8,128)(2,1)S(1)} %gate.11), channel_id=1, source_target_pairs={{0,1},{1,0},{2,3},{3,2},{4,5},{5,4},{6,7},{7,6},{8,9},{9,8},{10,11... | collective-permute-start | bytes 1572872 | tf_op jit(solution)/shard_map/ppermute | solution.py:449
  47.1 3.7 %collective-permute-start.15 = (bf16[256,1024]{1,0:T(8,128)(2,1)S(1)}, bf16[256,1024]{1,0:T(8,128)(2,1)S(1)}, u32[]{:S(2)}, u32[]{:S(2)}) collective-permute-start(bf16[256,1024]{1,0:T(8,128)(2,1)S(1)} %gate.10.refs_4_), channel_id=1, source_target_pairs={{0,1},{1,0},{2,3},{3,2},{4,5},{5,4},{6,7},{7,6},{8,9},{9,8},{10,11... | collective-permute-start | bytes 1572872 | tf_op jit(solution)/shard_map/ppermute | solution.py:449

commit v6 on v5

--- a/solution.py
+++ b/solution.py
@@ -16,7 +16,8 @@
 
 SCALE = 8.0
 SHORT = 0.02
-LONG = 3
+YFIRST = True
+LONG = 3.0
 
 
 def cost(us):
@@ -247,6 +248,7 @@
                 parts.append(dot(weighted, v[: (i + 1) * LANES]))
             total = jnp.concatenate(parts, axis=0)
             first = 0
+            scales, states = [], []
             for b in range(bit_count(count)):
                 at = block_bits + 1 + b
                 scale = w[:, at : at + 1]
@@ -254,8 +256,13 @@
                 if b >= low:
                     scale = scale * ((share >> (b - low)) & 1).astype(jnp.float32)
                 if b >= low or (part >> b) & 1:
-                    total = total + dot(q, level_ref[first + (n >> (b + 1)), h]) * scale
+                    scales.append(scale)
+                    states.append(level_ref[first + (n >> (b + 1)), h])
                 first += count >> (b + 1)
+            if states:
+                reached = dot(q, jnp.concatenate(states, axis=1))
+                for i, scale in enumerate(scales):
+                    total = total + reached[:, i * size : (i + 1) * size] * scale
             out_ref[at_block * STRETCH : (at_block + 1) * STRETCH, cols] = total.astype(out_ref.dtype)
 
 
@@ -295,45 +302,99 @@
     return call(kernel, out_shape, "local_attention", us, 8, args, after)[0]
 
 
-def finish_kernel(
-    heads, size, first, remotes, offset, part, parts, blocks, row, q_ref, local_ref, index_ref, table_ref, *refs
-):
-    state_refs, out_ref = refs[:remotes], refs[remotes]
-    start = (lax.axis_index("mp") ^ offset) * parts + part
-    position = lax.axis_index("ctx")
-    for i in range(blocks):
-        block = pl.ds(pl.multiple_of((start + i) * STRETCH, STRETCH), STRETCH)
-        weights = spread_weights(index_ref[start + i], table_ref[...])
+def remote_rows(heads, size, first, bits, q, local, weights, state_refs, h):
+    cols = slice(h * size, (h + 1) * size)
+    w = weights[:, h * LANES : (h + 1) * LANES]
+    total = local.astype(jnp.float32)
+    for b, state_ref in zip(bits, state_refs):
+        inside = ((lax.axis_index("ctx") >> b) & 1).astype(jnp.float32)
+        total = total + dot(q, state_ref[cols, :]) * (w[:, first + b : first + b + 1] * inside)
+    return total
+
+
+def block_rows(offset, part, parts):
+    at = (lax.axis_index("mp") ^ offset) * parts + part
+    return at, pl.ds(pl.multiple_of(at * STRETCH, STRETCH), STRETCH)
+
+
+def begin_kernel(heads, size, first, bits, parts, blocks, q_ref, local_ref, index_ref, table_ref, *refs):
+    state_refs, (out_ref, weights_ref) = refs[: len(bits)], refs[len(bits) :]
+    for i, (offset, part) in enumerate(blocks):
+        at, block = block_rows(offset, part, parts)
+        rows = slice(i * STRETCH, (i + 1) * STRETCH)
+        weights = spread_weights(index_ref[at], table_ref[...])
+        weights_ref[rows, :] = weights
         for h in range(heads):
             cols = slice(h * size, (h + 1) * size)
-            q = q_ref[block, cols]
-            w = weights[:, h * LANES : (h + 1) * LANES]
-            total = local_ref[(row + i) * STRETCH : (row + i + 1) * STRETCH, cols].astype(jnp.float32)
-            for b in range(remotes):
-                inside = ((position >> b) & 1).astype(jnp.float32)
-                reached = dot(q, state_refs[b][cols, :])
-                total = total + reached * (w[:, first + b : first + b + 1] * inside)
+            out_ref[rows, cols] = remote_rows(
+                heads, size, first, bits, q_ref[block, cols], local_ref[rows, cols], weights,
+                state_refs, h,
+            )
+
+
+def begin_rows(after, parts, blocks, queries, local, index_rows, table, states, first, us):
+    size = states[0].shape[1]
+    heads = queries.shape[1] // size
+    rows = len(blocks) * STRETCH
+    return call(
+        functools.partial(begin_kernel, heads, size, first, range(len(states)), parts, blocks),
+        [
+            jax.ShapeDtypeStruct((rows, queries.shape[1]), jnp.float32),
+            jax.ShapeDtypeStruct((rows, heads * LANES), jnp.float32),
+        ],
+        "begin_rows",
+        us,
+        4,
+        [queries, local, index_rows, table, *states],
+        after,
+    )
+
+
+def finish_kernel(heads, size, first, bits, offset, part, parts, blocks, row, ready, *refs):
+    q_ref, local_ref, *refs = refs
+    given, refs = refs[: 2 - ready], refs[2 - ready :]
+    state_refs, out_refs = refs[: len(bits)], refs[len(bits) :]
+    for i in range(blocks):
+        at, block = block_rows(offset, part + i, parts)
+        rows = slice((row + i) * STRETCH, (row + i + 1) * STRETCH)
+        if ready:
+            weights = given[0][rows, :]
+        else:
+            weights = spread_weights(given[0][at], given[1][...])
+        for h in range(heads):
+            cols = slice(h * size, (h + 1) * size)
+            total = remote_rows(
+                heads, size, first, bits, q_ref[block, cols], local_ref[rows, cols], weights,
+                state_refs, h,
+            )
             scale = lax.rsqrt(jnp.mean(total * total, axis=1, keepdims=True) + EPSILON)
-            out_ref[i * STRETCH : (i + 1) * STRETCH, cols] = (total * scale).astype(out_ref.dtype)
-
-
-def finish_rows(after, offset, part, blocks, row, queries, local, index_rows, table, states, first):
+            normed = (total * scale).astype(out_refs[0].dtype)
+            low = 0
+            for out_ref in out_refs:
+                high = low + out_ref.shape[0]
+                begin, end = max(low, i * STRETCH), min(high, (i + 1) * STRETCH)
+                if begin < end:
+                    out_ref[begin - low : end - low, cols] = normed[
+                        begin - i * STRETCH : end - i * STRETCH
+                    ]
+                low = high
+
+
+def finish_rows(after, offset, part, blocks, row, queries, local, given, states, bits, size, first, cuts):
     tokens, width = queries.shape
-    size = states[0].shape[1]
-    heads = width // size
     parts = tokens // STRETCH // lax.axis_size("mp")
-    (out,) = call(
+    return call(
         functools.partial(
-            finish_kernel, heads, size, first, len(states), offset, part, parts, blocks, row
+            finish_kernel, width // size, size, first, bits, offset, part, parts, blocks, row,
+            len(given) == 1,
         ),
-        [jax.ShapeDtypeStruct((blocks * STRETCH, width), jnp.bfloat16)],
+        [jax.ShapeDtypeStruct((n, width), jnp.bfloat16) for n in cuts],
         "finish_rows",
         blocks,
         4,
-        [queries, local, index_rows, table, *states],
+        [queries, local, *given, *states],
         after,
     )
-    return out
 
 
 def split_refs(groups, refs):
@@ -343,11 +404,11 @@
     return a_refs, w_refs, refs
 
 
-def products(groups, a_refs, w_refs, cols, columns, part):
+def products(groups, a_refs, w_refs, cols, columns, run):
     total = None
     mine = lax.axis_index("ctx")
     for g, a_ref, chunks in zip(groups, a_refs, w_refs):
-        rows = slice(part * STRETCH, (part + 1) * STRETCH) if a_ref.shape[0] > STRETCH else slice(None)
+        rows = slice(None) if a_ref.shape[0] == run[1] - run[0] else slice(*run)
         width = columns // len(chunks)
         for place, ref in zip(g[cols // width], chunks[cols // width]):
             depth = ref.shape[0]
@@ -361,31 +422,31 @@
     return total
 
 
-def start_kernel(groups, *refs):
+def start_kernel(groups, runs, *refs):
     a_refs, w_refs, outs = split_refs(groups, refs)
     columns = outs[0].shape[1]
-    for part, out in enumerate(outs):
+    for run, out in zip(runs, outs):
         for cols in range(0, columns, TILE):
-            out[:, cols : cols + TILE] = products(groups, a_refs, w_refs, cols, columns, part)
-
-
-def add_kernel(groups, part, *refs):
+            out[:, cols : cols + TILE] = products(groups, a_refs, w_refs, cols, columns, run)
+
+
+def add_kernel(groups, run, *refs):
     a_refs, w_refs, (before, out) = split_refs(groups, refs)
     columns = out.shape[1]
     for cols in range(0, columns, TILE):
         tile = slice(cols, cols + TILE)
-        out[:, tile] = before[:, tile] + products(groups, a_refs, w_refs, cols, columns, part)
-
-
-def last_kernel(groups, part, *refs):
+        out[:, tile] = before[:, tile] + products(groups, a_refs, w_refs, cols, columns, run)
+
+
+def last_kernel(groups, run, *refs):
     a_refs, w_refs, rest = split_refs(groups, refs)
     before, (out, tile_ref, sem) = rest[0], rest[-3:]
     columns = out.shape[1]
     copies = []
     for i, cols in enumerate(range(0, columns, TILE)):
-        total = before[:, cols : cols + TILE] + products(groups, a_refs, w_refs, cols, columns, part)
+        total = before[:, cols : cols + TILE] + products(groups, a_refs, w_refs, cols, columns, run)
         tile_ref[i] = total.astype(tile_ref.dtype)
-        to = out.at[pl.ds(part * STRETCH, STRETCH), pl.ds(cols, TILE)]
+        to = out.at[pl.ds(run[0], run[1] - run[0]), pl.ds(cols, TILE)]
         copies.append(pltpu.make_async_copy(tile_ref.at[i], to, sem.at[i]))
         copies[-1].start()
     for copy in copies:
@@ -397,11 +458,11 @@
     return groups, [a for a, _ in pairs] + [w for _, g in pairs for chunk in g for _, w in chunk]
 
 
-def project_start(pairs, parts, columns, after):
+def project_start(pairs, runs, columns, after):
     groups, arrays = operands(pairs)
     return call(
-        functools.partial(start_kernel, groups),
-        [jax.ShapeDtypeStruct((STRETCH, columns), jnp.float32)] * parts,
+        functools.partial(start_kernel, groups, runs),
+        [jax.ShapeDtypeStruct((end - begin, columns), jnp.float32) for begin, end in runs],
         "project_start",
         2.4,
         6,
@@ -410,10 +471,10 @@
     )
 
 
-def project_add(pairs, before, part):
+def project_add(pairs, before, run):
     groups, arrays = operands(pairs)
     return call(
-        functools.partial(add_kernel, groups, part),
+        functools.partial(add_kernel, groups, run),
         [jax.ShapeDtypeStruct(before.shape, before.dtype)],
         "project_add",
         1,
@@ -423,13 +484,13 @@
     )[0]
 
 
-def project_last(pairs, before, out, part, parts):
+def project_last(pairs, before, out, run, rows):
     groups, arrays = operands(pairs)
     columns = before.shape[1]
     extra = [] if out is None else [out]
     return call(
-        functools.partial(last_kernel, groups, part),
-        [jax.ShapeDtypeStruct((parts * STRETCH, columns), jnp.bfloat16)],
+        functools.partial(last_kernel, groups, run),
+        [jax.ShapeDtypeStruct((rows, columns), jnp.bfloat16)],
         "project_last",
         1.5,
         8,
@@ -438,7 +499,7 @@
         anywhere_out=(0,),
         input_output_aliases={len(arrays) + 1: 0} if extra else {},
         scratch_shapes=[
-            pltpu.VMEM((columns // TILE, STRETCH, TILE), jnp.bfloat16),
+            pltpu.VMEM((columns // TILE, run[1] - run[0], TILE), jnp.bfloat16),
             pltpu.SemaphoreType.DMA((columns // TILE,)),
         ],
     )[0]
@@ -470,7 +531,7 @@
 
     portions = slice_weight(out_weight, [min(2, ctx_size), min(4, ctx_size)])
     evens = list(range(2, mp_size, 2))
-    got = {j: [flip(p, "mp", j) for p in portions] for j in evens}
+    got = {j: [flip(portions[0], "mp", j)] for j in evens}
 
     levels, own = block_states(key_vectors, value_vectors, heads, size, portions)
     near = [flip(own, "ctx", b) for b in range(1, min(4, ctx_size))]
@@ -501,29 +562,43 @@
     held = [gate(got[j][0], ready) for j in evens]
     for j, x in zip(evens, held):
         got[j][0] = x
-        over_pair[j] = flip(x, "mp", 1)
         if ctx_size > 1:
             there[j] = flip(x, "ctx", 1)
-    close = local_attention(args, parts, own_blocks, after=[ready] + held, us=SHORT)
-    done = [close]
-
-    def finished(j, part, blocks, local, places):
+    portion = gate(portions[1], ready, *held) if YFIRST else portions[1]
+    for j in evens:
+        got[j].append(flip(portion, "mp", j))
+        over_pair[j] = flip(got[j][0], "mp", 1)
+    early = min(2, ctx_bits)
+    all_bits = range(ctx_bits)
+    far_local, far_weights = begin_rows(
+        [ready] + held, parts, far_blocks, queries, local, index_rows, terms, remote[:early], first,
+        SHORT,
+    )
+    done = [far_local]
+
+    def finished(j, part, blocks, local, places, cuts=None):
         nonlocal done
+        if places is far_blocks:
+            given, states, bits = [far_weights], remote[early:], all_bits[early:]
+        else:
+            given, states, bits = [index_rows, terms], remote, all_bits
         out = finish_rows(
-            done, j, part, blocks, places.index((j, part)), queries, local, index_rows, terms,
-            remote, first,
+            done, j, part, blocks, places.index((j, part)), queries, local, given, states, bits,
+            size, first, cuts or [blocks * STRETCH],
         )
-        done = [out]
-        return out
+        done = list(out)
+        return out if cuts else out[0]
 
     received = {}
     for j in far_groups[:-1]:
-        received[j] = [flip(finished(j, 0, parts, local, far_blocks), "mp", j)] * parts
+        received[j] = [flip(finished(j, 0, parts, far_local, far_blocks), "mp", j)]
     done += list(over_pair.values())
     last = far_groups[-1]
-    received[last] = [
-        flip(finished(last, part, 1, local, far_blocks), "mp", last) for part in range(parts - 1)
-    ]
+    rows = parts * STRETCH
+    tail = 3 * STRETCH // 4
+    runs = [(0, rows - tail), (rows - tail, rows)]
+    ahead, final = finished(last, 0, parts, far_local, far_blocks, cuts=[rows - tail, tail])
+    received[last] = [flip(ahead, "mp", last)]
     beside = local_attention(args, parts, mate_blocks, after=done, us=SHORT)
     done = [beside]
     for j in there:
@@ -535,11 +610,13 @@
         pieces[j] = [x] + [flip(x, "ctx", b) for b in range(1, min(4, ctx_size))]
         done.append(x)
 
-    final = finished(last, parts - 1, 1, local, far_blocks)
     theirs = finished(1, 0, parts, beside, mate_blocks)
+    close = local_attention(args, parts, own_blocks, after=done, us=SHORT)
     mine = finished(0, 0, parts, close, own_blocks)
 
-    over = done + [x for xs in received.values() for x in xs]
+    totals = project_start([(mine, [[(0, weight)]])], runs, columns, done)
+
+    over = list(totals) + [x for xs in received.values() for x in xs]
     for j in evens:
         pieces[j] = assemble(pieces[j], over)
         over.append(pieces[j])
@@ -554,20 +631,19 @@
             gathered[j][0].append((1, x))
             gathered[j + 1][0].append((1, flip(x, "mp", 1)))
 
-    early = [(mine, [[(0, weight)]])]
-    early += [(received[j][0], gathered[j]) for j in far_groups[:-1] if j % 2 == 0]
-    late = [(j, gathered[j]) for j in far_groups[:-1] if j % 2]
-    totals = project_start(early, parts, columns, over)
-    out = None
-    for part in range(parts):
-        total = totals[part]
-        pairs = [(theirs, [[(0, mate)]])]
-        pairs += [(received[j][part], w) for j, w in late + [(last, gathered[last])]]
-        if part + 1 == parts:
-            total = project_add(pairs[:-1], total, part)
-            pairs = pairs[-1:]
-        out = project_last(pairs, total, out, part, parts)
-    return out
+    straight = [(received[j][0], gathered[j]) for j in far_groups[:-1] if j % 2 == 0]
+    crossed = [(received[j][0], gathered[j]) for j in far_groups[:-1] if j % 2]
+    mates = [(theirs, [[(0, mate)]])]
+    totals = [
+        project_add(straight, totals[0], runs[0]),
+        project_add(straight + mates, totals[1], runs[1]),
+    ]
+    out = project_last(
+        mates + crossed + [(received[last][0], gathered[last])], totals[0], None, runs[0], rows
+    )
+    if crossed:
+        totals[1] = project_add(crossed, totals[1], runs[1])
+    return project_last([(received[last][1], gathered[last])], totals[1], out, runs[1], rows)
 
 
 def solution(mesh):

time: 55.4 us -> 54.7 us (0.987)
    pallas_call x22 -> x24, Pallas kernels: 26.1 us -> 26.1 us  [call(): pl.pallas_call(run, in_specs=[anywhere if i in anywhere_in else vmem for...]
  transfers between devices with their start and end apart: 18 -> 18, of which waited for: 7 -> 5; matrix products, arithmetic and copies ran while one was open for 0% -> 0% of each run, Pallas kernels for 44% -> 45%
where the time goes in v6:
time: 54.7 us; the launch traced here: 54.6 us
  Pallas kernels  26.1 us (48%)
  starting transfers between devices  18.2 us (33%)
  waiting for transfers between devices  8.2 us (15%)
  local copies, waits for them, and re-layouts  1.77 us (3%)
    pallas_call x24, Pallas kernels, call(): pl.pallas_call(run, in_specs=[anywhere if i in anywhere_in else vmem for...  26.1 us
    ppermute x18, starting transfers between devices, flip(): return lax.ppermute(x, axis, [(i, i ^ bits) for i in range(n)])  18.2 us
    ppermute x18, waiting for transfers between devices, flip(): return lax.ppermute(x, axis, [(i, i ^ bits) for i in range(n)])  8.2 us
    unnamed x14, local copies, waits for them, and re-layouts  1.77 us
  transfers between devices with their start and end apart: 18, of which 5 were waited for; matrix products, arithmetic and copies ran while one was open for 0% of the time, Pallas kernels for 45%

profile of v6, /device:TPU:0, one launch (start us, length us, event | category | flops | bytes accessed | tf_op | source)
XLA Modules:
  0.0 54.6 jit_solution(2539647748578801269)
XLA Ops:
  0.0 0.0 copy-start.2
  0.0 0.0 copy-start.1
  0.0 1.7 %copy-done.4 = bf16[512,2048]{1,0:T(8,128)(2,1)S(1)} copy-done((bf16[512,2048]{1,0:T(8,128)(2,1)S(1)}, bf16[512,2048]{1,0:T(8,128)(2,1)}, u32[]{:S(2)}) %copy-start.4) | copy-done | bytes 2097176
  1.7 0.1 slice_weight.1
  1.8 3.0 %collective-permute-start.4 = (bf16[256,1024]{1,0:T(8,128)(2,1)S(1)}, bf16[256,1024]{1,0:T(8,128)(2,1)S(1)}, u32[]{:S(2)}, u32[]{:S(2)}) collective-permute-start(bf16[256,1024]{1,0:T(8,128)(2,1)S(1)} %get-tuple-element.20.refs_2_), channel_id=1, source_target_pairs={{0,2},{1,3},{2,0},{3,1},{4,6},{5,7},{6,4},{7,5},{8,10},{9,11},{10,... | collective-permute-start | bytes 1572872 | tf_op jit(solution)/shard_map/ppermute | solution.py:510
  4.8 0.0 copy-done.2
  4.8 0.0 copy-done.1
  4.9 0.0 copy-start.3
  4.9 0.0 copy-start.6
  4.9 0.8 %block_states.1 = (bf16[7,4,128,128]{3,2,1,0:T(8,128)(2,1)S(1)}, bf16[512,128]{1,0:T(8,128)(2,1)S(1)}) custom-call(bf16[2048,512]{1,0:T(8,128)(2,1)S(1)} %copy-done.1, bf16[2048,512]{1,0:T(8,128)(2,1)S(1)} %copy-done.2, bf16[256,1024]{1,0:T(8,128)(2,1)S(1)} %get-tuple-element.20.refs_2_, bf16[128,1024]{1,0:T(8,128)(2,1)S(1)} %get-tuple-element.21.refs_3_.refs_0_), custom_call_target="tpu_custom_call" | custom-call | flops 8000000000 | bytes 24000000 | tf_op jit(solution)/shard_map/block_states/pallas_call | solution.py:37
  5.7 2.6 %collective-permute-start.2 = (bf16[512,128]{1,0:T(8,128)(2,1)S(1)}, bf16[512,128]{1,0:T(8,128)(2,1)S(1)}, u32[]{:S(2)}, u32[]{:S(2)}) collective-permute-start(bf16[512,128]{1,0:T(8,128)(2,1)S(1)} %get-tuple-element.23.refs_7_.refs_0_), channel_id=1, source_target_pairs={{0,12},{4,8},{8,4},{12,0},{16,28},{20,24},{24,20},{28,16},{1,13},{... | collective-permute-start | bytes 393224 | tf_op jit(solution)/shard_map/ppermute | solution.py:510
  8.3 0.5 collective-permute-start.1
  8.7 0.5 collective-permute-start
  9.2 0.0 copy-done.5
  9.2 0.0 collective-permute-start.3
  9.2 0.0 copy-done
  9.2 0.0 copy-done.3
  9.3 0.0 copy-done.6
  9.3 4.8 %local_attention.3 = (bf16[1024,512]{1,0:T(8,128)(2,1)S(1)}, bf16[512,2048]{1,0:T(8,128)(2,1)S(1)}, bf16[48,512]{1,0:T(8,128)(2,1)S(1)}) custom-call(bf16[512,2048]{1,0:T(8,128)(2,1)S(1)} %copy-done.5, bf16[2048,512]{1,0:T(8,128)(2,1)S(1)} %copy-done, bf16[2048,512]{1,0:T(8,128)(2,1)S(1)} %copy-done.1, bf16[2048,512]{1,0:T(8,128)(2,1)S(1)} %copy-done.2, ...), custom_call_target="tpu_custom_call" | custom-call | flops 32000000000 | bytes 96000000 | tf_op jit(solution)/shard_map/local_attention/pallas_call | solution.py:37
  14.1 0.0 collective-permute-done.2.refs_3_
  14.1 0.4 collective-permute-done.1.refs_2_
  14.5 0.0 collective-permute-done.refs_1_.refs_4_
  14.5 0.0 collective-permute-done.3.refs_5_.refs_2_
  14.5 0.1 merge_states.1
  14.6 2.7 %collective-permute-start.5 = (bf16[512,128]{1,0:T(8,128)(2,1)S(1)}, bf16[512,128]{1,0:T(8,128)(2,1)S(1)}, u32[]{:S(2)}, u32[]{:S(2)}) collective-permute-start(bf16[512,128]{1,0:T(8,128)(2,1)S(1)} %get-tuple-element.27.refs_1_.refs_6_), channel_id=1, source_target_pairs={{0,16},{4,20},{8,24},{12,28},{16,0},{20,4},{24,8},{28,12},{1,17},{... | collective-permute-start | bytes 393224 | tf_op jit(solution)/shard_map/ppermute | solution.py:510
  17.2 0.0 collective-permute-done.4.refs_0_
  17.2 1.4 %collective-permute-start.7 = (bf16[256,1024]{1,0:T(8,128)(2,1)S(1)}, bf16[256,1024]{1,0:T(8,128)(2,1)S(1)}, u32[]{:S(2)}, u32[]{:S(2)}) collective-permute-start(bf16[256,1024]{1,0:T(8,128)(2,1)S(1)} %gate.7.refs_7_.refs_2_.refs_1_), channel_id=1, source_target_pairs={{0,4},{4,0},{8,12},{12,8},{16,20},{20,16},{24,28},{28,24},{1,5},{5... | collective-permute-start | bytes 1572872 | tf_op jit(solution)/shard_map/ppermute | solution.py:510
  18.7 0.0 collective-permute-start.6
  18.7 1.4 %collective-permute-start.8 = (bf16[128,1024]{1,0:T(8,128)(2,1)S(1)}, bf16[128,1024]{1,0:T(8,128)(2,1)S(1)}, u32[]{:S(2)}, u32[]{:S(2)}) collective-permute-start(bf16[128,1024]{1,0:T(8,128)(2,1)S(1)} %gate.9), channel_id=1, source_target_pairs={{0,2},{1,3},{2,0},{3,1},{4,6},{5,7},{6,4},{7,5},{8,10},{9,11},{10,... | collective-permute-start | bytes 786440 | tf_op jit(solution)/shard_map/ppermute | solution.py:510
  20.0 1.5 %begin_rows.1 = (f32[1024,512]{1,0:T(8,128)S(1)}, f32[1024,512]{1,0:T(8,128)S(1)}) custom-call(bf16[2048,512]{1,0:T(8,128)(2,1)S(1)} %copy-done, bf16[1024,512]{1,0:T(8,128)(2,1)S(1)} %get-tuple-element.24.refs_4_.refs_1_, s32[8,1,256]{2,1,0:T(1,128)S(1)} %bitcast.2, bf16[48,512]{1,0:T(8,128)(2,1)S(1)} %get-tuple-element.25.refs_3_.refs_4_, ...), custom_call_target="tpu_custom_call" | custom-call | flops 160000000 | bytes 480000 | tf_op jit(solution)/shard_map/begin_rows/pallas_call | solution.py:37
  21.6 2.3 %collective-permute-done.5.refs_3_.refs_6_ = bf16[512,128]{1,0:T(8,128)(2,1)S(1)} collective-permute-done((bf16[512,128]{1,0:T(8,128)(2,1)S(1)}, bf16[512,128]{1,0:T(8,128)(2,1)S(1)}, u32[]{:S(2)}, u32[]{:S(2)}) %collective-permute-start.5) | collective-permute-done | bytes 131104 | tf_op jit(solution)/shard_map/ppermute | solution.py:510
  23.9 1.5 %finish_rows.4.refs_4_ = bf16[512,512]{1,0:T(8,128)(2,1)S(1)} custom-call(bf16[2048,512]{1,0:T(8,128)(2,1)S(1)} %copy-done, f32[1024,512]{1,0:T(8,128)S(1)} %get-tuple-element.28.refs_1_.refs_4_, f32[1024,512]{1,0:T(8,128)S(1)} %get-tuple-element.29.refs_2_, bf16[512,128]{1,0:T(8,128)(2,1)S(1)} %collective-permute-done.5.refs_3_.refs_6_, ...), custom_call_target="tpu_custom_call" | custom-call | flops 16000000000 | bytes 48000000 | tf_op jit(solution)/shard_map/finish_rows/pallas_call | solution.py:37
  25.3 1.0 %collective-permute-start.9 = (bf16[512,512]{1,0:T(8,128)(2,1)S(1)}, bf16[512,512]{1,0:T(8,128)(2,1)S(1)}, u32[]{:S(2)}, u32[]{:S(2)}) collective-permute-start(bf16[512,512]{1,0:T(8,128)(2,1)S(1)} %finish_rows.4.refs_4_), channel_id=1, source_target_pairs={{0,2},{1,3},{2,0},{3,1},{4,6},{5,7},{6,4},{7,5},{8,10},{9,11},{10,... | collective-permute-start | bytes 1572872 | tf_op jit(solution)/shard_map/ppermute | solution.py:510
  26.3 0.0 collective-permute-done.6.refs_5_.refs_3_.refs_1_
  26.3 1.5 %finish_rows.5 = (bf16[320,512]{1,0:T(8,128)(2,1)S(1)}, bf16[192,512]{1,0:T(8,128)(2,1)S(1)}) custom-call(bf16[2048,512]{1,0:T(8,128)(2,1)S(1)} %copy-done, f32[1024,512]{1,0:T(8,128)S(1)} %get-tuple-element.28.refs_1_.refs_4_, f32[1024,512]{1,0:T(8,128)S(1)} %get-tuple-element.29.refs_2_, bf16[512,128]{1,0:T(8,128)(2,1)S(1)} %collective-permute-done.5.refs_3_.refs_6_, ...), custom_call_target="tpu_custom_call" | custom-call | flops 16000000000 | bytes 48000000 | tf_op jit(solution)/shard_map/finish_rows/pallas_call | solution.py:37
  27.8 0.1 collective-permute-start.10
  27.9 2.0 %local_attention.4.refs_1_.refs_7_ = bf16[512,512]{1,0:T(8,128)(2,1)S(1)} custom-call(bf16[2048,512]{1,0:T(8,128)(2,1)S(1)} %copy-done, bf16[2048,512]{1,0:T(8,128)(2,1)S(1)} %copy-done.1, bf16[2048,512]{1,0:T(8,128)(2,1)S(1)} %copy-done.2, s32[8,1,256]{2,1,0:T(1,128)S(1)} %bitcast.3, bf16[48,512]{1,0:T(8,128)(2,1)S(1)} %get-tuple-element.25.refs_3_.refs_4_, ...), custom_call_target="tpu_custom_call" | custom-call | flops 160000000 | bytes 480000 | tf_op jit(solution)/shard_map/local_attention/pallas_call | solution.py:37
  29.9 1.0 %collective-permute-done.7.refs_0_ = bf16[256,1024]{1,0:T(8,128)(2,1)S(1)} collective-permute-done((bf16[256,1024]{1,0:T(8,128)(2,1)S(1)}, bf16[256,1024]{1,0:T(8,128)(2,1)S(1)}, u32[]{:S(2)}, u32[]{:S(2)}) %collective-permute-start.7) | collective-permute-done | bytes 524320 | tf_op jit(solution)/shard_map/ppermute | solution.py:510
  30.9 0.0 collective-permute-done.8.refs_0_
  30.9 2.5 %collective-permute-start.13 = (bf16[128,1024]{1,0:T(8,128)(2,1)S(1)}, bf16[128,1024]{1,0:T(8,128)(2,1)S(1)}, u32[]{:S(2)}, u32[]{:S(2)}) collective-permute-start(bf16[128,1024]{1,0:T(8,128)(2,1)S(1)} %gate.10.refs_9_.refs_0_), channel_id=1, source_target_pairs={{0,12},{4,8},{8,4},{12,0},{16,28},{20,24},{24,20},{28,16},{1,13},{... | collective-permute-start | bytes 786440 | tf_op jit(solution)/shard_map/ppermute | solution.py:510
  33.4 0.4 collective-permute-start.12
  33.9 0.5 collective-permute-start.11
  34.4 2.4 %finish_rows.6.refs_6_.refs_7_.refs_0_ = bf16[512,512]{1,0:T(8,128)(2,1)S(1)} custom-call(bf16[2048,512]{1,0:T(8,128)(2,1)S(1)} %copy-done, bf16[512,512]{1,0:T(8,128)(2,1)S(1)} %local_attention.4.refs_1_.refs_7_, s32[8,1,256]{2,1,0:T(1,128)S(1)} %bitcast.4, bf16[48,512]{1,0:T(8,128)(2,1)S(1)} %get-tuple-element.25.refs_3_.refs_4_, ...), custom_call_target="tpu_custom_call" | custom-call | flops 16000000000 | bytes 48000000 | tf_op jit(solution)/shard_map/finish_rows/pallas_call | solution.py:37
  36.8 2.0 %local_attention.5.refs_1_ = bf16[512,512]{1,0:T(8,128)(2,1)S(1)} custom-call(bf16[2048,512]{1,0:T(8,128)(2,1)S(1)} %copy-done, bf16[2048,512]{1,0:T(8,128)(2,1)S(1)} %copy-done.1, bf16[2048,512]{1,0:T(8,128)(2,1)S(1)} %copy-done.2, s32[8,1,256]{2,1,0:T(1,128)S(1)} %bitcast.5, bf16[48,512]{1,0:T(8,128)(2,1)S(1)} %get-tuple-element.25.refs_3_.refs_4_, ...), custom_call_target="tpu_custom_call" | custom-call | flops 160000000 | bytes 480000 | tf_op jit(solution)/shard_map/local_attention/pallas_call | solution.py:37
  38.9 2.3 %finish_rows.7.refs_0_.refs_2_ = bf16[512,512]{1,0:T(8,128)(2,1)S(1)} custom-call(bf16[2048,512]{1,0:T(8,128)(2,1)S(1)} %copy-done, bf16[512,512]{1,0:T(8,128)(2,1)S(1)} %local_attention.5.refs_1_, s32[8,1,256]{2,1,0:T(1,128)S(1)} %bitcast.6, bf16[48,512]{1,0:T(8,128)(2,1)S(1)} %get-tuple-element.25.refs_3_.refs_4_, ...), custom_call_target="tpu_custom_call" | custom-call | flops 16000000000 | bytes 48000000 | tf_op jit(solution)/shard_map/finish_rows/pallas_call | solution.py:37
  41.2 1.3 %project_start.1 = (f32[320,2048]{1,0:T(8,128)S(1)}, f32[192,2048]{1,0:T(8,128)S(1)}) custom-call(bf16[512,512]{1,0:T(8,128)(2,1)S(1)} %finish_rows.7.refs_0_.refs_2_, bf16[512,2048]{1,0:T(8,128)(2,1)S(1)} %get-tuple-element.32.refs_1_, bf16[512,512]{1,0:T(8,128)(2,1)S(1)} %finish_rows.7.refs_0_.refs_2_), custom_call_target="tpu_custom_call" | custom-call | flops 19200000000 | bytes 57600000 | tf_op jit(solution)/shard_map/project_start/pallas_call | solution.py:37
  42.4 0.0 collective-permute-done.9.refs_6_.refs_3_.refs_0_
  42.4 0.0 collective-permute-done.13.refs_3_
  42.4 3.6 %collective-permute-done.12.refs_2_ = bf16[128,1024]{1,0:T(8,128)(2,1)S(1)} collective-permute-done((bf16[128,1024]{1,0:T(8,128)(2,1)S(1)}, bf16[128,1024]{1,0:T(8,128)(2,1)S(1)}, u32[]{:S(2)}, u32[]{:S(2)}) %collective-permute-start.12) | collective-permute-done | bytes 262176 | tf_op jit(solution)/shard_map/ppermute | solution.py:510
  46.1 0.0 collective-permute-done.11.refs_1_
  46.1 0.0 collective-permute-done.10.refs_7_.refs_4_.refs_1_
  46.1 0.1 assemble.1.refs_5_.refs_4_.refs_3_
  46.2 0.1 collective-permute-start.16
  46.2 1.0 %collective-permute-start.14 = (bf16[192,512]{1,0:T(8,128)(2,1)S(1)}, bf16[192,512]{1,0:T(8,128)(2,1)S(1)}, u32[]{:S(2)}, u32[]{:S(2)}) collective-permute-start(bf16[192,512]{1,0:T(8,128)(2,1)S(1)} %gate.11), channel_id=1, source_target_pairs={{0,3},{1,2},{2,1},{3,0},{4,7},{5,6},{6,5},{7,4},{8,11},{9,10},{10,... | collective-permute-start | bytes 589832 | tf_op jit(solution)/shard_map/ppermute | solution.py:510
  47.3 0.1 collective-permute-start.17
  47.4 0.4 collective-permute-start.15
  47.8 1.0 %project_add.3.refs_6_ = f32[320,2048]{1,0:T(8,128)S(1)} custom-call(bf16[512,512]{1,0:T(8,128)(2,1)S(1)} %collective-permute-done.9.refs_6_.refs_3_.refs_0_, bf16[256,1024]{1,0:T(8,128)(2,1)S(1)} %gate.7.refs_7_.refs_2_.refs_1_, bf16[256,1024]{1,0:T(8,128)(2,1)S(1)} %gate.12.refs_3_.refs_2_, ...), custom_call_target="tpu_custom_call", output_to_operand_aliasing={{}: (4, {})} | custom-call | flops 8000000000 | bytes 24000000 | tf_op jit(solution)/shard_map/project_add/pallas_call | solution.py:37
  48.8 0.8 %collective-permute-done.17.refs_1_.refs_0_ = bf16[512,512]{1,0:T(8,128)(2,1)S(1)} collective-permute-done((bf16[512,512]{1,0:T(8,128)(2,1)S(1)}, bf16[512,512]{1,0:T(8,128)(2,1)S(1)}, u32[]{:S(2)}, u32[]{:S(2)}) %collective-permute-start.17) | collective-permute-done | bytes 524320 | tf_op jit(solution)/shard_map/ppermute | solution.py:510
  49.6 1.1 %project_add.2.refs_4_ = f32[192,2048]{1,0:T(8,128)S(1)} custom-call(bf16[512,512]{1,0:T(8,128)(2,1)S(1)} %collective-permute-done.9.refs_6_.refs_3_.refs_0_, bf16[512,512]{1,0:T(8,128)(2,1)S(1)} %collective-permute-done.17.refs_1_.refs_0_, bf16[256,1024]{1,0:T(8,128)(2,1)S(1)} %gate.7.refs_7_.refs_2_.refs_1_, ...), custom_call_target="tpu_custom_call", output_to_operand_aliasing={{}: (6, {})} | custom-call | flops 8000000000 | bytes 24000000 | tf_op jit(solution)/shard_map/project_add/pallas_call | solution.py:37
  50.8 0.0 collective-permute-done.15.refs_4_.refs_2_
  50.8 0.0 collective-permute-done.16.refs_5_.refs_3_
  50.8 2.3 %project_last.2.refs_5_ = bf16[512,2048]{1,0:T(8,128)(2,1)} custom-call(bf16[512,512]{1,0:T(8,128)(2,1)S(1)} %collective-permute-done.17.refs_1_.refs_0_, bf16[320,512]{1,0:T(8,128)(2,1)S(1)} %collective-permute-done.10.refs_7_.refs_4_.refs_1_, bf16[512,2048]{1,0:T(8,128)(2,1)S(1)} %collective-permute-done.3.refs_5_.refs_2_, ...), custom_call_target="tpu_custom_call" | custom-call | flops 12000000000 | bytes 36000000 | tf_op jit(solution)/shard_map/project_last/pallas_call | solution.py:37
  53.1 0.0 collective-permute-done.14.refs_0_
  53.1 1.3 %project_last.3 = bf16[512,2048]{1,0:T(8,128)(2,1)} custom-call(bf16[192,512]{1,0:T(8,128)(2,1)S(1)} %collective-permute-done.14.refs_0_, bf16[256,1024]{1,0:T(8,128)(2,1)S(1)} %collective-permute-done.6.refs_5_.refs_3_.refs_1_, bf16[256,1024]{1,0:T(8,128)(2,1)S(1)} %collective-permute-done.15.refs_4_.refs_2_, ...), custom_call_target="tpu_custom_call", output_to_operand_aliasing={{}: (5, {})} | custom-call | flops 12000000000 | bytes 36000000 | tf_op jit(solution)/shard_map/project_last/pallas_call | solution.py:37
  (10 shorter events, 0.0 us)
Async XLA Ops:
  0.0 4.8 %copy-start.2 = (bf16[2048,512]{1,0:T(8,128)(2,1)S(1)}, bf16[2048,512]{1,0:T(8,128)(2,1)}, u32[]{:S(2)}) copy-start(bf16[2048,512]{1,0:T(8,128)(2,1)} %refs_2_.5) | copy-start | bytes 6291460
  0.0 4.8 %copy-start.1 = (bf16[2048,512]{1,0:T(8,128)(2,1)S(1)}, bf16[2048,512]{1,0:T(8,128)(2,1)}, u32[]{:S(2)}) copy-start(bf16[2048,512]{1,0:T(8,128)(2,1)} %refs_1_.7) | copy-start | bytes 6291460
  0.0 1.7 %copy-start.4 = (bf16[512,2048]{1,0:T(8,128)(2,1)S(1)}, bf16[512,2048]{1,0:T(8,128)(2,1)}, u32[]{:S(2)}) copy-start(bf16[512,2048]{1,0:T(8,128)(2,1)} %refs_0_.12) | copy-start | bytes 6291460
  1.8 15.4 %collective-permute-start.4 = (bf16[256,1024]{1,0:T(8,128)(2,1)S(1)}, bf16[256,1024]{1,0:T(8,128)(2,1)S(1)}, u32[]{:S(2)}, u32[]{:S(2)}) collective-permute-start(bf16[256,1024]{1,0:T(8,128)(2,1)S(1)} %get-tuple-element.20.refs_2_), channel_id=1, source_target_pairs={{0,2},{1,3},{2,0},{3,1},{4,6},{5,7},{6,4},{7,5},{8,10},{9,11},{10,... | collective-permute-start | bytes 1572872 | tf_op jit(solution)/shard_map/ppermute | solution.py:510
  4.8 4.4 %copy-start.5 = (bf16[512,2048]{1,0:T(8,128)(2,1)S(1)}, bf16[512,2048]{1,0:T(8,128)(2,1)}, u32[]{:S(2)}) copy-start(bf16[512,2048]{1,0:T(8,128)(2,1)} %refs_0_.12) | copy-start | bytes 6291460
  4.9 4.4 %copy-start = (bf16[2048,512]{1,0:T(8,128)(2,1)S(1)}, bf16[2048,512]{1,0:T(8,128)(2,1)}, u32[]{:S(2)}) copy-start(bf16[2048,512]{1,0:T(8,128)(2,1)} %refs_0_.19) | copy-start | bytes 6291460
  4.9 4.4 %copy-start.3 = (s32[2048]{0:T(1024)S(1)}, s32[2048]{0:T(1024)}, u32[]{:S(2)}) copy-start(s32[2048]{0:T(1024)} %param.9) | copy-start | bytes 24580
  4.9 4.4 %copy-start.6 = (f32[16,4,20]{2,1,0:T(4,128)S(1)}, f32[16,4,20]{2,1,0:T(4,128)}, u32[]{:S(2)}) copy-start(f32[16,4,20]{2,1,0:T(4,128)} %refs_5_.1) | copy-start | bytes 15364
  5.7 8.4 %collective-permute-start.2 = (bf16[512,128]{1,0:T(8,128)(2,1)S(1)}, bf16[512,128]{1,0:T(8,128)(2,1)S(1)}, u32[]{:S(2)}, u32[]{:S(2)}) collective-permute-start(bf16[512,128]{1,0:T(8,128)(2,1)S(1)} %get-tuple-element.23.refs_7_.refs_0_), channel_id=1, source_target_pairs={{0,12},{4,8},{8,4},{12,0},{16,28},{20,24},{24,20},{28,16},{1,13},{... | collective-permute-start | bytes 393224 | tf_op jit(solution)/shard_map/ppermute | solution.py:510
  8.3 6.2 %collective-permute-start.1 = (bf16[512,128]{1,0:T(8,128)(2,1)S(1)}, bf16[512,128]{1,0:T(8,128)(2,1)S(1)}, u32[]{:S(2)}, u32[]{:S(2)}) collective-permute-start(bf16[512,128]{1,0:T(8,128)(2,1)S(1)} %get-tuple-element.23.refs_7_.refs_0_), channel_id=1, source_target_pairs={{0,8},{4,12},{8,0},{12,4},{16,24},{20,28},{24,16},{28,20},{1,9},{5... | collective-permute-start | bytes 393224 | tf_op jit(solution)/shard_map/ppermute | solution.py:510
  8.7 5.8 %collective-permute-start = (bf16[512,128]{1,0:T(8,128)(2,1)S(1)}, bf16[512,128]{1,0:T(8,128)(2,1)S(1)}, u32[]{:S(2)}, u32[]{:S(2)}) collective-permute-start(bf16[512,128]{1,0:T(8,128)(2,1)S(1)} %get-tuple-element.23.refs_7_.refs_0_), channel_id=1, source_target_pairs={{0,4},{4,0},{8,12},{12,8},{16,20},{20,16},{24,28},{28,24},{1,5},{5... | collective-permute-start | bytes 393224 | tf_op jit(solution)/shard_map/ppermute | solution.py:510
  9.2 5.3 %collective-permute-start.3 = (bf16[512,2048]{1,0:T(8,128)(2,1)S(1)}, bf16[512,2048]{1,0:T(8,128)(2,1)S(1)}, u32[]{:S(2)}, u32[]{:S(2)}) collective-permute-start(bf16[512,2048]{1,0:T(8,128)(2,1)S(1)} %copy-done.5), channel_id=1, source_target_pairs={{0,1},{1,0},{2,3},{3,2},{4,5},{5,4},{6,7},{7,6},{8,9},{9,8},{10,11... | collective-permute-start | bytes 6291464 | tf_op jit(solution)/shard_map/ppermute | solution.py:510
  14.6 9.3 %collective-permute-start.5 = (bf16[512,128]{1,0:T(8,128)(2,1)S(1)}, bf16[512,128]{1,0:T(8,128)(2,1)S(1)}, u32[]{:S(2)}, u32[]{:S(2)}) collective-permute-start(bf16[512,128]{1,0:T(8,128)(2,1)S(1)} %get-tuple-element.27.refs_1_.refs_6_), channel_id=1, source_target_pairs={{0,16},{4,20},{8,24},{12,28},{16,0},{20,4},{24,8},{28,12},{1,17},{... | collective-permute-start | bytes 393224 | tf_op jit(solution)/shard_map/ppermute | solution.py:510
  17.2 13.7 %collective-permute-start.7 = (bf16[256,1024]{1,0:T(8,128)(2,1)S(1)}, bf16[256,1024]{1,0:T(8,128)(2,1)S(1)}, u32[]{:S(2)}, u32[]{:S(2)}) collective-permute-start(bf16[256,1024]{1,0:T(8,128)(2,1)S(1)} %gate.7.refs_7_.refs_2_.refs_1_), channel_id=1, source_target_pairs={{0,4},{4,0},{8,12},{12,8},{16,20},{20,16},{24,28},{28,24},{1,5},{5... | collective-permute-start | bytes 1572872 | tf_op jit(solution)/shard_map/ppermute | solution.py:510
  18.7 7.7 %collective-permute-start.6 = (bf16[256,1024]{1,0:T(8,128)(2,1)S(1)}, bf16[256,1024]{1,0:T(8,128)(2,1)S(1)}, u32[]{:S(2)}, u32[]{:S(2)}) collective-permute-start(bf16[256,1024]{1,0:T(8,128)(2,1)S(1)} %gate.7.refs_7_.refs_2_.refs_1_), channel_id=1, source_target_pairs={{0,1},{1,0},{2,3},{3,2},{4,5},{5,4},{6,7},{7,6},{8,9},{9,8},{10,11... | collective-permute-start | bytes 1572872 | tf_op jit(solution)/shard_map/ppermute | solution.py:510
  18.7 12.2 %collective-permute-start.8 = (bf16[128,1024]{1,0:T(8,128)(2,1)S(1)}, bf16[128,1024]{1,0:T(8,128)(2,1)S(1)}, u32[]{:S(2)}, u32[]{:S(2)}) collective-permute-start(bf16[128,1024]{1,0:T(8,128)(2,1)S(1)} %gate.9), channel_id=1, source_target_pairs={{0,2},{1,3},{2,0},{3,1},{4,6},{5,7},{6,4},{7,5},{8,10},{9,11},{10,... | collective-permute-start | bytes 786440 | tf_op jit(solution)/shard_map/ppermute | solution.py:510
  25.3 17.1 %collective-permute-start.9 = (bf16[512,512]{1,0:T(8,128)(2,1)S(1)}, bf16[512,512]{1,0:T(8,128)(2,1)S(1)}, u32[]{:S(2)}, u32[]{:S(2)}) collective-permute-start(bf16[512,512]{1,0:T(8,128)(2,1)S(1)} %finish_rows.4.refs_4_), channel_id=1, source_target_pairs={{0,2},{1,3},{2,0},{3,1},{4,6},{5,7},{6,4},{7,5},{8,10},{9,11},{10,... | collective-permute-start | bytes 1572872 | tf_op jit(solution)/shard_map/ppermute | solution.py:510
  27.8 18.3 %collective-permute-start.10 = (bf16[320,512]{1,0:T(8,128)(2,1)S(1)}, bf16[320,512]{1,0:T(8,128)(2,1)S(1)}, u32[]{:S(2)}, u32[]{:S(2)}) collective-permute-start(bf16[320,512]{1,0:T(8,128)(2,1)S(1)} %get-tuple-element.31.refs_6_), channel_id=1, source_target_pairs={{0,3},{1,2},{2,1},{3,0},{4,7},{5,6},{6,5},{7,4},{8,11},{9,10},{10,... | collective-permute-start | bytes 983048 | tf_op jit(solution)/shard_map/ppermute | solution.py:510
  30.9 11.5 %collective-permute-start.13 = (bf16[128,1024]{1,0:T(8,128)(2,1)S(1)}, bf16[128,1024]{1,0:T(8,128)(2,1)S(1)}, u32[]{:S(2)}, u32[]{:S(2)}) collective-permute-start(bf16[128,1024]{1,0:T(8,128)(2,1)S(1)} %gate.10.refs_9_.refs_0_), channel_id=1, source_target_pairs={{0,12},{4,8},{8,4},{12,0},{16,28},{20,24},{24,20},{28,16},{1,13},{... | collective-permute-start | bytes 786440 | tf_op jit(solution)/shard_map/ppermute | solution.py:510
  33.4 12.6 %collective-permute-start.12 = (bf16[128,1024]{1,0:T(8,128)(2,1)S(1)}, bf16[128,1024]{1,0:T(8,128)(2,1)S(1)}, u32[]{:S(2)}, u32[]{:S(2)}) collective-permute-start(bf16[128,1024]{1,0:T(8,128)(2,1)S(1)} %gate.10.refs_9_.refs_0_), channel_id=1, source_target_pairs={{0,8},{4,12},{8,0},{12,4},{16,24},{20,28},{24,16},{28,20},{1,9},{5... | collective-permute-start | bytes 786440 | tf_op jit(solution)/shard_map/ppermute | solution.py:510
  33.9 12.2 %collective-permute-start.11 = (bf16[128,1024]{1,0:T(8,128)(2,1)S(1)}, bf16[128,1024]{1,0:T(8,128)(2,1)S(1)}, u32[]{:S(2)}, u32[]{:S(2)}) collective-permute-start(bf16[128,1024]{1,0:T(8,128)(2,1)S(1)} %gate.10.refs_9_.refs_0_), channel_id=1, source_target_pairs={{0,4},{4,0},{8,12},{12,8},{16,20},{20,16},{24,28},{28,24},{1,5},{5... | collective-permute-start | bytes 786440 | tf_op jit(solution)/shard_map/ppermute | solution.py:510
  46.2 4.6 %collective-permute-start.16 = (bf16[512,1024]{1,0:T(8,128)(2,1)S(1)}, bf16[512,1024]{1,0:T(8,128)(2,1)S(1)}, u32[]{:S(2)}, u32[]{:S(2)}) collective-permute-start(bf16[512,1024]{1,0:T(8,128)(2,1)S(1)} %assemble.1.refs_5_.refs_4_.refs_3_), channel_id=1, source_target_pairs={{0,1},{1,0},{2,3},{3,2},{4,5},{5,4},{6,7},{7,6},{8,9},{9,8},{10,11... | collective-permute-start | bytes 3145736 | tf_op jit(solution)/shard_map/ppermute | solution.py:510
  46.2 6.9 %collective-permute-start.14 = (bf16[192,512]{1,0:T(8,128)(2,1)S(1)}, bf16[192,512]{1,0:T(8,128)(2,1)S(1)}, u32[]{:S(2)}, u32[]{:S(2)}) collective-permute-start(bf16[192,512]{1,0:T(8,128)(2,1)S(1)} %gate.11), channel_id=1, source_target_pairs={{0,3},{1,2},{2,1},{3,0},{4,7},{5,6},{6,5},{7,4},{8,11},{9,10},{10,... | collective-permute-start | bytes 589832 | tf_op jit(solution)/shard_map/ppermute | solution.py:510
  47.3 2.4 %collective-permute-start.17 = (bf16[512,512]{1,0:T(8,128)(2,1)S(1)}, bf16[512,512]{1,0:T(8,128)(2,1)S(1)}, u32[]{:S(2)}, u32[]{:S(2)}) collective-permute-start(bf16[512,512]{1,0:T(8,128)(2,1)S(1)} %gate.13), channel_id=1, source_target_pairs={{0,1},{1,0},{2,3},{3,2},{4,5},{5,4},{6,7},{7,6},{8,9},{9,8},{10,11... | collective-permute-start | bytes 1572872 | tf_op jit(solution)/shard_map/ppermute | solution.py:510
  47.4 3.4 %collective-permute-start.15 = (bf16[256,1024]{1,0:T(8,128)(2,1)S(1)}, bf16[256,1024]{1,0:T(8,128)(2,1)S(1)}, u32[]{:S(2)}, u32[]{:S(2)}) collective-permute-start(bf16[256,1024]{1,0:T(8,128)(2,1)S(1)} %gate.12.refs_3_.refs_2_), channel_id=1, source_target_pairs={{0,1},{1,0},{2,3},{3,2},{4,5},{5,4},{6,7},{7,6},{8,9},{9,8},{10,11... | collective-permute-start | bytes 1572872 | tf_op jit(solution)/shard_map/ppermute | solution.py:510

commit v7 on v6

--- a/solution.py
+++ b/solution.py
@@ -634,15 +634,11 @@
     straight = [(received[j][0], gathered[j]) for j in far_groups[:-1] if j % 2 == 0]
     crossed = [(received[j][0], gathered[j]) for j in far_groups[:-1] if j % 2]
     mates = [(theirs, [[(0, mate)]])]
-    totals = [
-        project_add(straight, totals[0], runs[0]),
-        project_add(straight + mates, totals[1], runs[1]),
-    ]
+    totals = [project_add(straight, totals[i], runs[i]) for i in range(2)]
     out = project_last(
         mates + crossed + [(received[last][0], gathered[last])], totals[0], None, runs[0], rows
     )
-    if crossed:
-        totals[1] = project_add(crossed, totals[1], runs[1])
+    totals[1] = project_add(mates + crossed, totals[1], runs[1])
     return project_last([(received[last][1], gathered[last])], totals[1], out, runs[1], rows)
 
 

time: 54.7 us -> 54.5 us (level)
    pallas_call x24 -> x25, Pallas kernels: 26.1 us -> 26.3 us  [call(): pl.pallas_call(run, in_specs=[anywhere if i in anywhere_in else vmem for...]
  transfers between devices with their start and end apart: 18 -> 18, of which waited for: 5 -> 6; matrix products, arithmetic and copies ran while one was open for 0% -> 0% of each run, Pallas kernels for 45% -> 46%
where the time goes in v7:
time: 54.5 us; the launch traced here: 54.4 us
  Pallas kernels  26.3 us (48%)
  starting transfers between devices  18.2 us (33%)
  waiting for transfers between devices  7.75 us (14%)
  local copies, waits for them, and re-layouts  1.77 us (3%)
    pallas_call x25, Pallas kernels, call(): pl.pallas_call(run, in_specs=[anywhere if i in anywhere_in else vmem for...  26.3 us
    ppermute x18, starting transfers between devices, flip(): return lax.ppermute(x, axis, [(i, i ^ bits) for i in range(n)])  18.2 us
    ppermute x18, waiting for transfers between devices, flip(): return lax.ppermute(x, axis, [(i, i ^ bits) for i in range(n)])  7.75 us
    unnamed x14, local copies, waits for them, and re-layouts  1.77 us
  transfers between devices with their start and end apart: 18, of which 6 were waited for; matrix products, arithmetic and copies ran while one was open for 0% of the time, Pallas kernels for 46%

profile of v7, /device:TPU:0, one launch (start us, length us, event | category | flops | bytes accessed | tf_op | source)
XLA Modules:
  0.0 54.4 jit_solution(4350475249602939188)
XLA Ops:
  0.0 0.0 copy-start.2
  0.0 1.7 %copy-done.4 = bf16[512,2048]{1,0:T(8,128)(2,1)S(1)} copy-done((bf16[512,2048]{1,0:T(8,128)(2,1)S(1)}, bf16[512,2048]{1,0:T(8,128)(2,1)}, u32[]{:S(2)}) %copy-start.4) | copy-done | bytes 2097176
  1.7 0.1 slice_weight.1
  1.8 3.0 %collective-permute-start.4 = (bf16[256,1024]{1,0:T(8,128)(2,1)S(1)}, bf16[256,1024]{1,0:T(8,128)(2,1)S(1)}, u32[]{:S(2)}, u32[]{:S(2)}) collective-permute-start(bf16[256,1024]{1,0:T(8,128)(2,1)S(1)} %get-tuple-element.20.refs_2_), channel_id=1, source_target_pairs={{0,2},{1,3},{2,0},{3,1},{4,6},{5,7},{6,4},{7,5},{8,10},{9,11},{10,... | collective-permute-start | bytes 1572872 | tf_op jit(solution)/shard_map/ppermute | solution.py:510
  4.8 0.0 copy-done.2
  4.8 0.0 copy-done.1
  4.9 0.0 copy-start.3
  4.9 0.0 copy-start.6
  4.9 0.8 %block_states.1 = (bf16[7,4,128,128]{3,2,1,0:T(8,128)(2,1)S(1)}, bf16[512,128]{1,0:T(8,128)(2,1)S(1)}) custom-call(bf16[2048,512]{1,0:T(8,128)(2,1)S(1)} %copy-done.1, bf16[2048,512]{1,0:T(8,128)(2,1)S(1)} %copy-done.2, bf16[256,1024]{1,0:T(8,128)(2,1)S(1)} %get-tuple-element.20.refs_2_, bf16[128,1024]{1,0:T(8,128)(2,1)S(1)} %get-tuple-element.21.refs_3_.refs_0_), custom_call_target="tpu_custom_call" | custom-call | flops 8000000000 | bytes 24000000 | tf_op jit(solution)/shard_map/block_states/pallas_call | solution.py:37
  5.7 2.6 %collective-permute-start.2 = (bf16[512,128]{1,0:T(8,128)(2,1)S(1)}, bf16[512,128]{1,0:T(8,128)(2,1)S(1)}, u32[]{:S(2)}, u32[]{:S(2)}) collective-permute-start(bf16[512,128]{1,0:T(8,128)(2,1)S(1)} %get-tuple-element.23.refs_7_.refs_0_), channel_id=1, source_target_pairs={{0,12},{4,8},{8,4},{12,0},{16,28},{20,24},{24,20},{28,16},{1,13},{... | collective-permute-start | bytes 393224 | tf_op jit(solution)/shard_map/ppermute | solution.py:510
  8.3 0.5 collective-permute-start.1
  8.7 0.5 collective-permute-start
  9.2 0.0 copy-done.5
  9.2 0.0 collective-permute-start.3
  9.2 0.0 copy-done
  9.2 0.0 copy-done.3
  9.3 0.0 copy-done.6
  9.3 4.8 %local_attention.3 = (bf16[1024,512]{1,0:T(8,128)(2,1)S(1)}, bf16[512,2048]{1,0:T(8,128)(2,1)S(1)}, bf16[48,512]{1,0:T(8,128)(2,1)S(1)}) custom-call(bf16[512,2048]{1,0:T(8,128)(2,1)S(1)} %copy-done.5, bf16[2048,512]{1,0:T(8,128)(2,1)S(1)} %copy-done, bf16[2048,512]{1,0:T(8,128)(2,1)S(1)} %copy-done.1, bf16[2048,512]{1,0:T(8,128)(2,1)S(1)} %copy-done.2, ...), custom_call_target="tpu_custom_call" | custom-call | flops 32000000000 | bytes 96000000 | tf_op jit(solution)/shard_map/local_attention/pallas_call | solution.py:37
  14.1 0.0 collective-permute-done.2.refs_3_
  14.1 0.4 collective-permute-done.1.refs_2_
  14.5 0.0 collective-permute-done.refs_1_.refs_4_
  14.5 0.0 collective-permute-done.3.refs_5_.refs_1_.refs_2_
  14.5 0.1 merge_states.1
  14.6 2.7 %collective-permute-start.5 = (bf16[512,128]{1,0:T(8,128)(2,1)S(1)}, bf16[512,128]{1,0:T(8,128)(2,1)S(1)}, u32[]{:S(2)}, u32[]{:S(2)}) collective-permute-start(bf16[512,128]{1,0:T(8,128)(2,1)S(1)} %get-tuple-element.27.refs_1_.refs_6_), channel_id=1, source_target_pairs={{0,16},{4,20},{8,24},{12,28},{16,0},{20,4},{24,8},{28,12},{1,17},{... | collective-permute-start | bytes 393224 | tf_op jit(solution)/shard_map/ppermute | solution.py:510
  17.2 0.0 collective-permute-done.4.refs_0_
  17.2 1.4 %collective-permute-start.7 = (bf16[256,1024]{1,0:T(8,128)(2,1)S(1)}, bf16[256,1024]{1,0:T(8,128)(2,1)S(1)}, u32[]{:S(2)}, u32[]{:S(2)}) collective-permute-start(bf16[256,1024]{1,0:T(8,128)(2,1)S(1)} %gate.7.refs_7_.refs_2_.refs_1_), channel_id=1, source_target_pairs={{0,4},{4,0},{8,12},{12,8},{16,20},{20,16},{24,28},{28,24},{1,5},{5... | collective-permute-start | bytes 1572872 | tf_op jit(solution)/shard_map/ppermute | solution.py:510
  18.7 0.0 collective-permute-start.6
  18.7 1.4 %collective-permute-start.8 = (bf16[128,1024]{1,0:T(8,128)(2,1)S(1)}, bf16[128,1024]{1,0:T(8,128)(2,1)S(1)}, u32[]{:S(2)}, u32[]{:S(2)}) collective-permute-start(bf16[128,1024]{1,0:T(8,128)(2,1)S(1)} %gate.9), channel_id=1, source_target_pairs={{0,2},{1,3},{2,0},{3,1},{4,6},{5,7},{6,4},{7,5},{8,10},{9,11},{10,... | collective-permute-start | bytes 786440 | tf_op jit(solution)/shard_map/ppermute | solution.py:510
  20.0 1.5 %begin_rows.1 = (f32[1024,512]{1,0:T(8,128)S(1)}, f32[1024,512]{1,0:T(8,128)S(1)}) custom-call(bf16[2048,512]{1,0:T(8,128)(2,1)S(1)} %copy-done, bf16[1024,512]{1,0:T(8,128)(2,1)S(1)} %get-tuple-element.24.refs_4_.refs_1_, s32[8,1,256]{2,1,0:T(1,128)S(1)} %bitcast.2, bf16[48,512]{1,0:T(8,128)(2,1)S(1)} %get-tuple-element.25.refs_3_.refs_4_, ...), custom_call_target="tpu_custom_call" | custom-call | flops 160000000 | bytes 480000 | tf_op jit(solution)/shard_map/begin_rows/pallas_call | solution.py:37
  21.6 2.3 %collective-permute-done.5.refs_3_.refs_6_ = bf16[512,128]{1,0:T(8,128)(2,1)S(1)} collective-permute-done((bf16[512,128]{1,0:T(8,128)(2,1)S(1)}, bf16[512,128]{1,0:T(8,128)(2,1)S(1)}, u32[]{:S(2)}, u32[]{:S(2)}) %collective-permute-start.5) | collective-permute-done | bytes 131104 | tf_op jit(solution)/shard_map/ppermute | solution.py:510
  23.9 1.5 %finish_rows.4.refs_4_ = bf16[512,512]{1,0:T(8,128)(2,1)S(1)} custom-call(bf16[2048,512]{1,0:T(8,128)(2,1)S(1)} %copy-done, f32[1024,512]{1,0:T(8,128)S(1)} %get-tuple-element.28.refs_1_.refs_4_, f32[1024,512]{1,0:T(8,128)S(1)} %get-tuple-element.29.refs_2_, bf16[512,128]{1,0:T(8,128)(2,1)S(1)} %collective-permute-done.5.refs_3_.refs_6_, ...), custom_call_target="tpu_custom_call" | custom-call | flops 16000000000 | bytes 48000000 | tf_op jit(solution)/shard_map/finish_rows/pallas_call | solution.py:37
  25.3 1.0 %collective-permute-start.9 = (bf16[512,512]{1,0:T(8,128)(2,1)S(1)}, bf16[512,512]{1,0:T(8,128)(2,1)S(1)}, u32[]{:S(2)}, u32[]{:S(2)}) collective-permute-start(bf16[512,512]{1,0:T(8,128)(2,1)S(1)} %finish_rows.4.refs_4_), channel_id=1, source_target_pairs={{0,2},{1,3},{2,0},{3,1},{4,6},{5,7},{6,4},{7,5},{8,10},{9,11},{10,... | collective-permute-start | bytes 1572872 | tf_op jit(solution)/shard_map/ppermute | solution.py:510
  26.3 0.0 collective-permute-done.6.refs_5_.refs_3_.refs_1_
  26.3 1.5 %finish_rows.5 = (bf16[320,512]{1,0:T(8,128)(2,1)S(1)}, bf16[192,512]{1,0:T(8,128)(2,1)S(1)}) custom-call(bf16[2048,512]{1,0:T(8,128)(2,1)S(1)} %copy-done, f32[1024,512]{1,0:T(8,128)S(1)} %get-tuple-element.28.refs_1_.refs_4_, f32[1024,512]{1,0:T(8,128)S(1)} %get-tuple-element.29.refs_2_, bf16[512,128]{1,0:T(8,128)(2,1)S(1)} %collective-permute-done.5.refs_3_.refs_6_, ...), custom_call_target="tpu_custom_call" | custom-call | flops 16000000000 | bytes 48000000 | tf_op jit(solution)/shard_map/finish_rows/pallas_call | solution.py:37
  27.8 0.1 collective-permute-start.10
  27.9 2.0 %local_attention.4.refs_1_.refs_7_ = bf16[512,512]{1,0:T(8,128)(2,1)S(1)} custom-call(bf16[2048,512]{1,0:T(8,128)(2,1)S(1)} %copy-done, bf16[2048,512]{1,0:T(8,128)(2,1)S(1)} %copy-done.1, bf16[2048,512]{1,0:T(8,128)(2,1)S(1)} %copy-done.2, s32[8,1,256]{2,1,0:T(1,128)S(1)} %bitcast.3, bf16[48,512]{1,0:T(8,128)(2,1)S(1)} %get-tuple-element.25.refs_3_.refs_4_, ...), custom_call_target="tpu_custom_call" | custom-call | flops 160000000 | bytes 480000 | tf_op jit(solution)/shard_map/local_attention/pallas_call | solution.py:37
  29.9 1.0 %collective-permute-done.7.refs_0_ = bf16[256,1024]{1,0:T(8,128)(2,1)S(1)} collective-permute-done((bf16[256,1024]{1,0:T(8,128)(2,1)S(1)}, bf16[256,1024]{1,0:T(8,128)(2,1)S(1)}, u32[]{:S(2)}, u32[]{:S(2)}) %collective-permute-start.7) | collective-permute-done | bytes 524320 | tf_op jit(solution)/shard_map/ppermute | solution.py:510
  30.9 0.0 collective-permute-done.8.refs_0_
  30.9 2.5 %collective-permute-start.13 = (bf16[128,1024]{1,0:T(8,128)(2,1)S(1)}, bf16[128,1024]{1,0:T(8,128)(2,1)S(1)}, u32[]{:S(2)}, u32[]{:S(2)}) collective-permute-start(bf16[128,1024]{1,0:T(8,128)(2,1)S(1)} %gate.10.refs_9_.refs_0_), channel_id=1, source_target_pairs={{0,12},{4,8},{8,4},{12,0},{16,28},{20,24},{24,20},{28,16},{1,13},{... | collective-permute-start | bytes 786440 | tf_op jit(solution)/shard_map/ppermute | solution.py:510
  33.4 0.4 collective-permute-start.12
  33.9 0.5 collective-permute-start.11
  34.4 2.4 %finish_rows.6.refs_6_.refs_7_.refs_0_ = bf16[512,512]{1,0:T(8,128)(2,1)S(1)} custom-call(bf16[2048,512]{1,0:T(8,128)(2,1)S(1)} %copy-done, bf16[512,512]{1,0:T(8,128)(2,1)S(1)} %local_attention.4.refs_1_.refs_7_, s32[8,1,256]{2,1,0:T(1,128)S(1)} %bitcast.4, bf16[48,512]{1,0:T(8,128)(2,1)S(1)} %get-tuple-element.25.refs_3_.refs_4_, ...), custom_call_target="tpu_custom_call" | custom-call | flops 16000000000 | bytes 48000000 | tf_op jit(solution)/shard_map/finish_rows/pallas_call | solution.py:37
  36.8 2.0 %local_attention.5.refs_1_ = bf16[512,512]{1,0:T(8,128)(2,1)S(1)} custom-call(bf16[2048,512]{1,0:T(8,128)(2,1)S(1)} %copy-done, bf16[2048,512]{1,0:T(8,128)(2,1)S(1)} %copy-done.1, bf16[2048,512]{1,0:T(8,128)(2,1)S(1)} %copy-done.2, s32[8,1,256]{2,1,0:T(1,128)S(1)} %bitcast.5, bf16[48,512]{1,0:T(8,128)(2,1)S(1)} %get-tuple-element.25.refs_3_.refs_4_, ...), custom_call_target="tpu_custom_call" | custom-call | flops 160000000 | bytes 480000 | tf_op jit(solution)/shard_map/local_attention/pallas_call | solution.py:37
  38.9 2.3 %finish_rows.7.refs_0_.refs_2_ = bf16[512,512]{1,0:T(8,128)(2,1)S(1)} custom-call(bf16[2048,512]{1,0:T(8,128)(2,1)S(1)} %copy-done, bf16[512,512]{1,0:T(8,128)(2,1)S(1)} %local_attention.5.refs_1_, s32[8,1,256]{2,1,0:T(1,128)S(1)} %bitcast.6, bf16[48,512]{1,0:T(8,128)(2,1)S(1)} %get-tuple-element.25.refs_3_.refs_4_, ...), custom_call_target="tpu_custom_call" | custom-call | flops 16000000000 | bytes 48000000 | tf_op jit(solution)/shard_map/finish_rows/pallas_call | solution.py:37
  41.2 1.3 %project_start.1 = (f32[320,2048]{1,0:T(8,128)S(1)}, f32[192,2048]{1,0:T(8,128)S(1)}) custom-call(bf16[512,512]{1,0:T(8,128)(2,1)S(1)} %finish_rows.7.refs_0_.refs_2_, bf16[512,2048]{1,0:T(8,128)(2,1)S(1)} %get-tuple-element.32.refs_1_, bf16[512,512]{1,0:T(8,128)(2,1)S(1)} %finish_rows.7.refs_0_.refs_2_), custom_call_target="tpu_custom_call" | custom-call | flops 19200000000 | bytes 57600000 | tf_op jit(solution)/shard_map/project_start/pallas_call | solution.py:37
  42.4 0.0 collective-permute-done.9.refs_6_.refs_3_.refs_0_
  42.4 0.0 collective-permute-done.13.refs_3_
  42.4 3.6 %collective-permute-done.12.refs_2_ = bf16[128,1024]{1,0:T(8,128)(2,1)S(1)} collective-permute-done((bf16[128,1024]{1,0:T(8,128)(2,1)S(1)}, bf16[128,1024]{1,0:T(8,128)(2,1)S(1)}, u32[]{:S(2)}, u32[]{:S(2)}) %collective-permute-start.12) | collective-permute-done | bytes 262176 | tf_op jit(solution)/shard_map/ppermute | solution.py:510
  46.1 0.0 collective-permute-done.11.refs_1_
  46.1 0.0 collective-permute-done.10.refs_7_.refs_4_.refs_1_
  46.1 0.1 assemble.1.refs_5_.refs_3_
  46.1 0.1 collective-permute-start.16
  46.2 1.0 %collective-permute-start.14 = (bf16[192,512]{1,0:T(8,128)(2,1)S(1)}, bf16[192,512]{1,0:T(8,128)(2,1)S(1)}, u32[]{:S(2)}, u32[]{:S(2)}) collective-permute-start(bf16[192,512]{1,0:T(8,128)(2,1)S(1)} %gate.11), channel_id=1, source_target_pairs={{0,3},{1,2},{2,1},{3,0},{4,7},{5,6},{6,5},{7,4},{8,11},{9,10},{10,... | collective-permute-start | bytes 589832 | tf_op jit(solution)/shard_map/ppermute | solution.py:510
  47.3 0.1 collective-permute-start.17
  47.4 0.4 collective-permute-start.15
  47.8 1.0 %project_add.5.refs_6_ = f32[320,2048]{1,0:T(8,128)S(1)} custom-call(bf16[512,512]{1,0:T(8,128)(2,1)S(1)} %collective-permute-done.9.refs_6_.refs_3_.refs_0_, bf16[256,1024]{1,0:T(8,128)(2,1)S(1)} %gate.7.refs_7_.refs_2_.refs_1_, bf16[256,1024]{1,0:T(8,128)(2,1)S(1)} %gate.12.refs_2_, ...), custom_call_target="tpu_custom_call", output_to_operand_aliasing={{}: (4, {})} | custom-call | flops 8000000000 | bytes 24000000 | tf_op jit(solution)/shard_map/project_add/pallas_call | solution.py:37
  48.8 0.7 %project_add.3.refs_2_ = f32[192,2048]{1,0:T(8,128)S(1)} custom-call(bf16[512,512]{1,0:T(8,128)(2,1)S(1)} %collective-permute-done.9.refs_6_.refs_3_.refs_0_, bf16[256,1024]{1,0:T(8,128)(2,1)S(1)} %gate.7.refs_7_.refs_2_.refs_1_, bf16[256,1024]{1,0:T(8,128)(2,1)S(1)} %gate.12.refs_2_, ...), custom_call_target="tpu_custom_call", output_to_operand_aliasing={{}: (4, {})} | custom-call | flops 8000000000 | bytes 24000000 | tf_op jit(solution)/shard_map/project_add/pallas_call | solution.py:37
  49.5 0.1 collective-permute-done.17.refs_0_
  49.6 0.7 %project_add.4.refs_4_ = f32[192,2048]{1,0:T(8,128)S(1)} custom-call(bf16[512,512]{1,0:T(8,128)(2,1)S(1)} %collective-permute-done.17.refs_0_, bf16[512,2048]{1,0:T(8,128)(2,1)S(1)} %collective-permute-done.3.refs_5_.refs_1_.refs_2_, f32[192,2048]{1,0:T(8,128)S(1)} %project_add.3.refs_2_), custom_call_target="tpu_custom_call", output_to_operand_aliasing={{}: (2, {})} | custom-call | flops 8000000000 | bytes 24000000 | tf_op jit(solution)/shard_map/project_add/pallas_call | solution.py:37
  50.3 0.0 collective-permute-done.15.refs_4_.refs_2_
  50.4 0.0 collective-permute-done.16.refs_5_.refs_3_
  50.4 2.3 %project_last.2.refs_5_ = bf16[512,2048]{1,0:T(8,128)(2,1)} custom-call(bf16[512,512]{1,0:T(8,128)(2,1)S(1)} %collective-permute-done.17.refs_0_, bf16[320,512]{1,0:T(8,128)(2,1)S(1)} %collective-permute-done.10.refs_7_.refs_4_.refs_1_, bf16[512,2048]{1,0:T(8,128)(2,1)S(1)} %collective-permute-done.3.refs_5_.refs_1_.refs_2_, ...), custom_call_target="tpu_custom_call" | custom-call | flops 12000000000 | bytes 36000000 | tf_op jit(solution)/shard_map/project_last/pallas_call | solution.py:37
  52.7 0.2 collective-permute-done.14.refs_0_
  52.9 1.3 %project_last.3 = bf16[512,2048]{1,0:T(8,128)(2,1)} custom-call(bf16[192,512]{1,0:T(8,128)(2,1)S(1)} %collective-permute-done.14.refs_0_, bf16[256,1024]{1,0:T(8,128)(2,1)S(1)} %collective-permute-done.6.refs_5_.refs_3_.refs_1_, bf16[256,1024]{1,0:T(8,128)(2,1)S(1)} %collective-permute-done.15.refs_4_.refs_2_, ...), custom_call_target="tpu_custom_call", output_to_operand_aliasing={{}: (5, {})} | custom-call | flops 12000000000 | bytes 36000000 | tf_op jit(solution)/shard_map/project_last/pallas_call | solution.py:37
  (11 shorter events, 0.0 us)
Async XLA Ops:
  0.0 4.8 %copy-start.2 = (bf16[2048,512]{1,0:T(8,128)(2,1)S(1)}, bf16[2048,512]{1,0:T(8,128)(2,1)}, u32[]{:S(2)}) copy-start(bf16[2048,512]{1,0:T(8,128)(2,1)} %refs_2_.5) | copy-start | bytes 6291460
  0.0 4.8 %copy-start.1 = (bf16[2048,512]{1,0:T(8,128)(2,1)S(1)}, bf16[2048,512]{1,0:T(8,128)(2,1)}, u32[]{:S(2)}) copy-start(bf16[2048,512]{1,0:T(8,128)(2,1)} %refs_1_.7) | copy-start | bytes 6291460
  0.0 1.7 %copy-start.4 = (bf16[512,2048]{1,0:T(8,128)(2,1)S(1)}, bf16[512,2048]{1,0:T(8,128)(2,1)}, u32[]{:S(2)}) copy-start(bf16[512,2048]{1,0:T(8,128)(2,1)} %refs_0_.12) | copy-start | bytes 6291460
  1.8 15.4 %collective-permute-start.4 = (bf16[256,1024]{1,0:T(8,128)(2,1)S(1)}, bf16[256,1024]{1,0:T(8,128)(2,1)S(1)}, u32[]{:S(2)}, u32[]{:S(2)}) collective-permute-start(bf16[256,1024]{1,0:T(8,128)(2,1)S(1)} %get-tuple-element.20.refs_2_), channel_id=1, source_target_pairs={{0,2},{1,3},{2,0},{3,1},{4,6},{5,7},{6,4},{7,5},{8,10},{9,11},{10,... | collective-permute-start | bytes 1572872 | tf_op jit(solution)/shard_map/ppermute | solution.py:510
  4.8 4.4 %copy-start.5 = (bf16[512,2048]{1,0:T(8,128)(2,1)S(1)}, bf16[512,2048]{1,0:T(8,128)(2,1)}, u32[]{:S(2)}) copy-start(bf16[512,2048]{1,0:T(8,128)(2,1)} %refs_0_.12) | copy-start | bytes 6291460
  4.9 4.4 %copy-start = (bf16[2048,512]{1,0:T(8,128)(2,1)S(1)}, bf16[2048,512]{1,0:T(8,128)(2,1)}, u32[]{:S(2)}) copy-start(bf16[2048,512]{1,0:T(8,128)(2,1)} %refs_0_.19) | copy-start | bytes 6291460
  4.9 4.4 %copy-start.3 = (s32[2048]{0:T(1024)S(1)}, s32[2048]{0:T(1024)}, u32[]{:S(2)}) copy-start(s32[2048]{0:T(1024)} %param.9) | copy-start | bytes 24580
  4.9 4.4 %copy-start.6 = (f32[16,4,20]{2,1,0:T(4,128)S(1)}, f32[16,4,20]{2,1,0:T(4,128)}, u32[]{:S(2)}) copy-start(f32[16,4,20]{2,1,0:T(4,128)} %refs_5_.1) | copy-start | bytes 15364
  5.7 8.4 %collective-permute-start.2 = (bf16[512,128]{1,0:T(8,128)(2,1)S(1)}, bf16[512,128]{1,0:T(8,128)(2,1)S(1)}, u32[]{:S(2)}, u32[]{:S(2)}) collective-permute-start(bf16[512,128]{1,0:T(8,128)(2,1)S(1)} %get-tuple-element.23.refs_7_.refs_0_), channel_id=1, source_target_pairs={{0,12},{4,8},{8,4},{12,0},{16,28},{20,24},{24,20},{28,16},{1,13},{... | collective-permute-start | bytes 393224 | tf_op jit(solution)/shard_map/ppermute | solution.py:510
  8.3 6.2 %collective-permute-start.1 = (bf16[512,128]{1,0:T(8,128)(2,1)S(1)}, bf16[512,128]{1,0:T(8,128)(2,1)S(1)}, u32[]{:S(2)}, u32[]{:S(2)}) collective-permute-start(bf16[512,128]{1,0:T(8,128)(2,1)S(1)} %get-tuple-element.23.refs_7_.refs_0_), channel_id=1, source_target_pairs={{0,8},{4,12},{8,0},{12,4},{16,24},{20,28},{24,16},{28,20},{1,9},{5... | collective-permute-start | bytes 393224 | tf_op jit(solution)/shard_map/ppermute | solution.py:510
  8.7 5.8 %collective-permute-start = (bf16[512,128]{1,0:T(8,128)(2,1)S(1)}, bf16[512,128]{1,0:T(8,128)(2,1)S(1)}, u32[]{:S(2)}, u32[]{:S(2)}) collective-permute-start(bf16[512,128]{1,0:T(8,128)(2,1)S(1)} %get-tuple-element.23.refs_7_.refs_0_), channel_id=1, source_target_pairs={{0,4},{4,0},{8,12},{12,8},{16,20},{20,16},{24,28},{28,24},{1,5},{5... | collective-permute-start | bytes 393224 | tf_op jit(solution)/shard_map/ppermute | solution.py:510
  9.2 5.3 %collective-permute-start.3 = (bf16[512,2048]{1,0:T(8,128)(2,1)S(1)}, bf16[512,2048]{1,0:T(8,128)(2,1)S(1)}, u32[]{:S(2)}, u32[]{:S(2)}) collective-permute-start(bf16[512,2048]{1,0:T(8,128)(2,1)S(1)} %copy-done.5), channel_id=1, source_target_pairs={{0,1},{1,0},{2,3},{3,2},{4,5},{5,4},{6,7},{7,6},{8,9},{9,8},{10,11... | collective-permute-start | bytes 6291464 | tf_op jit(solution)/shard_map/ppermute | solution.py:510
  14.6 9.3 %collective-permute-start.5 = (bf16[512,128]{1,0:T(8,128)(2,1)S(1)}, bf16[512,128]{1,0:T(8,128)(2,1)S(1)}, u32[]{:S(2)}, u32[]{:S(2)}) collective-permute-start(bf16[512,128]{1,0:T(8,128)(2,1)S(1)} %get-tuple-element.27.refs_1_.refs_6_), channel_id=1, source_target_pairs={{0,16},{4,20},{8,24},{12,28},{16,0},{20,4},{24,8},{28,12},{1,17},{... | collective-permute-start | bytes 393224 | tf_op jit(solution)/shard_map/ppermute | solution.py:510
  17.2 13.7 %collective-permute-start.7 = (bf16[256,1024]{1,0:T(8,128)(2,1)S(1)}, bf16[256,1024]{1,0:T(8,128)(2,1)S(1)}, u32[]{:S(2)}, u32[]{:S(2)}) collective-permute-start(bf16[256,1024]{1,0:T(8,128)(2,1)S(1)} %gate.7.refs_7_.refs_2_.refs_1_), channel_id=1, source_target_pairs={{0,4},{4,0},{8,12},{12,8},{16,20},{20,16},{24,28},{28,24},{1,5},{5... | collective-permute-start | bytes 1572872 | tf_op jit(solution)/shard_map/ppermute | solution.py:510
  18.7 7.7 %collective-permute-start.6 = (bf16[256,1024]{1,0:T(8,128)(2,1)S(1)}, bf16[256,1024]{1,0:T(8,128)(2,1)S(1)}, u32[]{:S(2)}, u32[]{:S(2)}) collective-permute-start(bf16[256,1024]{1,0:T(8,128)(2,1)S(1)} %gate.7.refs_7_.refs_2_.refs_1_), channel_id=1, source_target_pairs={{0,1},{1,0},{2,3},{3,2},{4,5},{5,4},{6,7},{7,6},{8,9},{9,8},{10,11... | collective-permute-start | bytes 1572872 | tf_op jit(solution)/shard_map/ppermute | solution.py:510
  18.7 12.2 %collective-permute-start.8 = (bf16[128,1024]{1,0:T(8,128)(2,1)S(1)}, bf16[128,1024]{1,0:T(8,128)(2,1)S(1)}, u32[]{:S(2)}, u32[]{:S(2)}) collective-permute-start(bf16[128,1024]{1,0:T(8,128)(2,1)S(1)} %gate.9), channel_id=1, source_target_pairs={{0,2},{1,3},{2,0},{3,1},{4,6},{5,7},{6,4},{7,5},{8,10},{9,11},{10,... | collective-permute-start | bytes 786440 | tf_op jit(solution)/shard_map/ppermute | solution.py:510
  25.3 17.1 %collective-permute-start.9 = (bf16[512,512]{1,0:T(8,128)(2,1)S(1)}, bf16[512,512]{1,0:T(8,128)(2,1)S(1)}, u32[]{:S(2)}, u32[]{:S(2)}) collective-permute-start(bf16[512,512]{1,0:T(8,128)(2,1)S(1)} %finish_rows.4.refs_4_), channel_id=1, source_target_pairs={{0,2},{1,3},{2,0},{3,1},{4,6},{5,7},{6,4},{7,5},{8,10},{9,11},{10,... | collective-permute-start | bytes 1572872 | tf_op jit(solution)/shard_map/ppermute | solution.py:510
  27.8 18.3 %collective-permute-start.10 = (bf16[320,512]{1,0:T(8,128)(2,1)S(1)}, bf16[320,512]{1,0:T(8,128)(2,1)S(1)}, u32[]{:S(2)}, u32[]{:S(2)}) collective-permute-start(bf16[320,512]{1,0:T(8,128)(2,1)S(1)} %get-tuple-element.31.refs_6_), channel_id=1, source_target_pairs={{0,3},{1,2},{2,1},{3,0},{4,7},{5,6},{6,5},{7,4},{8,11},{9,10},{10,... | collective-permute-start | bytes 983048 | tf_op jit(solution)/shard_map/ppermute | solution.py:510
  30.9 11.5 %collective-permute-start.13 = (bf16[128,1024]{1,0:T(8,128)(2,1)S(1)}, bf16[128,1024]{1,0:T(8,128)(2,1)S(1)}, u32[]{:S(2)}, u32[]{:S(2)}) collective-permute-start(bf16[128,1024]{1,0:T(8,128)(2,1)S(1)} %gate.10.refs_9_.refs_0_), channel_id=1, source_target_pairs={{0,12},{4,8},{8,4},{12,0},{16,28},{20,24},{24,20},{28,16},{1,13},{... | collective-permute-start | bytes 786440 | tf_op jit(solution)/shard_map/ppermute | solution.py:510
  33.4 12.6 %collective-permute-start.12 = (bf16[128,1024]{1,0:T(8,128)(2,1)S(1)}, bf16[128,1024]{1,0:T(8,128)(2,1)S(1)}, u32[]{:S(2)}, u32[]{:S(2)}) collective-permute-start(bf16[128,1024]{1,0:T(8,128)(2,1)S(1)} %gate.10.refs_9_.refs_0_), channel_id=1, source_target_pairs={{0,8},{4,12},{8,0},{12,4},{16,24},{20,28},{24,16},{28,20},{1,9},{5... | collective-permute-start | bytes 786440 | tf_op jit(solution)/shard_map/ppermute | solution.py:510
  33.9 12.2 %collective-permute-start.11 = (bf16[128,1024]{1,0:T(8,128)(2,1)S(1)}, bf16[128,1024]{1,0:T(8,128)(2,1)S(1)}, u32[]{:S(2)}, u32[]{:S(2)}) collective-permute-start(bf16[128,1024]{1,0:T(8,128)(2,1)S(1)} %gate.10.refs_9_.refs_0_), channel_id=1, source_target_pairs={{0,4},{4,0},{8,12},{12,8},{16,20},{20,16},{24,28},{28,24},{1,5},{5... | collective-permute-start | bytes 786440 | tf_op jit(solution)/shard_map/ppermute | solution.py:510
  46.1 4.2 %collective-permute-start.16 = (bf16[512,1024]{1,0:T(8,128)(2,1)S(1)}, bf16[512,1024]{1,0:T(8,128)(2,1)S(1)}, u32[]{:S(2)}, u32[]{:S(2)}) collective-permute-start(bf16[512,1024]{1,0:T(8,128)(2,1)S(1)} %assemble.1.refs_5_.refs_3_), channel_id=1, source_target_pairs={{0,1},{1,0},{2,3},{3,2},{4,5},{5,4},{6,7},{7,6},{8,9},{9,8},{10,11... | collective-permute-start | bytes 3145736 | tf_op jit(solution)/shard_map/ppermute | solution.py:510
  46.2 6.7 %collective-permute-start.14 = (bf16[192,512]{1,0:T(8,128)(2,1)S(1)}, bf16[192,512]{1,0:T(8,128)(2,1)S(1)}, u32[]{:S(2)}, u32[]{:S(2)}) collective-permute-start(bf16[192,512]{1,0:T(8,128)(2,1)S(1)} %gate.11), channel_id=1, source_target_pairs={{0,3},{1,2},{2,1},{3,0},{4,7},{5,6},{6,5},{7,4},{8,11},{9,10},{10,... | collective-permute-start | bytes 589832 | tf_op jit(solution)/shard_map/ppermute | solution.py:510
  47.3 2.4 %collective-permute-start.17 = (bf16[512,512]{1,0:T(8,128)(2,1)S(1)}, bf16[512,512]{1,0:T(8,128)(2,1)S(1)}, u32[]{:S(2)}, u32[]{:S(2)}) collective-permute-start(bf16[512,512]{1,0:T(8,128)(2,1)S(1)} %gate.13), channel_id=1, source_target_pairs={{0,1},{1,0},{2,3},{3,2},{4,5},{5,4},{6,7},{7,6},{8,9},{9,8},{10,11... | collective-permute-start | bytes 1572872 | tf_op jit(solution)/shard_map/ppermute | solution.py:510
  47.4 3.0 %collective-permute-start.15 = (bf16[256,1024]{1,0:T(8,128)(2,1)S(1)}, bf16[256,1024]{1,0:T(8,128)(2,1)S(1)}, u32[]{:S(2)}, u32[]{:S(2)}) collective-permute-start(bf16[256,1024]{1,0:T(8,128)(2,1)S(1)} %gate.12.refs_2_), channel_id=1, source_target_pairs={{0,1},{1,0},{2,3},{3,2},{4,5},{5,4},{6,7},{7,6},{8,9},{9,8},{10,11... | collective-permute-start | bytes 1572872 | tf_op jit(solution)/shard_map/ppermute | solution.py:510
